TPU v7x, 512 devices: a whole 4x4x16 slice. The times are simulated.
512 devices in a mesh: lon: 16 (over y, z_hi, core), frame: 32 (over x, z_lo).
Axes of the slice: x: 4, y: 4, z: 16 (z_hi: 2, z_lo: 8; z = z_hi * 8 + z_lo), core: 2. Of those that a mesh axis runs over, the one named last changes fastest.
Arguments:
- latents: bfloat16 [160, 32, 64, 640], P('frame', None, 'lon'), may hold values from -6 to 6
- spatial_kernel: bfloat16 [5760, 640], P('frame', 'lon'), may hold values from -0.078125 to 0.078125
- spatial_bias: float32 [640], replicated, may hold values from -4 to 4
- temporal_kernel: bfloat16 [1920, 640], replicated, may hold values from -0.125 to 0.125
- temporal_bias: float32 [640], replicated, may hold values from -4 to 4
Outputs:
- block_output: bfloat16 [160, 32, 64, 640], P('frame', None, 'lon')
All inputs are finite; a program needn't handle non-finite values.
Results may differ from a plain program's by a relative error of at most 0.0031.
Values may be sent and summed in bfloat16 or wider, within the bound.
No kernel may reach another device: no remote copies, remote signals or barrier semaphores. Data moves between devices by JAX's collectives and lax.ppermute only.
A program may use at most 128 MiB of HBM per device.

v0:
```python
import jax
import jax.numpy as jnp
from jax import lax
from jax.sharding import PartitionSpec as P


def padded_2(shard, sides, width, wrap):
    for axis, dim in sides:
        devices, length = (lax.axis_size(axis), shard.shape[dim])
        up = [(i, (i + 1) % devices) for i in range(devices if wrap else devices - 1)]
        down = [(j, i) for i, j in up]
        last = lax.slice_in_dim(shard, length - width, length, axis=dim)
        first = lax.slice_in_dim(shard, 0, width, axis=dim)
        before = lax.ppermute(last, axis, up)
        after = lax.ppermute(first, axis, down)
        shard = jnp.concatenate([before, shard, after], axis=dim)
    return shard


def collect_taps(padded, lat_rows, lon_cols):
    columns = []
    for offset_lat in range(3):
        for offset_lon in range(3):
            columns.append(
                padded[
                    ..., offset_lat : offset_lat + lat_rows, offset_lon : offset_lon + lon_cols, :
                ]
            )
    return jnp.concatenate(columns, axis=-1)


def spatial_layer(block, spatial_kernel, spatial_bias):
    frames, lat_rows, lon_cols, channels = block.shape
    wrapped = padded_2(block, (("lon", 2),), 1, True)
    padded = jnp.pad(wrapped, ((0, 0), (1, 1), (0, 0), (0, 0)))
    tap_rows = collect_taps(padded, lat_rows, lon_cols).reshape(
        frames * lat_rows * lon_cols, 9 * channels
    )
    full_rows = lax.all_gather(spatial_kernel, "frame", axis=0, tiled=True)
    summed = jnp.dot(
        tap_rows,
        lax.all_gather(full_rows, "lon", axis=1, tiled=True),
        preferred_element_type=jnp.float32,
    )
    activated = jax.nn.silu(summed + spatial_bias).astype(jnp.bfloat16)
    return activated.reshape(frames, lat_rows, lon_cols, channels)


def body(latents, spatial_kernel, spatial_bias, temporal_kernel, temporal_bias):
    frames = latents.shape[0]
    channels = latents.shape[3]
    hidden = spatial_layer(latents, spatial_kernel, spatial_bias)
    framed = padded_2(hidden, (("frame", 0),), 1, False)
    stacked = jnp.concatenate(
        [framed[:frames], framed[1 : frames + 1], framed[2 : frames + 2]], axis=-1
    )
    stacked = stacked.reshape(-1, 3 * channels)
    mixed = jnp.dot(stacked, temporal_kernel, preferred_element_type=jnp.float32) + temporal_bias
    result = latents.astype(jnp.float32) + jax.nn.silu(mixed).reshape(latents.shape)
    return result.astype(jnp.bfloat16)


def solution(mesh):
    placed = (P("frame", None, "lon", None), P("frame", "lon"), P(), P(), P())
    return jax.shard_map(
        body, mesh=mesh, in_specs=placed, out_specs=P("frame", None, "lon", None), check_vma=False
    )
```

profile of v0, /device:TPU:2, one launch (start us, length us, event | category | flops | bytes accessed | tf_op | source)
XLA Modules:
  0.0 359.2 jit_solution(2263640038592454637)
XLA Ops:
  6.5 0.0 copy-start
  6.5 0.0 copy-start.1
  6.5 0.0 all-gather.3.cloned.1.call-start
  6.5 119.8 %all-gather = bf16[32,180,40]{1,2,0:T(8,128)(2,1)S(1)} all-gather(bf16[1,180,40]{1,2,0:T(8,128)(2,1)} %bitcast.6), channel_id=1, replica_groups=mesh['lon'=16,'frame'=32] {'frame'}, dimensions={0}, use_global_device_ids=true | all-gather | bytes 475200 | tf_op jit(solution)/shard_map/all_gather | solution.py:39
  126.4 1.0 copy.13
  127.4 2.8 reshape.22
  130.1 0.0 all-gather.3.cloned.1.call-update
  130.1 0.0 copy-done.1
  130.2 0.6 fusion.18
  130.8 1.9 collective-permute-start.1
  132.8 2.4 collective-permute-start
  135.2 5.9 %collective-permute-done.1 = bf16[5,32,1,640]{3,1,2,0:T(8,128)(2,1)S(1)} collective-permute-done((bf16[5,32,1,640]{3,1,2,0:T(8,128)(2,1)S(1)}, bf16[5,32,1,640]{3,1,2,0:T(8,128)(2,1)S(1)}, u32[]{:S(2)}, u32[]{:S(2)}) %collective-permute-start.1) | collective-permute-done | bytes 204832 | tf_op jit(solution)/shard_map/ppermute | solution.py:15
  141.1 0.3 copy.10
  141.4 9.8 %collective-permute-done = bf16[5,32,1,640]{3,1,2,0:T(8,128)(2,1)S(1)} collective-permute-done((bf16[5,32,1,640]{3,1,2,0:T(8,128)(2,1)S(1)}, bf16[5,32,1,640]{3,1,2,0:T(8,128)(2,1)S(1)}, u32[]{:S(2)}, u32[]{:S(2)}) %collective-permute-start) | collective-permute-done | bytes 204832 | tf_op jit(solution)/shard_map/ppermute | solution.py:14
  151.2 0.3 copy.9
  151.6 1.4 fusion.11
  152.9 1.3 slice_dynamic-update-slice_fusion.5
  154.2 1.4 slice_dynamic-update-slice_fusion.4
  155.6 1.4 slice_dynamic-update-slice_fusion.3
  157.0 1.8 fusion.15
  158.8 1.3 constant_dynamic-update-slice_fusion
  160.1 2.1 fusion.14
  162.2 1.3 slice_dynamic-update-slice_fusion.2
  163.5 1.4 slice_dynamic-update-slice_fusion.1
  164.8 1.4 slice_dynamic-update-slice_fusion
  166.2 0.0 copy-start.3
  166.2 12.2 %reshape.18 = bf16[640,5760]{1,0:T(8,128)(2,1)} reshape(bf16[5,32,4,5760]{3,2,1,0:T(4,128)(2,1)} %slice_dynamic-update-slice_fusion) | data formatting | bytes 14745600 | tf_op jit(solution)/shard_map/reshape | solution.py:36
  178.5 123.6 %all-gather.3.cloned.1.call-done = bf16[5760,640]{0,1:T(8,128)(2,1)} async-done(((bf16[5760,40]{0,1:T(8,128)(2,1)}), bf16[5760,640]{0,1:T(8,128)(2,1)}) %all-gather.3.cloned.1.call-update) | async-done | bytes 7372816 | tf_op jit(solution)/shard_map/all_gather | solution.py:42
  302.0 0.0 copy-done.3
  302.0 10.5 %multiply_convert_fusion = bf16[640,640]{1,0:T(8,128)(2,1)S(1)} fusion(bf16[640,5760]{1,0:T(8,128)(2,1)} %reshape.18, bf16[5760,640]{0,1:T(8,128)(2,1)} %all-gather.3.cloned.1.call-done, f32[640]{0:T(1024)S(1)} %copy-done.3), kind=kOutput, calls=%fused_computation.16 | convolution fusion | flops 4721049600 | bytes 15567360 | tf_op jit(solution)/shard_map/dot_general | solution.py:40
  312.5 0.0 copy-start.2
  312.5 0.9 copy-done.2
  313.4 0.7 fusion.17
  314.1 1.6 slice.67
  315.7 1.9 collective-permute-start.2
  317.6 0.7 slice.70
  318.4 11.6 %collective-permute-start.3 = (bf16[1,32,4,640]{3,2,1,0:T(4,128)(2,1)}, bf16[1,32,4,640]{3,2,1,0:T(4,128)(2,1)S(1)}, u32[]{:S(2)}, u32[]{:S(2)}) collective-permute-start(bf16[1,32,4,640]{3,2,1,0:T(4,128)(2,1)} %slice.70), channel_id=1, source_target_pairs={{1,0},{2,1},{3,2},{4,3},{5,4},{6,5},{7,6},{8,7},{9,8},{10,9},{11,1... | collective-permute-start | bytes 491528 | tf_op jit(solution)/shard_map/ppermute | solution.py:15
  330.0 2.4 reshape.19
  332.4 0.1 collective-permute-done.2
  332.5 1.2 collective-permute-done.3
  333.7 3.7 %pad_maximum_fusion.1 = (bf16[5,32,4,640]{3,2,1,0:T(4,128)(2,1)}, bf16[5,32,4,640]{3,2,1,0:T(4,128)(2,1)}) fusion(bf16[5,32,4,640]{3,2,1,0:T(4,128)(2,1)} %reshape.19, bf16[1,32,4,640]{3,2,1,0:T(4,128)(2,1)} %collective-permute-done.2, bf16[1,32,4,640]{3,2,1,0:T(4,128)(2,1)S(1)} %collective-permute-done.3), kind=kLoop, calls=%fused_computation.18 | loop fusion | flops 819200 | bytes 2785280 | tf_op jit(solution)/shard_map/concatenate | solution.py:16
  337.4 2.3 concatenate.32
  339.6 2.3 concatenate.34
  341.9 0.0 copy-done
  341.9 0.0 copy-done.4
  341.9 5.0 %divide_multiply_fusion = f32[640,640]{1,0:T(8,128)} fusion(bf16[1920,640]{1,0:T(8,128)(2,1)S(1)} %copy-done, bf16[640,640]{1,0:T(8,128)(2,1)} %concatenate.34, bf16[640,640]{1,0:T(8,128)(2,1)} %copy-done.2, bf16[640,640]{1,0:T(8,128)(2,1)} %concatenate.32, f32[640]{0:T(1024)S(1)} %copy-done.4), kind=kOutput, calls=%fused_computation.15 | convolution fusion | flops 1582284800 | bytes 6556160 | tf_op jit(solution)/shard_map/dot_general | solution.py:58
  346.9 2.7 reshape.20
  349.7 2.7 add_convert_fusion
  (3 shorter events, 0.1 us)
Async XLA Ops:
  6.5 335.4 %copy-start = (bf16[1920,640]{1,0:T(8,128)(2,1)S(1)}, bf16[1920,640]{1,0:T(8,128)(2,1)}, u32[]{:S(2)}) copy-start(bf16[1920,640]{1,0:T(8,128)(2,1)} %param.8) | copy-start | bytes 7372804
  6.5 123.6 %copy-start.1 = (bf16[5,32,4,640]{3,2,1,0:T(4,128)(2,1)S(1)}, bf16[5,32,4,640]{3,2,1,0:T(4,128)(2,1)}, u32[]{:S(2)}) copy-start(bf16[5,32,4,640]{3,2,1,0:T(4,128)(2,1)} %param.5) | copy-start | bytes 2457604
  6.5 295.5 %all-gather.3.cloned.1.call-start = ((), (), s32[]{:S(2)}) async-start(), calls=%async_computation | async-start | bytes 7833600 | tf_op jit(solution)/shard_map/all_gather | solution.py:42
  130.8 10.3 %collective-permute-start.1 = (bf16[5,32,1,640]{3,1,2,0:T(8,128)(2,1)S(1)}, bf16[5,32,1,640]{3,1,2,0:T(8,128)(2,1)S(1)}, u32[]{:S(2)}, u32[]{:S(2)}) collective-permute-start(bf16[5,32,1,640]{3,1,2,0:T(8,128)(2,1)S(1)} %copy.15), channel_id=1, source_target_pairs={{32,0},{64,32},{96,64},{128,96},{160,128},{192,160},{224,192},{256... | collective-permute-start | bytes 614408 | tf_op jit(solution)/shard_map/ppermute | solution.py:15
  132.8 18.4 %collective-permute-start = (bf16[5,32,1,640]{3,1,2,0:T(8,128)(2,1)S(1)}, bf16[5,32,1,640]{3,1,2,0:T(8,128)(2,1)S(1)}, u32[]{:S(2)}, u32[]{:S(2)}) collective-permute-start(bf16[5,32,1,640]{3,1,2,0:T(8,128)(2,1)S(1)} %copy.14), channel_id=1, source_target_pairs={{0,32},{32,64},{64,96},{96,128},{128,160},{160,192},{192,224},{224... | collective-permute-start | bytes 614408 | tf_op jit(solution)/shard_map/ppermute | solution.py:14
  166.2 135.8 %copy-start.3 = (f32[640]{0:T(1024)S(1)}, f32[640]{0:T(1024)}, u32[]{:S(2)}) copy-start(f32[640]{0:T(1024)} %param.7) | copy-start | bytes 7684
  312.5 0.9 copy-start.2
  315.7 16.8 %collective-permute-start.2 = (bf16[1,32,4,640]{3,2,1,0:T(4,128)(2,1)}, bf16[1,32,4,640]{3,2,1,0:T(4,128)(2,1)}, u32[]{:S(2)}, u32[]{:S(2)}) collective-permute-start(bf16[1,32,4,640]{3,2,1,0:T(4,128)(2,1)} %slice.67), channel_id=1, source_target_pairs={{0,1},{1,2},{2,3},{3,4},{4,5},{5,6},{6,7},{7,8},{8,9},{9,10},{10,1... | collective-permute-start | bytes 491528 | tf_op jit(solution)/shard_map/ppermute | solution.py:14
  318.4 15.3 %collective-permute-start.3 = (bf16[1,32,4,640]{3,2,1,0:T(4,128)(2,1)}, bf16[1,32,4,640]{3,2,1,0:T(4,128)(2,1)S(1)}, u32[]{:S(2)}, u32[]{:S(2)}) collective-permute-start(bf16[1,32,4,640]{3,2,1,0:T(4,128)(2,1)} %slice.70), channel_id=1, source_target_pairs={{1,0},{2,1},{3,2},{4,3},{5,4},{6,5},{7,6},{8,7},{9,8},{10,9},{11,1... | collective-permute-start | bytes 491528 | tf_op jit(solution)/shard_map/ppermute | solution.py:15
  332.4 9.5 %copy-start.4 = (f32[640]{0:T(1024)S(1)}, f32[640]{0:T(1024)}, u32[]{:S(2)}) copy-start(f32[640]{0:T(1024)} %param.9) | copy-start | bytes 7684
Sparse Core Ops, SparseCore 0:
  130.3 171.7 all-gather.2
where the time goes:
time: 360 us; the launch traced here: 359 us
  waiting for transfers between devices  141 us (39%)
  blocking collectives  120 us (33%)
  local copies, waits for them, and re-layouts  40.3 us (11%)
  starting transfers between devices  17.8 us (5%)
  matrix products  15.5 us (4%)
  between operations  13.5 us (4%)
  other arithmetic  11.7 us (3%)
    all_gather x1, waiting for transfers between devices, spatial_layer(): lax.all_gather(full_rows, 'lon', axis=1, tiled=True)  124 us
    all_gather x1, blocking collectives, spatial_layer(): full_rows = lax.all_gather(spatial_kernel, 'frame', axis=0, tiled=True)  120 us
    ppermute x2, starting transfers between devices, padded_2(): after = lax.ppermute(first, axis, down)  13.5 us
    reshape x1, local copies, waits for them, and re-layouts, spatial_layer(): collect_taps(padded, lat_rows, lon_cols)  12.2 us
    unnamed x19, local copies, waits for them, and re-layouts  11.7 us
    dot_general x1, matrix products, spatial_layer(): jnp.dot(tap_rows, lax.all_gather(full_rows, 'lon', axis=1, tiled=True), p...  10.5 us
    ppermute x2, waiting for transfers between devices, padded_2(): before = lax.ppermute(last, axis, up)  9.95 us
  transfers between devices with their start and end apart: 5, of which 5 were waited for; matrix products, arithmetic and copies ran while one was open for 9% of the time, Pallas kernels for 0%

commit v1 on v0

v1 whole, which is shorter than its diff:
```python
import jax
import jax.numpy as jnp
from jax import lax
from jax.sharding import PartitionSpec as P

LONS = 16
FRAMES_AXIS = 32
Y = 4
X = 4
Z_LO = 8


def lon_index(y, z_hi, core):
    return y * 4 + z_hi * 2 + core


def frame_index(x, z_lo):
    return x * Z_LO + z_lo


def z_groups():
    return [
        [
            lon_index(y, z_hi, core) * FRAMES_AXIS + frame_index(x, z_lo)
            for z_hi in range(2)
            for z_lo in range(Z_LO)
        ]
        for x in range(X)
        for y in range(Y)
        for core in range(2)
    ]


def x_groups():
    return [[frame_index(x, z_lo) for x in range(X)] for z_lo in range(Z_LO)]


def from_y(k):
    return [(((y + k) % Y) * 4 + r, y * 4 + r) for y in range(Y) for r in range(4)]


CORES = [(i, i ^ 1) for i in range(LONS)]
FAR = [(i, (i + 1) % LONS if i % 2 else (i - 1) % LONS) for i in range(LONS)]


def copies(piece, count):
    return jnp.broadcast_to(piece[None], (count,) + piece.shape)


def gather_rows(spatial_kernel):
    shard = spatial_kernel.T
    cols, rows = shard.shape
    along_z = lax.all_to_all(
        copies(shard, 16), ("lon", "frame"), 0, 0, axis_index_groups=z_groups()
    )
    along_z = along_z.reshape(2, Z_LO, cols, rows).transpose(0, 2, 1, 3)
    along_z = along_z.reshape(2 * cols, Z_LO * rows)
    along_x = lax.all_to_all(copies(along_z, X), "frame", 0, 0, axis_index_groups=x_groups())
    return along_x.transpose(1, 0, 2).reshape(2 * cols, X * Z_LO * rows)


def own_order(blocks, axis):
    lon = lax.axis_index("lon")
    y, core = lon // 4, lon % 2
    shape = blocks.shape
    split = blocks.reshape(shape[:axis] + (Y, 2, 2, 40) + shape[axis + 1 :])
    twice = jnp.concatenate([split, split], axis=axis)
    turned = lax.dynamic_slice_in_dim(twice, y, Y, axis=axis)
    first = jnp.take(turned, jnp.array(0), axis=axis + 2)
    second = jnp.take(turned, jnp.array(1), axis=axis + 2)
    own = jnp.where(core == 0, first, second)
    other = jnp.where(core == 0, second, first)
    return jnp.concatenate([own, other], axis=axis).reshape(shape)


def body(latents, spatial_kernel, spatial_bias, temporal_kernel, temporal_bias):
    frames, lat_rows, lon_cols, channels = latents.shape
    positions = frames * lat_rows
    core = lax.axis_index("lon") % 2
    mine = gather_rows(spatial_kernel)

    mine, latents_then = lax.optimization_barrier((mine, latents))
    pieces = [mine] + [lax.ppermute(mine, "lon", from_y(k)) for k in (1, 2, 3)]
    columns = latents_then.transpose(2, 0, 1, 3)
    far = lax.ppermute(jnp.where(core == 1, columns[-1], columns[0]), "lon", FAR)
    near = lax.ppermute(jnp.where(core == 1, columns[0], columns[-1]), "lon", CORES)
    before = jnp.where(core == 1, near, far)
    after = jnp.where(core == 1, far, near)
    wide = jnp.concatenate([before[None], columns, after[None]], axis=0)
    wide = jnp.pad(wide, ((0, 0), (0, 0), (1, 1), (0, 0)))
    taps = [
        wide[b : b + lon_cols, :, a : a + lat_rows].reshape(lon_cols * positions, channels)
        for a in range(3)
        for b in range(3)
    ]
    tap_rows = jnp.concatenate(taps, axis=-1)

    half = jnp.concatenate(pieces, axis=0)
    whole = jnp.concatenate([half, lax.ppermute(half, "lon", CORES)], axis=0)
    summed = lax.dot_general(
        tap_rows, whole, (((1,), (1,)), ((), ())), preferred_element_type=jnp.float32
    )
    hidden = jax.nn.silu(summed + own_order(spatial_bias, 0)).astype(jnp.bfloat16)
    hidden = hidden.reshape(lon_cols, frames, lat_rows, channels)

    up = [(i, i + 1) for i in range(FRAMES_AXIS - 1)]
    down = [(i + 1, i) for i in range(FRAMES_AXIS - 1)]
    earlier = lax.ppermute(hidden[:, -1:], "frame", up)
    later = lax.ppermute(hidden[:, :1], "frame", down)
    framed = jnp.concatenate([earlier, hidden, later], axis=1)
    stacked = jnp.concatenate([framed[:, k : k + frames] for k in range(3)], axis=-1)
    ordered = own_order(temporal_kernel.reshape(3, channels, channels), 1)
    mixed = jnp.dot(
        stacked.reshape(-1, 3 * channels),
        ordered.reshape(3 * channels, channels),
        preferred_element_type=jnp.float32,
    )
    mixed = (mixed + temporal_bias).reshape(lon_cols, frames, lat_rows, channels)
    result = columns.astype(jnp.float32) + jax.nn.silu(mixed)
    return result.astype(jnp.bfloat16).transpose(1, 2, 0, 3)


def solution(mesh):
    placed = (P("frame", None, "lon", None), P("frame", "lon"), P(), P(), P())
    return jax.shard_map(
        body, mesh=mesh, in_specs=placed, out_specs=P("frame", None, "lon", None), check_vma=False
    )
```

time: 360 us -> 150 us (0.42)
  the two profiles are of different devices: /device:TPU:2 before, /device:TPU:1 now
where the time goes in v1:
time: 150 us; the launch traced here: 149 us
  starting transfers between devices  64.9 us (43%)
  waiting for transfers between devices  52.2 us (35%)
  local copies, waits for them, and re-layouts  19.6 us (13%)
  matrix products  8.2 us (5%)
  other arithmetic  3.6 us (2%)
    all_to_all x1, starting transfers between devices, gather_rows(): lax.all_to_all(copies(shard, 16), ('lon', 'frame'), 0, 0, axis_index_grou...  15.7 us
    all_to_all x1, waiting for transfers between devices, gather_rows(): lax.all_to_all(copies(shard, 16), ('lon', 'frame'), 0, 0, axis_index_grou...  14.4 us
    ppermute x1, waiting for transfers between devices, body(): lax.ppermute(jnp.where(core == 1, columns[-1], columns[0]), 'lon', FAR)  12.2 us
    ppermute x1, starting transfers between devices, body(): earlier = lax.ppermute(hidden[:, -1:], 'frame', up)  11 us
    ppermute x1, starting transfers between devices, body(): lax.ppermute(jnp.where(core == 1, columns[0], columns[-1]), 'lon', CORES)  10.5 us
    ppermute x1, starting transfers between devices, body(): lax.ppermute(jnp.where(core == 1, columns[-1], columns[0]), 'lon', FAR)  10.1 us
    ppermute x3, starting transfers between devices, body(): pieces = [mine] + [lax.ppermute(mine, 'lon', from_y(k)) for k in (1, 2, 3)]  9.5 us
    all_to_all x1, waiting for transfers between devices, gather_rows(): lax.all_to_all(copies(along_z, X), 'frame', 0, 0, axis_index_groups=x_gro...  8.05 us
  transfers between devices with their start and end apart: 10, of which 7 were waited for; matrix products, arithmetic and copies ran while one was open for 5% of the time, Pallas kernels for 0%

profile of v1, /device:TPU:1, one launch (start us, length us, event | category | flops | bytes accessed | tf_op | source)
XLA Modules:
  0.0 149.0 jit_solution(1721601138271901531)
XLA Ops:
  0.0 1.6 %broadcast_in_dim.32 = bf16[16,40,180]{2,1,0:T(8,128)(2,1)} broadcast(bf16[40,180]{1,0:T(8,128)(2,1)} %bitcast.81), dimensions={1,2} | broadcast | bytes 244800 | tf_op jit(solution)/shard_map/broadcast_in_dim | solution.py:47
  1.6 15.7 %all-to-all-start = ((bf16[16,40,180]{2,1,0:T(8,128)(2,1)}), bf16[16,40,180]{2,1,0:T(8,128)(2,1)S(1)}, u32[]{:S(2)}, u32[]{:S(2)}) async-start(bf16[16,40,180]{2,1,0:T(8,128)(2,1)} %broadcast_in_dim.32), calls=%async_computation | async-start | bytes 655360 | tf_op jit(solution)/shard_map/all_to_all | solution.py:53
  17.4 0.8 reshape.70
  18.2 14.4 %all-to-all-done = bf16[16,40,180]{2,1,0:T(8,128)(2,1)S(1)} async-done(((bf16[16,40,180]{2,1,0:T(8,128)(2,1)}), bf16[16,40,180]{2,1,0:T(8,128)(2,1)S(1)}, u32[]{:S(2)}, u32[]{:S(2)}) %all-to-all-start) | async-done | bytes 230432 | tf_op jit(solution)/shard_map/all_to_all | solution.py:53
  32.7 0.3 broadcast_in_dim.33
  33.0 1.0 broadcast_in_dim.34
  34.0 4.2 %all-to-all-start.1 = ((bf16[4,80,1440]{2,1,0:T(8,128)(2,1)}), bf16[4,80,1440]{2,1,0:T(8,128)(2,1)}, u32[]{:S(2)}, u32[]{:S(2)}) async-start(bf16[4,80,1440]{2,1,0:T(8,128)(2,1)} %broadcast_in_dim.34), calls=%async_computation.1 | async-start | bytes 1966080 | tf_op jit(solution)/shard_map/all_to_all | solution.py:58
  38.4 1.0 fusion.1
  39.4 0.2 broadcast_select_fusion.1
  39.7 8.1 %all-to-all-done.1 = bf16[4,80,1440]{2,1,0:T(8,128)(2,1)} async-done(((bf16[4,80,1440]{2,1,0:T(8,128)(2,1)}), bf16[4,80,1440]{2,1,0:T(8,128)(2,1)}, u32[]{:S(2)}, u32[]{:S(2)}) %all-to-all-start.1) | async-done | bytes 921632 | tf_op jit(solution)/shard_map/all_to_all | solution.py:58
  47.7 2.9 %copy.23 = bf16[80,4,1440]{2,1,0:T(4,128)(2,1)} copy(bf16[80,4,1440]{2,0,1:T(8,128)(2,1)} %bitcast.3) | data formatting | bytes 1843200 | tf_op jit(solution)/shard_map/transpose | solution.py:59
  50.6 2.3 %reshape.60 = bf16[80,5760]{1,0:T(8,128)(2,1)S(1)} reshape(bf16[80,4,1440]{2,1,0:T(4,128)(2,1)} %copy.23) | data formatting | bytes 1843200 | tf_op jit(solution)/shard_map/reshape | solution.py:59
  53.0 4.6 %collective-permute-start.2 = (bf16[80,5760]{1,0:T(8,128)(2,1)S(1)}, bf16[80,5760]{1,0:T(8,128)(2,1)S(1)}, u32[]{:S(2)}, u32[]{:S(2)}) collective-permute-start(bf16[80,5760]{1,0:T(8,128)(2,1)S(1)} %reshape.60), channel_id=1, source_target_pairs={{128,0},{160,32},{192,64},{224,96},{256,128},{288,160},{320,192},{... | collective-permute-start | bytes 2764808 | tf_op jit(solution)/shard_map/ppermute | solution.py:83
  57.6 2.3 %collective-permute-start.3 = (bf16[80,5760]{1,0:T(8,128)(2,1)S(1)}, bf16[80,5760]{1,0:T(8,128)(2,1)S(1)}, u32[]{:S(2)}, u32[]{:S(2)}) collective-permute-start(bf16[80,5760]{1,0:T(8,128)(2,1)S(1)} %reshape.60), channel_id=1, source_target_pairs={{256,0},{288,32},{320,64},{352,96},{384,128},{416,160},{448,192},{... | collective-permute-start | bytes 2764808 | tf_op jit(solution)/shard_map/ppermute | solution.py:83
  59.9 2.6 %collective-permute-start.4 = (bf16[80,5760]{1,0:T(8,128)(2,1)S(1)}, bf16[80,5760]{1,0:T(8,128)(2,1)S(1)}, u32[]{:S(2)}, u32[]{:S(2)}) collective-permute-start(bf16[80,5760]{1,0:T(8,128)(2,1)S(1)} %reshape.60), channel_id=1, source_target_pairs={{384,0},{416,32},{448,64},{480,96},{0,128},{32,160},{64,192},{96,2... | collective-permute-start | bytes 2764808 | tf_op jit(solution)/shard_map/ppermute | solution.py:83
  62.5 1.2 copy.33
  63.8 10.5 %collective-permute-start = (bf16[5,32,640]{2,1,0:T(8,128)(2,1)S(1)}, bf16[5,32,640]{2,1,0:T(8,128)(2,1)S(1)}, u32[]{:S(2)}, u32[]{:S(2)}) collective-permute-start(bf16[5,32,640]{2,1,0:T(8,128)(2,1)S(1)} %get-tuple-element.73), channel_id=1, source_target_pairs={{0,32},{32,0},{64,96},{96,64},{128,160},{160,128},{192,224},{224,1... | collective-permute-start | bytes 614408 | tf_op jit(solution)/shard_map/ppermute | solution.py:86
  74.3 10.1 %collective-permute-start.1 = (bf16[5,32,640]{2,1,0:T(8,128)(2,1)S(1)}, bf16[5,32,640]{2,1,0:T(8,128)(2,1)S(1)}, u32[]{:S(2)}, u32[]{:S(2)}) collective-permute-start(bf16[5,32,640]{2,1,0:T(8,128)(2,1)S(1)} %get-tuple-element.74), channel_id=1, source_target_pairs={{0,480},{32,64},{64,32},{96,128},{128,96},{160,192},{192,160},{224... | collective-permute-start | bytes 614408 | tf_op jit(solution)/shard_map/ppermute | solution.py:85
  84.5 12.2 %collective-permute-done.1 = bf16[5,32,640]{2,1,0:T(8,128)(2,1)S(1)} collective-permute-done((bf16[5,32,640]{2,1,0:T(8,128)(2,1)S(1)}, bf16[5,32,640]{2,1,0:T(8,128)(2,1)S(1)}, u32[]{:S(2)}, u32[]{:S(2)}) %collective-permute-start.1) | collective-permute-done | bytes 204832 | tf_op jit(solution)/shard_map/ppermute | solution.py:85
  96.8 0.7 fusion.12
  97.5 7.8 %collective-permute-done.4 = bf16[80,5760]{1,0:T(8,128)(2,1)S(1)} collective-permute-done((bf16[80,5760]{1,0:T(8,128)(2,1)S(1)}, bf16[80,5760]{1,0:T(8,128)(2,1)S(1)}, u32[]{:S(2)}, u32[]{:S(2)}) %collective-permute-start.4) | collective-permute-done | bytes 921632 | tf_op jit(solution)/shard_map/ppermute | solution.py:83
  105.3 0.5 pad_maximum_fusion
  105.8 2.6 %collective-permute-start.5 = (bf16[320,5760]{1,0:T(8,128)(2,1)S(1)}, bf16[320,5760]{1,0:T(8,128)(2,1)S(1)}, u32[]{:S(2)}, u32[]{:S(2)}) collective-permute-start(bf16[320,5760]{1,0:T(8,128)(2,1)S(1)} %pad_maximum_fusion), channel_id=1, source_target_pairs={{0,32},{32,0},{64,96},{96,64},{128,160},{160,128},{192,224},{224,1... | collective-permute-start | bytes 11059208 | tf_op jit(solution)/shard_map/ppermute | solution.py:99
  108.4 0.7 fusion.19
  109.2 0.1 constant_dynamic-update-slice_fusion.7
  109.3 0.1 constant_dynamic-update-slice_fusion.6
  109.5 0.2 pad_maximum_fusion.4
  109.7 0.1 constant_dynamic-update-slice_fusion.5
  109.8 0.1 constant_dynamic-update-slice_fusion.4
  109.9 0.1 constant_dynamic-update-slice_fusion.3
  110.1 0.1 constant_dynamic-update-slice_fusion.2
  110.2 0.1 constant_dynamic-update-slice_fusion.1
  110.3 0.1 constant_dynamic-update-slice_fusion
  110.5 0.1 constant_dynamic-update-slice_fusion.12
  110.8 2.6 %copy-done.2 = bf16[640,5760]{1,0:T(8,128)(2,1)} copy-done((bf16[640,5760]{1,0:T(8,128)(2,1)}, bf16[640,5760]{1,0:T(8,128)(2,1)S(1)}, u32[]{:S(2)}) %copy-start.2) | copy-done | bytes 7372824
  113.4 0.9 collective-permute-done.5
  114.3 0.5 constant_dynamic-update-slice_fusion.9
  114.8 2.6 %copy-done.3 = bf16[640,5760]{1,0:T(8,128)(2,1)S(1)} copy-done((bf16[640,5760]{1,0:T(8,128)(2,1)S(1)}, bf16[640,5760]{1,0:T(8,128)(2,1)}, u32[]{:S(2)}) %copy-start.3) | copy-done | bytes 7372824
  117.4 6.0 %multiply_convert_fusion = bf16[640,640]{1,0:T(8,128)(2,1)S(1)} fusion(bf16[640,5760]{1,0:T(8,128)(2,1)S(1)} %copy-done.3, bf16[640,5760]{1,0:T(8,128)(2,1)S(1)} %constant_dynamic-update-slice_fusion.9, f32[640]{0:T(1024)S(1)} %add.48), kind=kOutput, calls=%fused_computation.18 | convolution fusion | flops 4721049600 | bytes 15567360 | tf_op jit(solution)/shard_map/dot_general | solution.py:100
  123.4 11.0 %collective-permute-start.6 = (bf16[4,1,32,640]{3,2,1,0:T(8,128)(2,1)S(1)}, bf16[4,1,32,640]{3,2,1,0:T(8,128)(2,1)S(1)}, u32[]{:S(2)}, u32[]{:S(2)}) collective-permute-start(bf16[4,1,32,640]{3,2,1,0:T(8,128)(2,1)S(1)} %get-tuple-element.67), channel_id=1, source_target_pairs={{0,1},{1,2},{2,3},{3,4},{4,5},{5,6},{6,7},{7,8},{8,9},{9,10},{10,1... | collective-permute-start | bytes 491528 | tf_op jit(solution)/shard_map/ppermute | solution.py:108
  134.4 1.3 collective-permute-start.7
  135.7 0.3 pad_maximum_fusion.1
  136.0 1.6 %collective-permute-done.6 = bf16[4,1,32,640]{3,2,1,0:T(8,128)(2,1)S(1)} collective-permute-done((bf16[4,1,32,640]{3,2,1,0:T(8,128)(2,1)S(1)}, bf16[4,1,32,640]{3,2,1,0:T(8,128)(2,1)S(1)}, u32[]{:S(2)}, u32[]{:S(2)}) %collective-permute-start.6) | collective-permute-done | bytes 163872 | tf_op jit(solution)/shard_map/ppermute | solution.py:108
  137.6 7.3 %collective-permute-done.7 = bf16[4,1,32,640]{3,2,1,0:T(8,128)(2,1)S(1)} collective-permute-done((bf16[4,1,32,640]{3,2,1,0:T(8,128)(2,1)S(1)}, bf16[4,1,32,640]{3,2,1,0:T(8,128)(2,1)S(1)}, u32[]{:S(2)}, u32[]{:S(2)}) %collective-permute-start.7) | collective-permute-done | bytes 163872 | tf_op jit(solution)/shard_map/ppermute | solution.py:109
  144.9 0.1 pad_maximum_fusion.3
  145.1 2.2 %fusion.13 = f32[640,640]{1,0:T(8,128)S(1)} fusion(bf16[1920,640]{1,0:T(8,128)(2,1)S(1)} %bitcast.74, bf16[640,640]{1,0:T(8,128)(2,1)S(1)} %bitcast.80, bf16[640,640]{1,0:T(8,128)(2,1)S(1)} %multiply_convert_fusion, bf16[640,640]{1,0:T(8,128)(2,1)S(1)} %bitcast.79, f32[640]{0:T(1024)S(1)} %copy-done.4), kind=kOutput, calls=%fused_computation.21 | convolution fusion | flops 1580646400 | bytes 6556160 | tf_op jit(solution)/shard_map/dot_general | solution.py:113
  147.3 0.4 fusion.16
  147.7 1.3 copy.27
  (24 shorter events, 0.7 us)
Async XLA Ops:
  0.0 38.4 %copy-start.1 = (bf16[1920,640]{1,0:T(8,128)(2,1)S(1)}, bf16[1920,640]{1,0:T(8,128)(2,1)}, u32[]{:S(2)}) copy-start(bf16[1920,640]{1,0:T(8,128)(2,1)} %param.16) | copy-start | bytes 7372804
  1.6 31.0 %all-to-all-start = ((bf16[16,40,180]{2,1,0:T(8,128)(2,1)}), bf16[16,40,180]{2,1,0:T(8,128)(2,1)S(1)}, u32[]{:S(2)}, u32[]{:S(2)}) async-start(bf16[16,40,180]{2,1,0:T(8,128)(2,1)} %broadcast_in_dim.32), calls=%async_computation | async-start | bytes 655360 | tf_op jit(solution)/shard_map/all_to_all | solution.py:53
  34.0 13.7 %all-to-all-start.1 = ((bf16[4,80,1440]{2,1,0:T(8,128)(2,1)}), bf16[4,80,1440]{2,1,0:T(8,128)(2,1)}, u32[]{:S(2)}, u32[]{:S(2)}) async-start(bf16[4,80,1440]{2,1,0:T(8,128)(2,1)} %broadcast_in_dim.34), calls=%async_computation.1 | async-start | bytes 1966080 | tf_op jit(solution)/shard_map/all_to_all | solution.py:58
  53.0 44.5 %collective-permute-start.2 = (bf16[80,5760]{1,0:T(8,128)(2,1)S(1)}, bf16[80,5760]{1,0:T(8,128)(2,1)S(1)}, u32[]{:S(2)}, u32[]{:S(2)}) collective-permute-start(bf16[80,5760]{1,0:T(8,128)(2,1)S(1)} %reshape.60), channel_id=1, source_target_pairs={{128,0},{160,32},{192,64},{224,96},{256,128},{288,160},{320,192},{... | collective-permute-start | bytes 2764808 | tf_op jit(solution)/shard_map/ppermute | solution.py:83
  57.6 39.9 %collective-permute-start.3 = (bf16[80,5760]{1,0:T(8,128)(2,1)S(1)}, bf16[80,5760]{1,0:T(8,128)(2,1)S(1)}, u32[]{:S(2)}, u32[]{:S(2)}) collective-permute-start(bf16[80,5760]{1,0:T(8,128)(2,1)S(1)} %reshape.60), channel_id=1, source_target_pairs={{256,0},{288,32},{320,64},{352,96},{384,128},{416,160},{448,192},{... | collective-permute-start | bytes 2764808 | tf_op jit(solution)/shard_map/ppermute | solution.py:83
  59.9 45.4 %collective-permute-start.4 = (bf16[80,5760]{1,0:T(8,128)(2,1)S(1)}, bf16[80,5760]{1,0:T(8,128)(2,1)S(1)}, u32[]{:S(2)}, u32[]{:S(2)}) collective-permute-start(bf16[80,5760]{1,0:T(8,128)(2,1)S(1)} %reshape.60), channel_id=1, source_target_pairs={{384,0},{416,32},{448,64},{480,96},{0,128},{32,160},{64,192},{96,2... | collective-permute-start | bytes 2764808 | tf_op jit(solution)/shard_map/ppermute | solution.py:83
  63.8 20.7 %collective-permute-start = (bf16[5,32,640]{2,1,0:T(8,128)(2,1)S(1)}, bf16[5,32,640]{2,1,0:T(8,128)(2,1)S(1)}, u32[]{:S(2)}, u32[]{:S(2)}) collective-permute-start(bf16[5,32,640]{2,1,0:T(8,128)(2,1)S(1)} %get-tuple-element.73), channel_id=1, source_target_pairs={{0,32},{32,0},{64,96},{96,64},{128,160},{160,128},{192,224},{224,1... | collective-permute-start | bytes 614408 | tf_op jit(solution)/shard_map/ppermute | solution.py:86
  74.3 22.4 %collective-permute-start.1 = (bf16[5,32,640]{2,1,0:T(8,128)(2,1)S(1)}, bf16[5,32,640]{2,1,0:T(8,128)(2,1)S(1)}, u32[]{:S(2)}, u32[]{:S(2)}) collective-permute-start(bf16[5,32,640]{2,1,0:T(8,128)(2,1)S(1)} %get-tuple-element.74), channel_id=1, source_target_pairs={{0,480},{32,64},{64,32},{96,128},{128,96},{160,192},{192,160},{224... | collective-permute-start | bytes 614408 | tf_op jit(solution)/shard_map/ppermute | solution.py:85
  105.8 8.4 %collective-permute-start.5 = (bf16[320,5760]{1,0:T(8,128)(2,1)S(1)}, bf16[320,5760]{1,0:T(8,128)(2,1)S(1)}, u32[]{:S(2)}, u32[]{:S(2)}) collective-permute-start(bf16[320,5760]{1,0:T(8,128)(2,1)S(1)} %pad_maximum_fusion), channel_id=1, source_target_pairs={{0,32},{32,0},{64,96},{96,64},{128,160},{160,128},{192,224},{224,1... | collective-permute-start | bytes 11059208 | tf_op jit(solution)/shard_map/ppermute | solution.py:99
  110.4 3.0 %copy-start.2 = (bf16[640,5760]{1,0:T(8,128)(2,1)}, bf16[640,5760]{1,0:T(8,128)(2,1)S(1)}, u32[]{:S(2)}) copy-start(bf16[640,5760]{1,0:T(8,128)(2,1)S(1)} %constant_dynamic-update-slice_fusion) | copy-start | bytes 22118404
  114.3 3.1 %copy-start.3 = (bf16[640,5760]{1,0:T(8,128)(2,1)S(1)}, bf16[640,5760]{1,0:T(8,128)(2,1)}, u32[]{:S(2)}) copy-start(bf16[640,5760]{1,0:T(8,128)(2,1)} %copy-done.2) | copy-start | bytes 22118404
  123.4 14.1 %collective-permute-start.6 = (bf16[4,1,32,640]{3,2,1,0:T(8,128)(2,1)S(1)}, bf16[4,1,32,640]{3,2,1,0:T(8,128)(2,1)S(1)}, u32[]{:S(2)}, u32[]{:S(2)}) collective-permute-start(bf16[4,1,32,640]{3,2,1,0:T(8,128)(2,1)S(1)} %get-tuple-element.67), channel_id=1, source_target_pairs={{0,1},{1,2},{2,3},{3,4},{4,5},{5,6},{6,7},{7,8},{8,9},{9,10},{10,1... | collective-permute-start | bytes 491528 | tf_op jit(solution)/shard_map/ppermute | solution.py:108
  134.4 10.5 %collective-permute-start.7 = (bf16[4,1,32,640]{3,2,1,0:T(8,128)(2,1)S(1)}, bf16[4,1,32,640]{3,2,1,0:T(8,128)(2,1)S(1)}, u32[]{:S(2)}, u32[]{:S(2)}) collective-permute-start(bf16[4,1,32,640]{3,2,1,0:T(8,128)(2,1)S(1)} %get-tuple-element.68), channel_id=1, source_target_pairs={{1,0},{2,1},{3,2},{4,3},{5,4},{6,5},{7,6},{8,7},{9,8},{10,9},{11,1... | collective-permute-start | bytes 491528 | tf_op jit(solution)/shard_map/ppermute | solution.py:109
  135.7 9.3 %copy-start.4 = (f32[640]{0:T(1024)S(1)}, f32[640]{0:T(1024)}, u32[]{:S(2)}) copy-start(f32[640]{0:T(1024)} %param.17) | copy-start | bytes 7684
  145.0 2.2 %copy-start = (bf16[5,32,4,640]{3,2,1,0:T(4,128)(2,1)S(1)}, bf16[5,32,4,640]{3,2,1,0:T(4,128)(2,1)}, u32[]{:S(2)}) copy-start(bf16[5,32,4,640]{3,2,1,0:T(4,128)(2,1)} %param.13) | copy-start | bytes 2457604

commit v2 on v1

v2 whole, which is shorter than its diff:
```python
import jax
import jax.numpy as jnp
import numpy as np
from jax import lax
from jax.sharding import PartitionSpec as P

LONS = 16
FRAMES_AXIS = 32
Y = 4
X = 4
Z_LO = 8


def lon_index(y, z_hi, core):
    return y * 4 + z_hi * 2 + core


def frame_index(x, z_lo):
    return x * Z_LO + z_lo


def z_groups():
    return [
        [
            lon_index(y, z_hi, core) * FRAMES_AXIS + frame_index(x, z_lo)
            for z_hi in range(2)
            for z_lo in range(Z_LO)
        ]
        for x in range(X)
        for y in range(Y)
        for core in range(2)
    ]


def x_groups():
    return [[frame_index(x, z_lo) for x in range(X)] for z_lo in range(Z_LO)]


def from_y(k):
    return [(((y + k) % Y) * 4 + r, y * 4 + r) for y in range(Y) for r in range(4)]


CORES = [(i, i ^ 1) for i in range(LONS)]
FAR = [(i, (i + 1) % LONS if i % 2 else (i - 1) % LONS) for i in range(LONS)]

ARRIVALS = (
    ((0, 0), (0, 1)),
    ((3, 0), (1, 1)),
    ((3, 1), (1, 0)),
    ((2, 0), (2, 1)),
)


def copies(piece, count):
    return jnp.broadcast_to(piece[None], (count,) + piece.shape)


def gather_rows(spatial_kernel):
    shard = spatial_kernel.T
    cols, rows = shard.shape
    along_z = lax.all_to_all(
        copies(shard, 16), ("lon", "frame"), 0, 0, axis_index_groups=z_groups()
    )
    along_z = along_z.reshape(2, Z_LO, cols, rows).transpose(0, 2, 1, 3)
    along_z = along_z.reshape(2 * cols, Z_LO * rows)
    along_x = lax.all_to_all(copies(along_z, X), "frame", 0, 0, axis_index_groups=x_groups())
    return jnp.concatenate([along_x[x] for x in range(X)], axis=1)


def arrival_order():
    lon = lax.axis_index("lon")
    blocks = [(k, z_hi, side) for arrival in ARRIVALS for side in range(2) for k, z_hi in arrival]
    ahead, z_hi, side = (jnp.asarray(np.repeat(np.array(v), 40)) for v in zip(*blocks))
    within = jnp.asarray(np.tile(np.arange(40), LONS))
    row = lax.rem(lon // 4 + ahead, Y)
    return lon_index(row, z_hi, (lon % 2) ^ side) * 40 + within


def gather_arrivals(mine):
    half = mine.shape[0] // 2
    low, high = mine[:half], mine[half:]
    low_behind = lax.ppermute(low, "lon", from_y(3))
    high_ahead = lax.ppermute(high, "lon", from_y(1))
    high_behind = lax.ppermute(high, "lon", from_y(3))
    low_ahead = lax.ppermute(low, "lon", from_y(1))
    low_across = lax.ppermute(low_behind, "lon", from_y(3))
    high_across = lax.ppermute(high_ahead, "lon", from_y(1))
    arrivals = [
        mine,
        jnp.concatenate([low_behind, high_ahead]),
        jnp.concatenate([high_behind, low_ahead]),
        jnp.concatenate([low_across, high_across]),
    ]
    return [(own, lax.ppermute(own, "lon", CORES)) for own in arrivals]


def widened(latents):
    core = lax.axis_index("lon") % 2
    columns = latents.transpose(2, 0, 1, 3)
    far = lax.ppermute(jnp.where(core == 1, columns[-1], columns[0]), "lon", FAR)
    near = lax.ppermute(jnp.where(core == 1, columns[0], columns[-1]), "lon", CORES)
    before = jnp.where(core == 1, near, far)
    after = jnp.where(core == 1, far, near)
    return columns, jnp.concatenate([before[None], columns, after[None]], axis=0)


def with_frames(wide):
    up = [(i, i + 1) for i in range(FRAMES_AXIS - 1)]
    down = [(i + 1, i) for i in range(FRAMES_AXIS - 1)]
    earlier = lax.ppermute(wide[:, -1:], "frame", up)
    later = lax.ppermute(wide[:, :1], "frame", down)
    return jnp.concatenate([earlier, wide, later], axis=1)


def body(latents, spatial_kernel, spatial_bias, temporal_kernel, temporal_bias):
    frames, lat_rows, lon_cols, channels = latents.shape
    columns, wide = widened(latents)
    mine = gather_rows(spatial_kernel)
    mine, wide, temporal_kernel = lax.optimization_barrier((mine, wide, temporal_kernel))
    arrivals = gather_arrivals(mine)

    wide = jnp.pad(with_frames(wide), ((0, 0), (0, 0), (1, 1), (0, 0)))
    taps = [
        wide[b : b + lon_cols, :, a : a + lat_rows].reshape(-1, channels)
        for a in range(3)
        for b in range(3)
    ]
    tap_rows = jnp.concatenate(taps, axis=-1)

    frame = lax.axis_index("frame")
    step = lax.broadcasted_iota(jnp.int32, (lon_cols, frames + 2, lat_rows, 1), 1)
    outside = ((step == 0) & (frame == 0)) | ((step == frames + 1) & (frame == FRAMES_AXIS - 1))
    outside = outside.reshape(-1, 1)
    order = arrival_order()[:, None] == lax.broadcasted_iota(jnp.int32, (channels, channels), 1)
    bias = jnp.sum(jnp.where(order, spatial_bias[None, :], 0.0), axis=1)
    parts, start = [], 0
    for group in (arrivals[:3], arrivals[3:]):
        rows = jnp.concatenate([piece for pair in group for piece in pair], axis=0)
        summed = lax.dot_general(
            tap_rows, rows, (((1,), (1,)), ((), ())), preferred_element_type=jnp.float32
        )
        active = jax.nn.silu(summed + bias[start : start + rows.shape[0]])
        parts.append(jnp.where(outside, 0.0, active).astype(jnp.bfloat16))
        start += rows.shape[0]
    hidden = jnp.concatenate(parts, axis=-1)
    hidden = hidden.reshape(lon_cols, frames + 2, lat_rows, channels)

    stacked = jnp.concatenate([hidden[:, k : k + frames] for k in range(3)], axis=-1)
    ordered = [
        jnp.dot(order.astype(jnp.bfloat16), temporal_kernel[k * channels : (k + 1) * channels])
        for k in range(3)
    ]
    mixed = jnp.dot(
        stacked.reshape(-1, 3 * channels),
        jnp.concatenate(ordered, axis=0),
        preferred_element_type=jnp.float32,
    )
    mixed = (mixed + temporal_bias).reshape(lon_cols, frames, lat_rows, channels)
    result = columns.astype(jnp.float32) + jax.nn.silu(mixed)
    return result.astype(jnp.bfloat16).transpose(1, 2, 0, 3)


def solution(mesh):
    placed = (P("frame", None, "lon", None), P("frame", "lon"), P(), P(), P())
    return jax.shard_map(
        body, mesh=mesh, in_specs=placed, out_specs=P("frame", None, "lon", None), check_vma=False
    )
```

time: 150 us -> 155 us (1.033)
  the two profiles are of different devices: /device:TPU:1 before, /device:TPU:481 now
where the time goes in v2:
time: 155 us; the launch traced here: 154 us
  starting transfers between devices  69.4 us (45%)
  waiting for transfers between devices  44.9 us (29%)
  local copies, waits for them, and re-layouts  21.4 us (14%)
  matrix products  16.2 us (10%)
  other arithmetic  1.58 us (1%)
    ppermute x4, starting transfers between devices, gather_arrivals(): return [(own, lax.ppermute(own, 'lon', CORES)) for own in arrivals]  18.6 us
    ppermute x1, waiting for transfers between devices, with_frames(): later = lax.ppermute(wide[:, :1], 'frame', down)  18.3 us
    ppermute x1, starting transfers between devices, widened(): lax.ppermute(jnp.where(core == 1, columns[-1], columns[0]), 'lon', FAR)  10.6 us
    dot_general x2, matrix products, body(): lax.dot_general(tap_rows, rows, (((1,), (1,)), ((), ())), preferred_eleme...  9.4 us
    unnamed x44, local copies, waits for them, and re-layouts  8.56 us
    all_to_all x1, starting transfers between devices, gather_rows(): lax.all_to_all(copies(shard, 16), ('lon', 'frame'), 0, 0, axis_index_grou...  8.29 us
    ppermute x1, waiting for transfers between devices, gather_arrivals(): high_across = lax.ppermute(high_ahead, 'lon', from_y(1))  8 us
    ppermute x1, waiting for transfers between devices, widened(): lax.ppermute(jnp.where(core == 1, columns[-1], columns[0]), 'lon', FAR)  7.79 us
  transfers between devices with their start and end apart: 16, of which 7 were waited for; matrix products, arithmetic and copies ran while one was open for 13% of the time, Pallas kernels for 0%

profile of v2, /device:TPU:481, one launch (start us, length us, event | category | flops | bytes accessed | tf_op | source)
XLA Modules:
  0.0 154.1 jit_solution(7765332032956947730)
XLA Ops:
  0.0 1.5 broadcast_in_dim.62
  1.5 8.3 %all-to-all-start = ((bf16[16,40,180]{2,1,0:T(8,128)(2,1)}), bf16[16,40,180]{2,1,0:T(8,128)(2,1)S(1)}, u32[]{:S(2)}, u32[]{:S(2)}) async-start(bf16[16,40,180]{2,1,0:T(8,128)(2,1)} %broadcast_in_dim.62), calls=%async_computation | async-start | bytes 655360 | tf_op jit(solution)/shard_map/all_to_all | solution.py:61
  9.8 1.2 copy.29
  11.1 3.1 %collective-permute-start = (bf16[5,32,640]{2,1,0:T(8,128)(2,1)S(1)}, bf16[5,32,640]{2,1,0:T(8,128)(2,1)S(1)}, u32[]{:S(2)}, u32[]{:S(2)}) collective-permute-start(bf16[5,32,640]{2,1,0:T(8,128)(2,1)S(1)} %get-tuple-element.31), channel_id=1, source_target_pairs={{0,32},{32,0},{64,96},{96,64},{128,160},{160,128},{192,224},{224,1... | collective-permute-start | bytes 614408 | tf_op jit(solution)/shard_map/ppermute | solution.py:101
  14.2 10.6 %collective-permute-start.1 = (bf16[5,32,640]{2,1,0:T(8,128)(2,1)S(1)}, bf16[5,32,640]{2,1,0:T(8,128)(2,1)S(1)}, u32[]{:S(2)}, u32[]{:S(2)}) collective-permute-start(bf16[5,32,640]{2,1,0:T(8,128)(2,1)S(1)} %get-tuple-element.32), channel_id=1, source_target_pairs={{0,480},{32,64},{64,32},{96,128},{128,96},{160,192},{192,160},{224... | collective-permute-start | bytes 614408 | tf_op jit(solution)/shard_map/ppermute | solution.py:100
  24.8 4.4 %all-to-all-done = bf16[16,40,180]{2,1,0:T(8,128)(2,1)S(1)} async-done(((bf16[16,40,180]{2,1,0:T(8,128)(2,1)}), bf16[16,40,180]{2,1,0:T(8,128)(2,1)S(1)}, u32[]{:S(2)}, u32[]{:S(2)}) %all-to-all-start) | async-done | bytes 230432 | tf_op jit(solution)/shard_map/all_to_all | solution.py:61
  29.3 0.3 broadcast_in_dim.63
  29.7 1.0 broadcast_in_dim.64
  30.7 4.0 %all-to-all-start.1 = ((bf16[4,80,1440]{2,1,0:T(8,128)(2,1)}), bf16[4,80,1440]{2,1,0:T(8,128)(2,1)S(1)}, u32[]{:S(2)}, u32[]{:S(2)}) async-start(bf16[4,80,1440]{2,1,0:T(8,128)(2,1)} %broadcast_in_dim.64), calls=%async_computation.1 | async-start | bytes 1966080 | tf_op jit(solution)/shard_map/all_to_all | solution.py:66
  34.8 0.3 select_reduce_fusion
  35.4 7.8 %collective-permute-done.1 = bf16[5,32,640]{2,1,0:T(8,128)(2,1)S(1)} collective-permute-done((bf16[5,32,640]{2,1,0:T(8,128)(2,1)S(1)}, bf16[5,32,640]{2,1,0:T(8,128)(2,1)S(1)}, u32[]{:S(2)}, u32[]{:S(2)}) %collective-permute-start.1) | collective-permute-done | bytes 204832 | tf_op jit(solution)/shard_map/ppermute | solution.py:100
  43.4 0.7 all-to-all-done.1
  44.1 0.9 slice_bitcast_fusion
  45.0 1.6 %concatenate.38 = bf16[80,5760]{1,0:T(8,128)(2,1)S(1)} concatenate(bf16[80,1440]{1,0:T(8,128)(2,1)} %get-tuple-element.28, bf16[80,1440]{1,0:T(8,128)(2,1)} %get-tuple-element.27, bf16[80,1440]{1,0:T(8,128)(2,1)} %get-tuple-element.26, bf16[80,1440]{1,0:T(8,128)(2,1)S(1)} %get-tuple-element.25), dimensions={1} | concatenate | bytes 1843200 | tf_op jit(solution)/shard_map/concatenate | solution.py:67
  46.8 9.9 %collective-permute-start.4 = (bf16[80,5760]{1,0:T(8,128)(2,1)S(1)}, bf16[80,5760]{1,0:T(8,128)(2,1)S(1)}, u32[]{:S(2)}, u32[]{:S(2)}) collective-permute-start(bf16[80,5760]{1,0:T(8,128)(2,1)S(1)} %concatenate.38), channel_id=1, source_target_pairs={{0,32},{32,0},{64,96},{96,64},{128,160},{160,128},{192,224},{224,1... | collective-permute-start | bytes 2764808 | tf_op jit(solution)/shard_map/ppermute | solution.py:94
  56.6 4.6 %collective-permute-start.6 = (bf16[40,5760]{1,0:T(8,128)(2,1)S(1)}, bf16[40,5760]{1,0:T(8,128)(2,1)S(1)}, u32[]{:S(2)}, u32[]{:S(2)}) collective-permute-start(bf16[40,5760]{1,0:T(8,128)(2,1)S(1)} %get-tuple-element.30), channel_id=1, source_target_pairs={{128,0},{160,32},{192,64},{224,96},{256,128},{288,160},{320,192},{... | collective-permute-start | bytes 1382408 | tf_op jit(solution)/shard_map/ppermute | solution.py:83
  61.2 1.9 %collective-permute-start.8 = (bf16[40,5760]{1,0:T(8,128)(2,1)S(1)}, bf16[40,5760]{1,0:T(8,128)(2,1)S(1)}, u32[]{:S(2)}, u32[]{:S(2)}) collective-permute-start(bf16[40,5760]{1,0:T(8,128)(2,1)S(1)} %get-tuple-element.30), channel_id=1, source_target_pairs={{384,0},{416,32},{448,64},{480,96},{0,128},{32,160},{64,192},{96,2... | collective-permute-start | bytes 1382408 | tf_op jit(solution)/shard_map/ppermute | solution.py:84
  63.2 0.9 fusion.12
  64.1 1.8 %fusion.13 = bf16[640,640]{1,0:T(8,128)(2,1)} fusion(bf16[1920,640]{1,0:T(8,128)(2,1)S(1)} %copy-done.9, s32[640]{0:T(1024)S(1)} %fusion.34), kind=kOutput, calls=%fused_computation.24 | convolution fusion | flops 524697600 | bytes 1642496 | tf_op jit(solution)/shard_map/dot_general | solution.py:150
  66.0 4.9 %collective-permute-start.2 = (bf16[6,1,32,640]{3,2,1,0:T(8,128)(2,1)S(1)}, bf16[6,1,32,640]{3,2,1,0:T(8,128)(2,1)S(1)}, u32[]{:S(2)}, u32[]{:S(2)}) collective-permute-start(bf16[6,1,32,640]{3,2,1,0:T(8,128)(2,1)S(1)} %get-tuple-element.21), channel_id=1, source_target_pairs={{0,1},{1,2},{2,3},{3,4},{4,5},{5,6},{6,7},{7,8},{8,9},{9,10},{10,1... | collective-permute-start | bytes 737288 | tf_op jit(solution)/shard_map/ppermute | solution.py:110
  70.9 1.9 %collective-permute-start.3 = (bf16[6,1,32,640]{3,2,1,0:T(8,128)(2,1)S(1)}, bf16[6,1,32,640]{3,2,1,0:T(8,128)(2,1)S(1)}, u32[]{:S(2)}, u32[]{:S(2)}) collective-permute-start(bf16[6,1,32,640]{3,2,1,0:T(8,128)(2,1)S(1)} %get-tuple-element.20), channel_id=1, source_target_pairs={{1,0},{2,1},{3,2},{4,3},{5,4},{6,5},{7,6},{8,7},{9,8},{10,9},{11,1... | collective-permute-start | bytes 737288 | tf_op jit(solution)/shard_map/ppermute | solution.py:111
  72.8 1.9 %fusion.14 = bf16[640,640]{1,0:T(8,128)(2,1)} fusion(bf16[1920,640]{1,0:T(8,128)(2,1)S(1)} %copy-done.9, s32[640]{0:T(1024)S(1)} %fusion.34), kind=kOutput, calls=%fused_computation.25 | convolution fusion | flops 524697600 | bytes 1642496 | tf_op jit(solution)/shard_map/dot_general | solution.py:150
  74.7 1.3 collective-permute-done.2
  76.0 1.9 %collective-permute-start.5 = (bf16[40,5760]{1,0:T(8,128)(2,1)S(1)}, bf16[40,5760]{1,0:T(8,128)(2,1)S(1)}, u32[]{:S(2)}, u32[]{:S(2)}) collective-permute-start(bf16[40,5760]{1,0:T(8,128)(2,1)S(1)} %get-tuple-element.29), channel_id=1, source_target_pairs={{384,0},{416,32},{448,64},{480,96},{0,128},{32,160},{64,192},{96,2... | collective-permute-start | bytes 1382408 | tf_op jit(solution)/shard_map/ppermute | solution.py:82
  77.9 0.2 constant_dynamic-update-slice_fusion.1
  78.1 18.3 %collective-permute-done.3 = bf16[6,1,32,640]{3,2,1,0:T(8,128)(2,1)S(1)} collective-permute-done((bf16[6,1,32,640]{3,2,1,0:T(8,128)(2,1)S(1)}, bf16[6,1,32,640]{3,2,1,0:T(8,128)(2,1)S(1)}, u32[]{:S(2)}, u32[]{:S(2)}) %collective-permute-start.3) | collective-permute-done | bytes 245792 | tf_op jit(solution)/shard_map/ppermute | solution.py:111
  96.5 4.2 %collective-permute-start.9 = (bf16[40,5760]{1,0:T(8,128)(2,1)S(1)}, bf16[40,5760]{1,0:T(8,128)(2,1)S(1)}, u32[]{:S(2)}, u32[]{:S(2)}) collective-permute-start(bf16[40,5760]{1,0:T(8,128)(2,1)S(1)} %get-tuple-element.29), channel_id=1, source_target_pairs={{128,0},{160,32},{192,64},{224,96},{256,128},{288,160},{320,192},{... | collective-permute-start | bytes 1382408 | tf_op jit(solution)/shard_map/ppermute | solution.py:85
  100.8 3.7 %pad_slice_fusion = (bf16[4,7,32,640]{3,2,1,0:T(8,128)(2,1)S(1)}, bf16[4,7,32,640]{3,2,1,0:T(8,128)(2,1)S(1)}, bf16[4,7,32,640]{3,2,1,0:T(8,128)(2,1)S(1)}, bf16...) fusion(bf16[6,7,32,640]{3,2,1,0:T(8,128)(2,1)S(1)} %constant_dy, ...), kind=kLoop, calls=%fused_computation.7 | loop fusion | bytes 15482880 | tf_op jit(solution)/shard_map/slice | solution.py:124
  106.2 3.9 %copy-done.1 = bf16[896,5760]{1,0:T(8,128)(2,1)} copy-done((bf16[896,5760]{1,0:T(8,128)(2,1)}, bf16[896,5760]{1,0:T(8,128)(2,1)S(1)}, u32[]{:S(2)}) %copy-start.1) | copy-done | bytes 10321944
  110.3 3.6 %collective-permute-start.7 = (bf16[80,5760]{1,0:T(8,128)(2,1)S(1)}, bf16[80,5760]{1,0:T(8,128)(2,1)S(1)}, u32[]{:S(2)}, u32[]{:S(2)}) collective-permute-start(bf16[80,5760]{1,0:T(8,128)(2,1)S(1)} %pad_maximum_fusion.3), channel_id=1, source_target_pairs={{0,32},{32,0},{64,96},{96,64},{128,160},{160,128},{192,224},{224,1... | collective-permute-start | bytes 2764808 | tf_op jit(solution)/shard_map/ppermute | solution.py:94
  114.0 1.9 %collective-permute-start.10 = (bf16[80,5760]{1,0:T(8,128)(2,1)S(1)}, bf16[80,5760]{1,0:T(8,128)(2,1)S(1)}, u32[]{:S(2)}, u32[]{:S(2)}) collective-permute-start(bf16[80,5760]{1,0:T(8,128)(2,1)S(1)} %pad_maximum_fusion.4), channel_id=1, source_target_pairs={{0,32},{32,0},{64,96},{96,64},{128,160},{160,128},{192,224},{224,1... | collective-permute-start | bytes 2764808 | tf_op jit(solution)/shard_map/ppermute | solution.py:94
  115.9 2.9 %collective-permute-start.12 = (bf16[40,5760]{1,0:T(8,128)(2,1)S(1)}, bf16[40,5760]{1,0:T(8,128)(2,1)S(1)}, u32[]{:S(2)}, u32[]{:S(2)}) collective-permute-start(bf16[40,5760]{1,0:T(8,128)(2,1)S(1)} %collective-permute-done.6), channel_id=1, source_target_pairs={{128,0},{160,32},{192,64},{224,96},{256,128},{288,160},{320,192},{... | collective-permute-start | bytes 1382408 | tf_op jit(solution)/shard_map/ppermute | solution.py:87
  118.8 2.4 %collective-permute-start.11 = (bf16[40,5760]{1,0:T(8,128)(2,1)S(1)}, bf16[40,5760]{1,0:T(8,128)(2,1)S(1)}, u32[]{:S(2)}, u32[]{:S(2)}) collective-permute-start(bf16[40,5760]{1,0:T(8,128)(2,1)S(1)} %collective-permute-done.5), channel_id=1, source_target_pairs={{384,0},{416,32},{448,64},{480,96},{0,128},{32,160},{64,192},{96,2... | collective-permute-start | bytes 1382408 | tf_op jit(solution)/shard_map/ppermute | solution.py:86
  121.4 8.0 %collective-permute-done.12 = bf16[40,5760]{1,0:T(8,128)(2,1)S(1)} collective-permute-done((bf16[40,5760]{1,0:T(8,128)(2,1)S(1)}, bf16[40,5760]{1,0:T(8,128)(2,1)S(1)}, u32[]{:S(2)}, u32[]{:S(2)}) %collective-permute-start.12) | collective-permute-done | bytes 460832 | tf_op jit(solution)/shard_map/ppermute | solution.py:87
  129.4 4.3 %collective-permute-done.11 = bf16[40,5760]{1,0:T(8,128)(2,1)S(1)} collective-permute-done((bf16[40,5760]{1,0:T(8,128)(2,1)S(1)}, bf16[40,5760]{1,0:T(8,128)(2,1)S(1)}, u32[]{:S(2)}, u32[]{:S(2)}) %collective-permute-start.11) | collective-permute-done | bytes 460832 | tf_op jit(solution)/shard_map/ppermute | solution.py:86
  133.8 3.2 %collective-permute-start.13 = (bf16[80,5760]{1,0:T(8,128)(2,1)S(1)}, bf16[80,5760]{1,0:T(8,128)(2,1)S(1)}, u32[]{:S(2)}, u32[]{:S(2)}) collective-permute-start(bf16[80,5760]{1,0:T(8,128)(2,1)S(1)} %pad_maximum_fusion.5), channel_id=1, source_target_pairs={{0,32},{32,0},{64,96},{96,64},{128,160},{160,128},{192,224},{224,1... | collective-permute-start | bytes 2764808 | tf_op jit(solution)/shard_map/ppermute | solution.py:94
  137.4 0.4 slice-done
  137.8 6.1 %select_convert_fusion = bf16[896,480]{0,1:T(8,128)(2,1)S(1)} fusion(bf16[896,5760]{1,0:T(8,128)(2,1)S(1)} %copy-done.2, bf16[480,5760]{1,0:T(8,128)(2,1)S(1)} %constant_dynamic-update-slice_fusion.12, f32[480]{0:T(512)S(1)} %slice-done, pred[896]{0:T(1024)(128)(4,1)S(1)} %or.14), kind=kOutput, calls=%fused_computation.19 | convolution fusion | flops 4957532160 | bytes 16714496 | tf_op jit(solution)/shard_map/dot_general | solution.py:139
  143.9 3.3 %select_convert_fusion.1 = bf16[896,160]{0,1:T(8,128)(2,1)S(1)} fusion(bf16[896,5760]{1,0:T(8,128)(2,1)S(1)} %copy-done.2, bf16[80,5760]{1,0:T(8,128)(2,1)S(1)} %collective-permute-done.13, bf16[40,5760]{1,0:T(8,128)(2,1)S(1)} %collective-permute-done.12, bf16[40,5760]{1,0:T(8,128)(2,1)S(1)} %collective-permute-done.11, f32[160]{0:T(256)S(1)} %slice.106, ...), kind=kOutput, calls=%fused_computation.41 | convolution fusion | flops 1658040320 | bytes 12453376 | tf_op jit(solution)/shard_map/dot_general | solution.py:139
  147.4 1.1 copy.24
  148.5 0.2 fusion.39
  148.8 0.2 pad_maximum_fusion
  149.0 0.4 copy-done.10
  149.4 0.5 copy-done.11
  149.9 0.2 copy-done.12
  150.2 2.2 %fusion.15 = f32[640,640]{1,0:T(8,128)S(1)} fusion(bf16[640,1920]{1,0:T(8,128)(2,1)S(1)} %bitcast.57, bf16[640,640]{1,0:T(8,128)(2,1)S(1)} %fusion.12, bf16[640,640]{1,0:T(8,128)(2,1)S(1)} %copy-done.11, bf16[640,640]{1,0:T(8,128)(2,1)S(1)} %copy-done.12, f32[640]{0:T(1024)S(1)} %copy-done.10), kind=kOutput, calls=%fused_computation.26 | convolution fusion | flops 1580646400 | bytes 6556160 | tf_op jit(solution)/shard_map/dot_general | solution.py:153
  152.3 0.4 fusion.27
  152.8 1.3 copy.25
  (66 shorter events, 3.4 us)
Async XLA Ops:
  1.5 27.8 %all-to-all-start = ((bf16[16,40,180]{2,1,0:T(8,128)(2,1)}), bf16[16,40,180]{2,1,0:T(8,128)(2,1)S(1)}, u32[]{:S(2)}, u32[]{:S(2)}) async-start(bf16[16,40,180]{2,1,0:T(8,128)(2,1)} %broadcast_in_dim.62), calls=%async_computation | async-start | bytes 655360 | tf_op jit(solution)/shard_map/all_to_all | solution.py:61
  11.1 24.3 %collective-permute-start = (bf16[5,32,640]{2,1,0:T(8,128)(2,1)S(1)}, bf16[5,32,640]{2,1,0:T(8,128)(2,1)S(1)}, u32[]{:S(2)}, u32[]{:S(2)}) collective-permute-start(bf16[5,32,640]{2,1,0:T(8,128)(2,1)S(1)} %get-tuple-element.31), channel_id=1, source_target_pairs={{0,32},{32,0},{64,96},{96,64},{128,160},{160,128},{192,224},{224,1... | collective-permute-start | bytes 614408 | tf_op jit(solution)/shard_map/ppermute | solution.py:101
  14.2 28.9 %collective-permute-start.1 = (bf16[5,32,640]{2,1,0:T(8,128)(2,1)S(1)}, bf16[5,32,640]{2,1,0:T(8,128)(2,1)S(1)}, u32[]{:S(2)}, u32[]{:S(2)}) collective-permute-start(bf16[5,32,640]{2,1,0:T(8,128)(2,1)S(1)} %get-tuple-element.32), channel_id=1, source_target_pairs={{0,480},{32,64},{64,32},{96,128},{128,96},{160,192},{192,160},{224... | collective-permute-start | bytes 614408 | tf_op jit(solution)/shard_map/ppermute | solution.py:100
  29.3 5.5 %copy-start.5 = (s32[640]{0:T(1024)S(1)}, s32[640]{0:T(1024)}, u32[]{:S(2)}) copy-start(s32[640]{0:T(1024)} %constant.73.clone) | copy-start | bytes 7684
  29.3 5.5 %copy-start.6 = (s32[640]{0:T(1024)S(1)}, s32[640]{0:T(1024)}, u32[]{:S(2)}) copy-start(s32[640]{0:T(1024)} %constant.78) | copy-start | bytes 7684
  29.3 5.5 %copy-start.7 = (s32[640]{0:T(1024)S(1)}, s32[640]{0:T(1024)}, u32[]{:S(2)}) copy-start(s32[640]{0:T(1024)} %constant.70.clone) | copy-start | bytes 7684
  29.3 5.5 %copy-start.8 = (s32[640]{0:T(1024)S(1)}, s32[640]{0:T(1024)}, u32[]{:S(2)}) copy-start(s32[640]{0:T(1024)} %constant.72.clone) | copy-start | bytes 7684
  29.3 5.5 %copy-start.4 = (f32[640]{0:T(1024)S(1)}, f32[640]{0:T(1024)}, u32[]{:S(2)}) copy-start(f32[640]{0:T(1024)} %param.11) | copy-start | bytes 7684
  30.7 13.4 %all-to-all-start.1 = ((bf16[4,80,1440]{2,1,0:T(8,128)(2,1)}), bf16[4,80,1440]{2,1,0:T(8,128)(2,1)S(1)}, u32[]{:S(2)}, u32[]{:S(2)}) async-start(bf16[4,80,1440]{2,1,0:T(8,128)(2,1)} %broadcast_in_dim.64), calls=%async_computation.1 | async-start | bytes 1966080 | tf_op jit(solution)/shard_map/all_to_all | solution.py:66
  35.1 9.9 %copy-start.3 = (f32[640]{0:T(1024)}, f32[640]{0:T(1024)S(1)}, u32[]{:S(2)}) copy-start(f32[640]{0:T(1024)S(1)} %select_reduce_fusion) | copy-start | bytes 7684
  46.6 16.5 %copy-start.9 = (bf16[1920,640]{1,0:T(8,128)(2,1)S(1)}, bf16[1920,640]{1,0:T(8,128)(2,1)}, u32[]{:S(2)}) copy-start(bf16[1920,640]{1,0:T(8,128)(2,1)} %param.12) | copy-start | bytes 7372804
  46.8 74.4 %collective-permute-start.4 = (bf16[80,5760]{1,0:T(8,128)(2,1)S(1)}, bf16[80,5760]{1,0:T(8,128)(2,1)S(1)}, u32[]{:S(2)}, u32[]{:S(2)}) collective-permute-start(bf16[80,5760]{1,0:T(8,128)(2,1)S(1)} %concatenate.38), channel_id=1, source_target_pairs={{0,32},{32,0},{64,96},{96,64},{128,160},{160,128},{192,224},{224,1... | collective-permute-start | bytes 2764808 | tf_op jit(solution)/shard_map/ppermute | solution.py:94
  56.6 49.6 %collective-permute-start.6 = (bf16[40,5760]{1,0:T(8,128)(2,1)S(1)}, bf16[40,5760]{1,0:T(8,128)(2,1)S(1)}, u32[]{:S(2)}, u32[]{:S(2)}) collective-permute-start(bf16[40,5760]{1,0:T(8,128)(2,1)S(1)} %get-tuple-element.30), channel_id=1, source_target_pairs={{128,0},{160,32},{192,64},{224,96},{256,128},{288,160},{320,192},{... | collective-permute-start | bytes 1382408 | tf_op jit(solution)/shard_map/ppermute | solution.py:83
  61.2 52.7 %collective-permute-start.8 = (bf16[40,5760]{1,0:T(8,128)(2,1)S(1)}, bf16[40,5760]{1,0:T(8,128)(2,1)S(1)}, u32[]{:S(2)}, u32[]{:S(2)}) collective-permute-start(bf16[40,5760]{1,0:T(8,128)(2,1)S(1)} %get-tuple-element.30), channel_id=1, source_target_pairs={{384,0},{416,32},{448,64},{480,96},{0,128},{32,160},{64,192},{96,2... | collective-permute-start | bytes 1382408 | tf_op jit(solution)/shard_map/ppermute | solution.py:84
  66.0 10.0 %collective-permute-start.2 = (bf16[6,1,32,640]{3,2,1,0:T(8,128)(2,1)S(1)}, bf16[6,1,32,640]{3,2,1,0:T(8,128)(2,1)S(1)}, u32[]{:S(2)}, u32[]{:S(2)}) collective-permute-start(bf16[6,1,32,640]{3,2,1,0:T(8,128)(2,1)S(1)} %get-tuple-element.21), channel_id=1, source_target_pairs={{0,1},{1,2},{2,3},{3,4},{4,5},{5,6},{6,7},{7,8},{8,9},{9,10},{10,1... | collective-permute-start | bytes 737288 | tf_op jit(solution)/shard_map/ppermute | solution.py:110
  70.9 25.6 %collective-permute-start.3 = (bf16[6,1,32,640]{3,2,1,0:T(8,128)(2,1)S(1)}, bf16[6,1,32,640]{3,2,1,0:T(8,128)(2,1)S(1)}, u32[]{:S(2)}, u32[]{:S(2)}) collective-permute-start(bf16[6,1,32,640]{3,2,1,0:T(8,128)(2,1)S(1)} %get-tuple-element.20), channel_id=1, source_target_pairs={{1,0},{2,1},{3,2},{4,3},{5,4},{6,5},{7,6},{8,7},{9,8},{10,9},{11,1... | collective-permute-start | bytes 737288 | tf_op jit(solution)/shard_map/ppermute | solution.py:111
  76.0 34.2 %collective-permute-start.5 = (bf16[40,5760]{1,0:T(8,128)(2,1)S(1)}, bf16[40,5760]{1,0:T(8,128)(2,1)S(1)}, u32[]{:S(2)}, u32[]{:S(2)}) collective-permute-start(bf16[40,5760]{1,0:T(8,128)(2,1)S(1)} %get-tuple-element.29), channel_id=1, source_target_pairs={{384,0},{416,32},{448,64},{480,96},{0,128},{32,160},{64,192},{96,2... | collective-permute-start | bytes 1382408 | tf_op jit(solution)/shard_map/ppermute | solution.py:82
  96.5 17.4 %collective-permute-start.9 = (bf16[40,5760]{1,0:T(8,128)(2,1)S(1)}, bf16[40,5760]{1,0:T(8,128)(2,1)S(1)}, u32[]{:S(2)}, u32[]{:S(2)}) collective-permute-start(bf16[40,5760]{1,0:T(8,128)(2,1)S(1)} %get-tuple-element.29), channel_id=1, source_target_pairs={{128,0},{160,32},{192,64},{224,96},{256,128},{288,160},{320,192},{... | collective-permute-start | bytes 1382408 | tf_op jit(solution)/shard_map/ppermute | solution.py:85
  106.2 4.0 %copy-start.1 = (bf16[896,5760]{1,0:T(8,128)(2,1)}, bf16[896,5760]{1,0:T(8,128)(2,1)S(1)}, u32[]{:S(2)}) copy-start(bf16[896,5760]{1,0:T(8,128)(2,1)S(1)} %constant_dynamic-update-slice_fusion.3) | copy-start | bytes 30965764
  110.3 26.8 %collective-permute-start.7 = (bf16[80,5760]{1,0:T(8,128)(2,1)S(1)}, bf16[80,5760]{1,0:T(8,128)(2,1)S(1)}, u32[]{:S(2)}, u32[]{:S(2)}) collective-permute-start(bf16[80,5760]{1,0:T(8,128)(2,1)S(1)} %pad_maximum_fusion.3), channel_id=1, source_target_pairs={{0,32},{32,0},{64,96},{96,64},{128,160},{160,128},{192,224},{224,1... | collective-permute-start | bytes 2764808 | tf_op jit(solution)/shard_map/ppermute | solution.py:94
  114.0 23.3 %collective-permute-start.10 = (bf16[80,5760]{1,0:T(8,128)(2,1)S(1)}, bf16[80,5760]{1,0:T(8,128)(2,1)S(1)}, u32[]{:S(2)}, u32[]{:S(2)}) collective-permute-start(bf16[80,5760]{1,0:T(8,128)(2,1)S(1)} %pad_maximum_fusion.4), channel_id=1, source_target_pairs={{0,32},{32,0},{64,96},{96,64},{128,160},{160,128},{192,224},{224,1... | collective-permute-start | bytes 2764808 | tf_op jit(solution)/shard_map/ppermute | solution.py:94
  115.9 13.5 %collective-permute-start.12 = (bf16[40,5760]{1,0:T(8,128)(2,1)S(1)}, bf16[40,5760]{1,0:T(8,128)(2,1)S(1)}, u32[]{:S(2)}, u32[]{:S(2)}) collective-permute-start(bf16[40,5760]{1,0:T(8,128)(2,1)S(1)} %collective-permute-done.6), channel_id=1, source_target_pairs={{128,0},{160,32},{192,64},{224,96},{256,128},{288,160},{320,192},{... | collective-permute-start | bytes 1382408 | tf_op jit(solution)/shard_map/ppermute | solution.py:87
  118.8 15.0 %collective-permute-start.11 = (bf16[40,5760]{1,0:T(8,128)(2,1)S(1)}, bf16[40,5760]{1,0:T(8,128)(2,1)S(1)}, u32[]{:S(2)}, u32[]{:S(2)}) collective-permute-start(bf16[40,5760]{1,0:T(8,128)(2,1)S(1)} %collective-permute-done.5), channel_id=1, source_target_pairs={{384,0},{416,32},{448,64},{480,96},{0,128},{32,160},{64,192},{96,2... | collective-permute-start | bytes 1382408 | tf_op jit(solution)/shard_map/ppermute | solution.py:86
  121.2 16.2 %copy-start.2 = (bf16[896,5760]{1,0:T(8,128)(2,1)S(1)}, bf16[896,5760]{1,0:T(8,128)(2,1)}, u32[]{:S(2)}) copy-start(bf16[896,5760]{1,0:T(8,128)(2,1)} %copy-done.1) | copy-start | bytes 30965764
  133.8 10.1 %collective-permute-start.13 = (bf16[80,5760]{1,0:T(8,128)(2,1)S(1)}, bf16[80,5760]{1,0:T(8,128)(2,1)S(1)}, u32[]{:S(2)}, u32[]{:S(2)}) collective-permute-start(bf16[80,5760]{1,0:T(8,128)(2,1)S(1)} %pad_maximum_fusion.5), channel_id=1, source_target_pairs={{0,32},{32,0},{64,96},{96,64},{128,160},{160,128},{192,224},{224,1... | collective-permute-start | bytes 2764808 | tf_op jit(solution)/shard_map/ppermute | solution.py:94
  137.2 0.7 slice-start
  148.7 0.7 copy-start.10
  148.8 1.2 copy-start.11
  148.8 1.4 copy-start.12
  150.2 2.2 %copy-start = (bf16[5,32,4,640]{3,2,1,0:T(4,128)(2,1)S(1)}, bf16[5,32,4,640]{3,2,1,0:T(4,128)(2,1)}, u32[]{:S(2)}) copy-start(bf16[5,32,4,640]{3,2,1,0:T(4,128)(2,1)} %param.9) | copy-start | bytes 2457604

commit v3 on v1

v3 whole, which is shorter than its diff:
```python
import jax
import jax.numpy as jnp
import numpy as np
from jax import lax
from jax.sharding import PartitionSpec as P

LONS = 16
FRAMES_AXIS = 32
Y = 4
X = 4
Z_LO = 8


def lon_index(y, z_hi, core):
    return y * 4 + z_hi * 2 + core


def frame_index(x, z_lo):
    return x * Z_LO + z_lo


def z_groups():
    return [
        [
            lon_index(y, z_hi, core) * FRAMES_AXIS + frame_index(x, z_lo)
            for z_hi in range(2)
            for z_lo in range(Z_LO)
        ]
        for x in range(X)
        for y in range(Y)
        for core in range(2)
    ]


def x_groups():
    return [[frame_index(x, z_lo) for x in range(X)] for z_lo in range(Z_LO)]


def from_y(k):
    return [(((y + k) % Y) * 4 + r, y * 4 + r) for y in range(Y) for r in range(4)]


CORES = [(i, i ^ 1) for i in range(LONS)]
FAR = [(i, (i + 1) % LONS if i % 2 else (i - 1) % LONS) for i in range(LONS)]


def copies(piece, count):
    return jnp.broadcast_to(piece[None], (count,) + piece.shape)


def gather_z(spatial_kernel):
    shard = spatial_kernel.T
    cols, rows = shard.shape
    along_z = lax.all_to_all(
        copies(shard, 16), ("lon", "frame"), 0, 0, axis_index_groups=z_groups()
    )
    along_z = along_z.reshape(2, Z_LO, cols, rows)
    return [jnp.concatenate([along_z[h, z] for z in range(Z_LO)], axis=1) for h in range(2)]


def over_x(block):
    return lax.all_to_all(copies(block, X), "frame", 0, 0, axis_index_groups=x_groups())


def over_y(block):
    return [block] + [lax.ppermute(block, "lon", from_y(k)) for k in (1, 2, 3)]


def joined_rows(along_x):
    return jnp.concatenate([along_x[x] for x in range(X)], axis=1)


def channel_order():
    lon = lax.axis_index("lon")
    blocks = [(y, z_hi, side) for side in range(2) for z_hi in range(2) for y in range(Y)]
    row, z_hi, side = (jnp.asarray(np.repeat(np.array(v), 40)) for v in zip(*blocks))
    within = jnp.asarray(np.tile(np.arange(40), LONS))
    row = lax.rem(lon // 4 + row, Y)
    return lon_index(row, z_hi, (lon % 2) ^ side) * 40 + within


def lon_halos(columns):
    core = lax.axis_index("lon") % 2
    far = lax.ppermute(jnp.where(core == 1, columns[-1], columns[0]), "lon", FAR)
    near = lax.ppermute(jnp.where(core == 1, columns[0], columns[-1]), "lon", CORES)
    return far, near


def frame_halos(wide):
    up = [(i, i + 1) for i in range(FRAMES_AXIS - 1)]
    down = [(i + 1, i) for i in range(FRAMES_AXIS - 1)]
    earlier = lax.ppermute(wide[:, -1:], "frame", up)
    later = lax.ppermute(wide[:, :1], "frame", down)
    return earlier, later


def tap_rows(wide, lon_cols, lat_rows):
    padded = jnp.pad(wide, ((0, 0), (0, 0), (1, 1), (0, 0)))
    taps = [
        padded[b : b + lon_cols, :, a : a + lat_rows].reshape(-1, padded.shape[-1])
        for a in range(3)
        for b in range(3)
    ]
    return jnp.concatenate(taps, axis=-1)


def active(rows, kernel_rows, bias):
    summed = lax.dot_general(
        rows, kernel_rows, (((1,), (1,)), ((), ())), preferred_element_type=jnp.float32
    )
    return jax.nn.silu(summed + bias)


def body(latents, spatial_kernel, spatial_bias, temporal_kernel, temporal_bias):
    frames, lat_rows, lon_cols, channels = latents.shape
    core = lax.axis_index("lon") % 2
    columns = latents.transpose(2, 0, 1, 3)
    far, near = lon_halos(columns)
    low, high = gather_z(spatial_kernel)
    high = jnp.concatenate(over_y(high))
    low = joined_rows(over_x(low))
    _, _, temporal_kernel = lax.optimization_barrier((low, high, temporal_kernel))
    low = over_y(low)
    high = over_x(high)
    far, near, columns, _ = lax.optimization_barrier((far, near, columns, low[1]))
    low = jnp.concatenate(low)

    order = channel_order()[:, None] == lax.broadcasted_iota(jnp.int32, (channels, channels), 1)
    ordered = [
        jnp.dot(order.astype(jnp.bfloat16), temporal_kernel[k * channels : (k + 1) * channels])
        for k in range(3)
    ]
    ordered = jnp.concatenate(ordered, axis=0)
    bias = jnp.sum(jnp.where(order, spatial_bias[None, :], 0.0), axis=1)

    before = jnp.where(core == 1, near, far)
    after = jnp.where(core == 1, far, near)
    wide = jnp.concatenate([before[None], columns, after[None]], axis=0)
    inner_rows = tap_rows(wide, lon_cols, lat_rows)
    earlier, later = frame_halos(wide)

    other_low = lax.ppermute(low, "lon", CORES)
    other_high = joined_rows(lax.ppermute(high, "lon", CORES))
    middle = jnp.concatenate([joined_rows(high), other_low])
    groups = (low, middle, other_high)
    ends = np.cumsum([rows.shape[0] for rows in groups])
    biases = [bias[end - rows.shape[0] : end] for rows, end in zip(groups, ends)]
    inner = [active(inner_rows, rows, part) for rows, part in zip(groups[:2], biases)]
    earlier, later, inner[1] = lax.optimization_barrier((earlier, later, inner[1]))
    outer_rows = tap_rows(jnp.concatenate([earlier, later], axis=1), lon_cols, lat_rows)
    outer = [active(outer_rows, rows, part) for rows, part in zip(groups, biases)]
    inner.append(active(inner_rows, groups[2], biases[2]))

    inner = jnp.concatenate(inner, axis=-1).astype(jnp.bfloat16)
    inner = inner.reshape(lon_cols, frames, lat_rows, channels)
    outer = jnp.concatenate(outer, axis=-1).astype(jnp.bfloat16)
    outer = outer.reshape(lon_cols, 2, lat_rows, channels)
    frame = lax.axis_index("frame")
    first = jnp.where(frame == 0, 0, outer[:, :1])
    final = jnp.where(frame == FRAMES_AXIS - 1, 0, outer[:, 1:])
    hidden = jnp.concatenate([first, inner, final], axis=1)

    stacked = jnp.concatenate([hidden[:, k : k + frames] for k in range(3)], axis=-1)
    mixed = jnp.dot(
        stacked.reshape(-1, 3 * channels), ordered, preferred_element_type=jnp.float32
    )
    mixed = (mixed + temporal_bias).reshape(lon_cols, frames, lat_rows, channels)
    result = columns.astype(jnp.float32) + jax.nn.silu(mixed)
    return result.astype(jnp.bfloat16).transpose(1, 2, 0, 3)


def solution(mesh):
    placed = (P("frame", None, "lon", None), P("frame", "lon"), P(), P(), P())
    return jax.shard_map(
        body, mesh=mesh, in_specs=placed, out_specs=P("frame", None, "lon", None), check_vma=False
    )
```

time: 150 us -> 177 us (1.18)
  the two profiles are of different devices: /device:TPU:1 before, /device:TPU:11 now
where the time goes in v3:
time: 177 us; the launch traced here: 175 us
  starting transfers between devices  86.2 us (49%)
  matrix products  38.3 us (22%)
  local copies, waits for them, and re-layouts  38.1 us (22%)
  other arithmetic  6.74 us (4%)
  waiting for transfers between devices  5.23 us (3%)
    dot_general x6, matrix products, active(): lax.dot_general(rows, kernel_rows, (((1,), (1,)), ((), ())), preferred_el...  27 us
    ppermute x6, starting transfers between devices, over_y(): return [block] + [lax.ppermute(block, 'lon', from_y(k)) for k in (1, 2, 3)]  18.7 us
    all_to_all x1, starting transfers between devices, gather_z(): lax.all_to_all(copies(shard, 16), ('lon', 'frame'), 0, 0, axis_index_grou...  14.9 us
    ppermute x1, starting transfers between devices, body(): other_low = lax.ppermute(low, 'lon', CORES)  13.7 us
    ppermute x1, starting transfers between devices, lon_halos(): lax.ppermute(jnp.where(core == 1, columns[-1], columns[0]), 'lon', FAR)  13.1 us
    all_to_all x2, starting transfers between devices, over_x(): lax.all_to_all(copies(block, X), 'frame', 0, 0, axis_index_groups=x_group...  9.01 us
    concatenate x3, local copies, waits for them, and re-layouts, joined_rows(): return jnp.concatenate([along_x[x] for x in range(X)], axis=1)  8 us
    ppermute x1, starting transfers between devices, frame_halos(): later = lax.ppermute(wide[:, :1], 'frame', down)  7.74 us
  transfers between devices with their start and end apart: 15, of which 1 were waited for; matrix products, arithmetic and copies ran while one was open for 29% of the time, Pallas kernels for 0%

profile of v3, /device:TPU:11, one launch (start us, length us, event | category | flops | bytes accessed | tf_op | source)
XLA Modules:
  0.0 175.3 jit_solution(736665571309410076)
XLA Ops:
  0.0 1.5 broadcast_in_dim.26
  1.6 14.9 %all-to-all-start = ((bf16[16,40,180]{2,1,0:T(8,128)(2,1)}), bf16[16,40,180]{2,1,0:T(8,128)(2,1)S(1)}, u32[]{:S(2)}, u32[]{:S(2)}) async-start(bf16[16,40,180]{2,1,0:T(8,128)(2,1)} %broadcast_in_dim.26), calls=%async_computation | async-start | bytes 655360 | tf_op jit(solution)/shard_map/all_to_all | solution.py:54
  16.5 1.2 copy.39
  18.5 13.1 %collective-permute-start = (bf16[5,32,640]{2,1,0:T(8,128)(2,1)}, bf16[5,32,640]{2,1,0:T(8,128)(2,1)}, u32[]{:S(2)}, u32[]{:S(2)}) collective-permute-start(bf16[5,32,640]{2,1,0:T(8,128)(2,1)} %get-tuple-element.40), channel_id=1, source_target_pairs={{0,480},{32,64},{64,32},{96,128},{128,96},{160,192},{192,160},{224... | collective-permute-start | bytes 614408 | tf_op jit(solution)/shard_map/ppermute | solution.py:84
  31.6 1.9 %collective-permute-start.1 = (bf16[5,32,640]{2,1,0:T(8,128)(2,1)}, bf16[5,32,640]{2,1,0:T(8,128)(2,1)}, u32[]{:S(2)}, u32[]{:S(2)}) collective-permute-start(bf16[5,32,640]{2,1,0:T(8,128)(2,1)} %get-tuple-element.39), channel_id=1, source_target_pairs={{0,32},{32,0},{64,96},{96,64},{128,160},{160,128},{192,224},{224,1... | collective-permute-start | bytes 614408 | tf_op jit(solution)/shard_map/ppermute | solution.py:85
  34.2 3.2 %collective-permute-start.7 = (bf16[40,1440]{1,0:T(8,128)(2,1)S(1)}, bf16[40,1440]{1,0:T(8,128)(2,1)S(1)}, u32[]{:S(2)}, u32[]{:S(2)}) collective-permute-start(bf16[40,1440]{1,0:T(8,128)(2,1)S(1)} %concatenate.91), channel_id=1, source_target_pairs={{384,0},{416,32},{448,64},{480,96},{0,128},{32,160},{64,192},{96,2... | collective-permute-start | bytes 345608 | tf_op jit(solution)/shard_map/ppermute | solution.py:66
  37.4 4.3 %collective-permute-start.6 = (bf16[40,1440]{1,0:T(8,128)(2,1)S(1)}, bf16[40,1440]{1,0:T(8,128)(2,1)S(1)}, u32[]{:S(2)}, u32[]{:S(2)}) collective-permute-start(bf16[40,1440]{1,0:T(8,128)(2,1)S(1)} %concatenate.91), channel_id=1, source_target_pairs={{256,0},{288,32},{320,64},{352,96},{384,128},{416,160},{448,192},{... | collective-permute-start | bytes 345608 | tf_op jit(solution)/shard_map/ppermute | solution.py:66
  41.7 2.3 %collective-permute-start.5 = (bf16[40,1440]{1,0:T(8,128)(2,1)S(1)}, bf16[40,1440]{1,0:T(8,128)(2,1)S(1)}, u32[]{:S(2)}, u32[]{:S(2)}) collective-permute-start(bf16[40,1440]{1,0:T(8,128)(2,1)S(1)} %concatenate.91), channel_id=1, source_target_pairs={{128,0},{160,32},{192,64},{224,96},{256,128},{288,160},{320,192},{... | collective-permute-start | bytes 345608 | tf_op jit(solution)/shard_map/ppermute | solution.py:66
  45.0 4.3 %all-to-all-start.1 = ((bf16[4,40,1440]{2,1,0:T(8,128)(2,1)}), bf16[4,40,1440]{2,1,0:T(8,128)(2,1)S(1)}, u32[]{:S(2)}, u32[]{:S(2)}) async-start(bf16[4,40,1440]{2,1,0:T(8,128)(2,1)} %broadcast_in_dim.27), calls=%async_computation.1 | async-start | bytes 983040 | tf_op jit(solution)/shard_map/all_to_all | solution.py:62
  50.0 5.2 %all-to-all-done.1 = bf16[4,40,1440]{2,1,0:T(8,128)(2,1)S(1)} async-done(((bf16[4,40,1440]{2,1,0:T(8,128)(2,1)}), bf16[4,40,1440]{2,1,0:T(8,128)(2,1)S(1)}, u32[]{:S(2)}, u32[]{:S(2)}) %all-to-all-start.1) | async-done | bytes 460832 | tf_op jit(solution)/shard_map/all_to_all | solution.py:62
  55.2 1.5 broadcast_in_dim.32
  56.7 4.7 %all-to-all-start.2 = ((bf16[4,160,1440]{2,1,0:T(8,128)(2,1)}), bf16[4,160,1440]{2,1,0:T(8,128)(2,1)S(1)}, u32[]{:S(2)}, u32[]{:S(2)}) async-start(bf16[4,160,1440]{2,1,0:T(8,128)(2,1)} %broadcast_in_dim.32), calls=%async_computation.2 | async-start | bytes 3932160 | tf_op jit(solution)/shard_map/all_to_all | solution.py:62
  62.2 1.3 concatenate.86
  63.5 3.2 %collective-permute-start.2 = (bf16[40,5760]{1,0:T(8,128)(2,1)S(1)}, bf16[40,5760]{1,0:T(8,128)(2,1)S(1)}, u32[]{:S(2)}, u32[]{:S(2)}) collective-permute-start(bf16[40,5760]{1,0:T(8,128)(2,1)S(1)} %concatenate.86), channel_id=1, source_target_pairs={{128,0},{160,32},{192,64},{224,96},{256,128},{288,160},{320,192},{... | collective-permute-start | bytes 1382408 | tf_op jit(solution)/shard_map/ppermute | solution.py:66
  66.7 2.3 %collective-permute-start.9 = (bf16[40,5760]{1,0:T(8,128)(2,1)S(1)}, bf16[40,5760]{1,0:T(8,128)(2,1)S(1)}, u32[]{:S(2)}, u32[]{:S(2)}) collective-permute-start(bf16[40,5760]{1,0:T(8,128)(2,1)S(1)} %concatenate.86), channel_id=1, source_target_pairs={{384,0},{416,32},{448,64},{480,96},{0,128},{32,160},{64,192},{96,2... | collective-permute-start | bytes 1382408 | tf_op jit(solution)/shard_map/ppermute | solution.py:66
  69.1 3.3 %collective-permute-start.8 = (bf16[40,5760]{1,0:T(8,128)(2,1)S(1)}, bf16[40,5760]{1,0:T(8,128)(2,1)S(1)}, u32[]{:S(2)}, u32[]{:S(2)}) collective-permute-start(bf16[40,5760]{1,0:T(8,128)(2,1)S(1)} %concatenate.86), channel_id=1, source_target_pairs={{256,0},{288,32},{320,64},{352,96},{384,128},{416,160},{448,192},{... | collective-permute-start | bytes 1382408 | tf_op jit(solution)/shard_map/ppermute | solution.py:66
  72.4 3.0 %fusion.8 = bf16[640,640]{1,0:T(8,128)(2,1)} fusion(bf16[1920,640]{1,0:T(8,128)(2,1)} %param.12, s32[640]{0:T(1024)S(1)} %fusion.27), kind=kOutput, calls=%fused_computation.13 | convolution fusion | flops 524697600 | bytes 1640960 | tf_op jit(solution)/shard_map/dot_general | solution.py:130
  75.4 1.9 %fusion.9 = bf16[640,640]{1,0:T(8,128)(2,1)} fusion(bf16[1920,640]{1,0:T(8,128)(2,1)S(1)} %copy-done.19, s32[640]{0:T(1024)S(1)} %fusion.27), kind=kOutput, calls=%fused_computation.14 | convolution fusion | flops 524697600 | bytes 1642496 | tf_op jit(solution)/shard_map/dot_general | solution.py:130
  77.2 1.9 %fusion.10 = bf16[640,640]{1,0:T(8,128)(2,1)} fusion(bf16[1920,640]{1,0:T(8,128)(2,1)S(1)} %copy-done.19, s32[640]{0:T(1024)S(1)} %fusion.27), kind=kOutput, calls=%fused_computation.15 | convolution fusion | flops 524697600 | bytes 1642496 | tf_op jit(solution)/shard_map/dot_general | solution.py:130
  79.1 1.2 select_bitcast_fusion.1
  80.5 0.8 fusion.32
  81.3 5.0 %collective-permute-start.3 = (bf16[6,1,32,640]{3,2,1,0:T(8,128)(2,1)}, bf16[6,1,32,640]{3,2,1,0:T(8,128)(2,1)S(1)}, u32[]{:S(2)}, u32[]{:S(2)}) collective-permute-start(bf16[6,1,32,640]{3,2,1,0:T(8,128)(2,1)} %get-tuple-element.34), channel_id=1, source_target_pairs={{0,1},{1,2},{2,3},{3,4},{4,5},{5,6},{6,7},{7,8},{8,9},{9,10},{10,1... | collective-permute-start | bytes 737288 | tf_op jit(solution)/shard_map/ppermute | solution.py:92
  86.4 7.7 %collective-permute-start.4 = (bf16[6,1,32,640]{3,2,1,0:T(8,128)(2,1)}, bf16[6,1,32,640]{3,2,1,0:T(8,128)(2,1)}, u32[]{:S(2)}, u32[]{:S(2)}) collective-permute-start(bf16[6,1,32,640]{3,2,1,0:T(8,128)(2,1)} %get-tuple-element.33), channel_id=1, source_target_pairs={{1,0},{2,1},{3,2},{4,3},{5,4},{6,5},{7,6},{8,7},{9,8},{10,9},{11,1... | collective-permute-start | bytes 737288 | tf_op jit(solution)/shard_map/ppermute | solution.py:93
  94.1 0.9 pad_slice_fusion
  95.4 1.5 pad_maximum_fusion.3
  96.9 13.7 %collective-permute-start.10 = (bf16[160,5760]{1,0:T(8,128)(2,1)}, bf16[160,5760]{1,0:T(8,128)(2,1)}, u32[]{:S(2)}, u32[]{:S(2)}) collective-permute-start(bf16[160,5760]{1,0:T(8,128)(2,1)} %pad_maximum_fusion.3), channel_id=1, source_target_pairs={{0,32},{32,0},{64,96},{96,64},{128,160},{160,128},{192,224},{224,1... | collective-permute-start | bytes 5529608 | tf_op jit(solution)/shard_map/ppermute | solution.py:142
  111.8 2.9 %copy-done.9 = bf16[640,5760]{1,0:T(8,128)(2,1)} copy-done((bf16[640,5760]{1,0:T(8,128)(2,1)}, bf16[640,5760]{1,0:T(8,128)(2,1)S(1)}, u32[]{:S(2)}) %copy-start.9) | copy-done | bytes 7372824
  114.7 3.0 %multiply_convert_fusion.1 = bf16[640,160]{0,1:T(8,128)(2,1)} fusion(bf16[640,5760]{1,0:T(8,128)(2,1)S(1)} %constant_dynamic-update-slice_fusion, f32[160]{0:T(256)S(1)} %get-tuple-element.74, bf16[40,5760]{1,0:T(8,128)(2,1)S(1)} %collective-permute-done.9, bf16[40,5760]{1,0:T(8,128)(2,1)S(1)} %collective-permute-done.8, ...), kind=kOutput, calls=%fused_computation.63 | convolution fusion | flops 1187635200 | bytes 9421440 | tf_op jit(solution)/shard_map/dot_general | solution.py:108
  117.7 1.8 %copy.31 = bf16[640,160]{1,0:T(8,128)(2,1)} copy(bf16[640,160]{0,1:T(8,128)(2,1)} %multiply_convert_fusion.1) | data formatting | bytes 409600 | tf_op jit(solution)/shard_map/convert.8
  119.6 1.2 slice_bitcast_fusion.4
  120.8 4.2 %concatenate.93 = bf16[160,5760]{1,0:T(8,128)(2,1)} concatenate(bf16[160,1440]{1,0:T(8,128)(2,1)} %get-tuple-element.26, bf16[160,1440]{1,0:T(8,128)(2,1)} %get-tuple-element.25, bf16[160,1440]{1,0:T(8,128)(2,1)} %get-tuple-element.24, bf16[160,1440]{1,0:T(8,128)(2,1)S(1)} %get-tuple-element.23), dimensions={1} | concatenate | bytes 3686400 | tf_op jit(solution)/shard_map/concatenate | solution.py:70
  124.9 2.1 %collective-permute-start.11 = (bf16[4,160,1440]{2,1,0:T(8,128)(2,1)S(1)}, bf16[4,160,1440]{2,1,0:T(8,128)(2,1)}, u32[]{:S(2)}, u32[]{:S(2)}) collective-permute-start(bf16[4,160,1440]{2,1,0:T(8,128)(2,1)S(1)} %all-to-all-done.2), channel_id=1, source_target_pairs={{0,32},{32,0},{64,96},{96,64},{128,160},{160,128},{192,224},{224,1... | collective-permute-start | bytes 5529608 | tf_op jit(solution)/shard_map/ppermute | solution.py:143
  127.0 8.1 %divide_multiply_fusion = bf16[640,320]{0,1:T(8,128)(2,1)} fusion(bf16[640,5760]{1,0:T(8,128)(2,1)} %copy-done.9, bf16[160,5760]{1,0:T(8,128)(2,1)} %collective-permute-done.10, bf16[160,5760]{1,0:T(8,128)(2,1)} %concatenate.93, f32[320]{0:T(512)S(1)} %slice.226), kind=kOutput, calls=%fused_computation.42 | convolution fusion | flops 2367897600 | bytes 11470080 | tf_op jit(solution)/shard_map/dot_general | solution.py:108
  135.2 1.0 constant_dynamic-update-slice_fusion.9
  137.1 1.6 copy-done.10
  138.7 3.4 %multiply_convert_fusion.2 = bf16[256,320]{0,1:T(8,128)(2,1)} fusion(bf16[256,5760]{1,0:T(8,128)(2,1)S(1)} %constant_dynamic-update-slice_fusion.11, bf16[160,5760]{1,0:T(8,128)(2,1)} %collective-permute-done.10, bf16[160,5760]{1,0:T(8,128)(2,1)S(1)} %copy-done.3, f32[320]{0:T(512)S(1)} %slice.226), kind=kOutput, calls=%fused_computation.65 | convolution fusion | flops 951582720 | bytes 6800640 | tf_op jit(solution)/shard_map/dot_general | solution.py:108
  142.1 1.1 copy.29
  143.2 3.3 %multiply_convert_fusion.4 = bf16[256,160]{0,1:T(8,128)(2,1)S(1)} fusion(bf16[256,5760]{1,0:T(8,128)(2,1)} %copy-done.10, f32[160]{0:T(256)S(1)} %copy-done.18, bf16[40,5760]{1,0:T(8,128)(2,1)} %copy-done.7, bf16[40,5760]{1,0:T(8,128)(2,1)} %copy-done.8, bf16[40,5760]{1,0:T(8,128)(2,1)} %copy-done.6, bf16[40,5760]{1,0:T(8,128)(2,1)S(1)} %copy-done.2), kind=kOutput, calls=%fused_computation.73 | convolution fusion | flops 479477760 | bytes 4874880 | tf_op jit(solution)/shard_map/dot_general | solution.py:108
  147.3 1.3 copy.32
  148.6 1.6 slice_bitcast_fusion
  150.2 2.6 %concatenate.100 = bf16[160,5760]{1,0:T(8,128)(2,1)} concatenate(bf16[160,1440]{1,0:T(8,128)(2,1)S(1)} %get-tuple-element.22, bf16[160,1440]{1,0:T(8,128)(2,1)S(1)} %get-tuple-element.21, bf16[160,1440]{1,0:T(8,128)(2,1)S(1)} %get-tuple-element.20, bf16[160,1440]{1,0:T(8,128)(2,1)S(1)} %get-tuple-element.19), dimensions={1} | concatenate | bytes 3686400 | tf_op jit(solution)/shard_map/concatenate | solution.py:70
  152.7 3.7 %multiply_convert_fusion.3 = bf16[256,160]{0,1:T(8,128)(2,1)S(1)} fusion(bf16[256,5760]{1,0:T(8,128)(2,1)} %copy-done.10, bf16[160,5760]{1,0:T(8,128)(2,1)} %concatenate.100, f32[160]{0:T(256)S(1)} %copy-done.16), kind=kOutput, calls=%fused_computation.72 | convolution fusion | flops 472104960 | bytes 4874880 | tf_op jit(solution)/shard_map/dot_general | solution.py:108
  156.4 5.5 %multiply_convert_fusion = bf16[640,160]{0,1:T(8,128)(2,1)S(1)} fusion(bf16[640,5760]{1,0:T(8,128)(2,1)} %copy-done.9, bf16[160,5760]{1,0:T(8,128)(2,1)S(1)} %copy-done.4, f32[160]{0:T(256)S(1)} %copy-done.16), kind=kOutput, calls=%fused_computation.62 | convolution fusion | flops 1180262400 | bytes 9421440 | tf_op jit(solution)/shard_map/dot_general | solution.py:108
  162.1 0.9 copy.33
  163.2 1.7 pad_maximum_fusion.9
  165.0 4.0 %concatenate.111 = bf16[640,1920]{1,0:T(8,128)(2,1)} concatenate(bf16[640,640]{1,0:T(8,128)(2,1)S(1)} %bitcast.120, bf16[640,160]{1,0:T(8,128)(2,1)S(1)} %copy-done, bf16[640,320]{1,0:T(8,128)(2,1)S(1)} %copy.32, bf16[640,160]{1,0:T(8,128)(2,1)} %copy.33, bf16[640,640]{1,0:T(8,128)(2,1)S(1)} %bitcast.119), dimensions={1} | concatenate | bytes 4915200 | tf_op jit(solution)/shard_map/concatenate | solution.py:163
  169.0 4.5 %fusion.11 = f32[640,640]{1,0:T(8,128)S(1)} fusion(bf16[640,1920]{1,0:T(8,128)(2,1)} %concatenate.111, bf16[640,640]{1,0:T(8,128)(2,1)} %fusion.8, bf16[640,640]{1,0:T(8,128)(2,1)} %fusion.9, bf16[640,640]{1,0:T(8,128)(2,1)} %fusion.10, f32[640]{0:T(1024)S(1)} %copy-done.20), kind=kOutput, calls=%fused_computation.16 | convolution fusion | flops 1580646400 | bytes 6556160 | tf_op jit(solution)/shard_map/dot_general | solution.py:164
  174.0 1.3 copy.37
  (92 shorter events, 7.7 us)
Async XLA Ops:
  0.0 33.6 %copy-start.12 = (s32[640]{0:T(1024)S(1)}, s32[640]{0:T(1024)}, u32[]{:S(2)}) copy-start(s32[640]{0:T(1024)} %constant.78.clone) | copy-start | bytes 7684
  0.0 33.6 %copy-start.13 = (s32[640]{0:T(1024)S(1)}, s32[640]{0:T(1024)}, u32[]{:S(2)}) copy-start(s32[640]{0:T(1024)} %constant.85) | copy-start | bytes 7684
  0.0 33.6 %copy-start.14 = (s32[640]{0:T(1024)S(1)}, s32[640]{0:T(1024)}, u32[]{:S(2)}) copy-start(s32[640]{0:T(1024)} %constant.75.clone) | copy-start | bytes 7684
  0.0 33.6 %copy-start.15 = (s32[640]{0:T(1024)S(1)}, s32[640]{0:T(1024)}, u32[]{:S(2)}) copy-start(s32[640]{0:T(1024)} %constant.77.clone) | copy-start | bytes 7684
  0.0 33.6 %copy-start.11 = (f32[640]{0:T(1024)S(1)}, f32[640]{0:T(1024)}, u32[]{:S(2)}) copy-start(f32[640]{0:T(1024)} %param.11) | copy-start | bytes 7684
  1.6 32.4 %all-to-all-start = ((bf16[16,40,180]{2,1,0:T(8,128)(2,1)}), bf16[16,40,180]{2,1,0:T(8,128)(2,1)S(1)}, u32[]{:S(2)}, u32[]{:S(2)}) async-start(bf16[16,40,180]{2,1,0:T(8,128)(2,1)} %broadcast_in_dim.26), calls=%async_computation | async-start | bytes 655360 | tf_op jit(solution)/shard_map/all_to_all | solution.py:54
  18.5 60.5 %collective-permute-start = (bf16[5,32,640]{2,1,0:T(8,128)(2,1)}, bf16[5,32,640]{2,1,0:T(8,128)(2,1)}, u32[]{:S(2)}, u32[]{:S(2)}) collective-permute-start(bf16[5,32,640]{2,1,0:T(8,128)(2,1)} %get-tuple-element.40), channel_id=1, source_target_pairs={{0,480},{32,64},{64,32},{96,128},{128,96},{160,192},{192,160},{224... | collective-permute-start | bytes 614408 | tf_op jit(solution)/shard_map/ppermute | solution.py:84
  31.6 47.4 %collective-permute-start.1 = (bf16[5,32,640]{2,1,0:T(8,128)(2,1)}, bf16[5,32,640]{2,1,0:T(8,128)(2,1)}, u32[]{:S(2)}, u32[]{:S(2)}) collective-permute-start(bf16[5,32,640]{2,1,0:T(8,128)(2,1)} %get-tuple-element.39), channel_id=1, source_target_pairs={{0,32},{32,0},{64,96},{96,64},{128,160},{160,128},{192,224},{224,1... | collective-permute-start | bytes 614408 | tf_op jit(solution)/shard_map/ppermute | solution.py:85
  34.2 15.8 %collective-permute-start.7 = (bf16[40,1440]{1,0:T(8,128)(2,1)S(1)}, bf16[40,1440]{1,0:T(8,128)(2,1)S(1)}, u32[]{:S(2)}, u32[]{:S(2)}) collective-permute-start(bf16[40,1440]{1,0:T(8,128)(2,1)S(1)} %concatenate.91), channel_id=1, source_target_pairs={{384,0},{416,32},{448,64},{480,96},{0,128},{32,160},{64,192},{96,2... | collective-permute-start | bytes 345608 | tf_op jit(solution)/shard_map/ppermute | solution.py:66
  37.4 12.6 %collective-permute-start.6 = (bf16[40,1440]{1,0:T(8,128)(2,1)S(1)}, bf16[40,1440]{1,0:T(8,128)(2,1)S(1)}, u32[]{:S(2)}, u32[]{:S(2)}) collective-permute-start(bf16[40,1440]{1,0:T(8,128)(2,1)S(1)} %concatenate.91), channel_id=1, source_target_pairs={{256,0},{288,32},{320,64},{352,96},{384,128},{416,160},{448,192},{... | collective-permute-start | bytes 345608 | tf_op jit(solution)/shard_map/ppermute | solution.py:66
  41.7 8.3 %collective-permute-start.5 = (bf16[40,1440]{1,0:T(8,128)(2,1)S(1)}, bf16[40,1440]{1,0:T(8,128)(2,1)S(1)}, u32[]{:S(2)}, u32[]{:S(2)}) collective-permute-start(bf16[40,1440]{1,0:T(8,128)(2,1)S(1)} %concatenate.91), channel_id=1, source_target_pairs={{128,0},{160,32},{192,64},{224,96},{256,128},{288,160},{320,192},{... | collective-permute-start | bytes 345608 | tf_op jit(solution)/shard_map/ppermute | solution.py:66
  45.0 10.2 %all-to-all-start.1 = ((bf16[4,40,1440]{2,1,0:T(8,128)(2,1)}), bf16[4,40,1440]{2,1,0:T(8,128)(2,1)S(1)}, u32[]{:S(2)}, u32[]{:S(2)}) async-start(bf16[4,40,1440]{2,1,0:T(8,128)(2,1)} %broadcast_in_dim.27), calls=%async_computation.1 | async-start | bytes 983040 | tf_op jit(solution)/shard_map/all_to_all | solution.py:62
  49.9 61.8 %copy-start.17 = (f32[160]{0:T(256)}, f32[160]{0:T(256)S(1)}, u32[]{:S(2)}) copy-start(f32[160]{0:T(256)S(1)} %get-tuple-element.74) | copy-start | bytes 1924
  56.7 62.8 %all-to-all-start.2 = ((bf16[4,160,1440]{2,1,0:T(8,128)(2,1)}), bf16[4,160,1440]{2,1,0:T(8,128)(2,1)S(1)}, u32[]{:S(2)}, u32[]{:S(2)}) async-start(bf16[4,160,1440]{2,1,0:T(8,128)(2,1)} %broadcast_in_dim.32), calls=%async_computation.2 | async-start | bytes 3932160 | tf_op jit(solution)/shard_map/all_to_all | solution.py:62
  63.5 48.2 %copy-start.1 = (bf16[40,5760]{1,0:T(8,128)(2,1)}, bf16[40,5760]{1,0:T(8,128)(2,1)S(1)}, u32[]{:S(2)}) copy-start(bf16[40,5760]{1,0:T(8,128)(2,1)S(1)} %concatenate.86) | copy-start | bytes 1382404
  63.5 11.9 %copy-start.19 = (bf16[1920,640]{1,0:T(8,128)(2,1)S(1)}, bf16[1920,640]{1,0:T(8,128)(2,1)}, u32[]{:S(2)}) copy-start(bf16[1920,640]{1,0:T(8,128)(2,1)} %param.12) | copy-start | bytes 7372804
  63.5 15.6 %collective-permute-start.2 = (bf16[40,5760]{1,0:T(8,128)(2,1)S(1)}, bf16[40,5760]{1,0:T(8,128)(2,1)S(1)}, u32[]{:S(2)}, u32[]{:S(2)}) collective-permute-start(bf16[40,5760]{1,0:T(8,128)(2,1)S(1)} %concatenate.86), channel_id=1, source_target_pairs={{128,0},{160,32},{192,64},{224,96},{256,128},{288,160},{320,192},{... | collective-permute-start | bytes 1382408 | tf_op jit(solution)/shard_map/ppermute | solution.py:66
  66.7 28.6 %collective-permute-start.9 = (bf16[40,5760]{1,0:T(8,128)(2,1)S(1)}, bf16[40,5760]{1,0:T(8,128)(2,1)S(1)}, u32[]{:S(2)}, u32[]{:S(2)}) collective-permute-start(bf16[40,5760]{1,0:T(8,128)(2,1)S(1)} %concatenate.86), channel_id=1, source_target_pairs={{384,0},{416,32},{448,64},{480,96},{0,128},{32,160},{64,192},{96,2... | collective-permute-start | bytes 1382408 | tf_op jit(solution)/shard_map/ppermute | solution.py:66
  69.1 26.3 %collective-permute-start.8 = (bf16[40,5760]{1,0:T(8,128)(2,1)S(1)}, bf16[40,5760]{1,0:T(8,128)(2,1)S(1)}, u32[]{:S(2)}, u32[]{:S(2)}) collective-permute-start(bf16[40,5760]{1,0:T(8,128)(2,1)S(1)} %concatenate.86), channel_id=1, source_target_pairs={{256,0},{288,32},{320,64},{352,96},{384,128},{416,160},{448,192},{... | collective-permute-start | bytes 1382408 | tf_op jit(solution)/shard_map/ppermute | solution.py:66
  79.1 32.7 %copy-start.6 = (bf16[40,5760]{1,0:T(8,128)(2,1)}, bf16[40,5760]{1,0:T(8,128)(2,1)S(1)}, u32[]{:S(2)}) copy-start(bf16[40,5760]{1,0:T(8,128)(2,1)S(1)} %collective-permute-done.2) | copy-start | bytes 1382404
  81.3 53.8 %collective-permute-start.3 = (bf16[6,1,32,640]{3,2,1,0:T(8,128)(2,1)}, bf16[6,1,32,640]{3,2,1,0:T(8,128)(2,1)S(1)}, u32[]{:S(2)}, u32[]{:S(2)}) collective-permute-start(bf16[6,1,32,640]{3,2,1,0:T(8,128)(2,1)} %get-tuple-element.34), channel_id=1, source_target_pairs={{0,1},{1,2},{2,3},{3,4},{4,5},{5,6},{6,7},{7,8},{8,9},{9,10},{10,1... | collective-permute-start | bytes 737288 | tf_op jit(solution)/shard_map/ppermute | solution.py:92
  86.4 48.8 %collective-permute-start.4 = (bf16[6,1,32,640]{3,2,1,0:T(8,128)(2,1)}, bf16[6,1,32,640]{3,2,1,0:T(8,128)(2,1)}, u32[]{:S(2)}, u32[]{:S(2)}) collective-permute-start(bf16[6,1,32,640]{3,2,1,0:T(8,128)(2,1)} %get-tuple-element.33), channel_id=1, source_target_pairs={{1,0},{2,1},{3,2},{4,3},{5,4},{6,5},{7,6},{8,7},{9,8},{10,9},{11,1... | collective-permute-start | bytes 737288 | tf_op jit(solution)/shard_map/ppermute | solution.py:93
  95.4 16.4 %copy-start.7 = (bf16[40,5760]{1,0:T(8,128)(2,1)}, bf16[40,5760]{1,0:T(8,128)(2,1)S(1)}, u32[]{:S(2)}) copy-start(bf16[40,5760]{1,0:T(8,128)(2,1)S(1)} %collective-permute-done.9) | copy-start | bytes 1382404
  95.4 16.4 %copy-start.8 = (bf16[40,5760]{1,0:T(8,128)(2,1)}, bf16[40,5760]{1,0:T(8,128)(2,1)S(1)}, u32[]{:S(2)}) copy-start(bf16[40,5760]{1,0:T(8,128)(2,1)S(1)} %collective-permute-done.8) | copy-start | bytes 1382404
  96.9 30.1 %collective-permute-start.10 = (bf16[160,5760]{1,0:T(8,128)(2,1)}, bf16[160,5760]{1,0:T(8,128)(2,1)}, u32[]{:S(2)}, u32[]{:S(2)}) collective-permute-start(bf16[160,5760]{1,0:T(8,128)(2,1)} %pad_maximum_fusion.3), channel_id=1, source_target_pairs={{0,32},{32,0},{64,96},{96,64},{128,160},{160,128},{192,224},{224,1... | collective-permute-start | bytes 5529608 | tf_op jit(solution)/shard_map/ppermute | solution.py:142
  111.7 3.0 %copy-start.9 = (bf16[640,5760]{1,0:T(8,128)(2,1)}, bf16[640,5760]{1,0:T(8,128)(2,1)S(1)}, u32[]{:S(2)}) copy-start(bf16[640,5760]{1,0:T(8,128)(2,1)S(1)} %constant_dynamic-update-slice_fusion) | copy-start | bytes 22118404
  124.9 23.6 %collective-permute-start.11 = (bf16[4,160,1440]{2,1,0:T(8,128)(2,1)S(1)}, bf16[4,160,1440]{2,1,0:T(8,128)(2,1)}, u32[]{:S(2)}, u32[]{:S(2)}) collective-permute-start(bf16[4,160,1440]{2,1,0:T(8,128)(2,1)S(1)} %all-to-all-done.2), channel_id=1, source_target_pairs={{0,32},{32,0},{64,96},{96,64},{128,160},{160,128},{192,224},{224,1... | collective-permute-start | bytes 5529608 | tf_op jit(solution)/shard_map/ppermute | solution.py:143
  136.6 2.1 %copy-start.3 = (bf16[160,5760]{1,0:T(8,128)(2,1)S(1)}, bf16[160,5760]{1,0:T(8,128)(2,1)}, u32[]{:S(2)}) copy-start(bf16[160,5760]{1,0:T(8,128)(2,1)} %concatenate.93) | copy-start | bytes 5529604
  137.0 1.6 copy-start.10
  138.7 4.5 %copy-start.2 = (bf16[40,5760]{1,0:T(8,128)(2,1)S(1)}, bf16[40,5760]{1,0:T(8,128)(2,1)}, u32[]{:S(2)}) copy-start(bf16[40,5760]{1,0:T(8,128)(2,1)} %copy-done.1) | copy-start | bytes 1382404
  138.7 4.5 %copy-start.18 = (f32[160]{0:T(256)S(1)}, f32[160]{0:T(256)}, u32[]{:S(2)}) copy-start(f32[160]{0:T(256)} %copy-done.17) | copy-start | bytes 1924
  148.5 4.2 %copy-start.16 = (f32[160]{0:T(256)S(1)}, f32[160]{0:T(256)}, u32[]{:S(2)}) copy-start(f32[160]{0:T(256)} %get-tuple-element.75) | copy-start | bytes 1924
  152.7 3.7 %copy-start.4 = (bf16[160,5760]{1,0:T(8,128)(2,1)S(1)}, bf16[160,5760]{1,0:T(8,128)(2,1)}, u32[]{:S(2)}) copy-start(bf16[160,5760]{1,0:T(8,128)(2,1)} %concatenate.100) | copy-start | bytes 5529604
  156.4 6.6 %copy-start.5 = (bf16[256,160]{1,0:T(8,128)(2,1)S(1)}, bf16[256,160]{1,0:T(8,128)(2,1)}, u32[]{:S(2)}) copy-start(bf16[256,160]{1,0:T(8,128)(2,1)} %copy.28) | copy-start | bytes 245764
  156.4 6.8 %copy-start = (bf16[640,160]{1,0:T(8,128)(2,1)S(1)}, bf16[640,160]{1,0:T(8,128)(2,1)}, u32[]{:S(2)}) copy-start(bf16[640,160]{1,0:T(8,128)(2,1)} %copy.31) | copy-start | bytes 614404
  165.0 4.0 %copy-start.20 = (f32[640]{0:T(1024)S(1)}, f32[640]{0:T(1024)}, u32[]{:S(2)}) copy-start(f32[640]{0:T(1024)} %param.13) | copy-start | bytes 7684

commit v4 on v3

--- a/solution.py
+++ b/solution.py
@@ -2,6 +2,8 @@
 import jax.numpy as jnp
 import numpy as np
 from jax import lax
+from jax.experimental import pallas as pl
+from jax.experimental.pallas import tpu as pltpu
 from jax.sharding import PartitionSpec as P
 
 LONS = 16
@@ -36,8 +38,8 @@
     return [[frame_index(x, z_lo) for x in range(X)] for z_lo in range(Z_LO)]
 
 
-def from_y(k):
-    return [(((y + k) % Y) * 4 + r, y * 4 + r) for y in range(Y) for r in range(4)]
+def across_y(k):
+    return [((y ^ k) * 4 + r, y * 4 + r) for y in range(Y) for r in range(4)]
 
 
 CORES = [(i, i ^ 1) for i in range(LONS)]
@@ -62,21 +64,39 @@
     return lax.all_to_all(copies(block, X), "frame", 0, 0, axis_index_groups=x_groups())
 
 
+def doubled_over_y(block):
+    block = jnp.concatenate([block, lax.ppermute(block, "lon", across_y(1))])
+    return jnp.concatenate([block, lax.ppermute(block, "lon", across_y(3))])
+
+
 def over_y(block):
-    return [block] + [lax.ppermute(block, "lon", from_y(k)) for k in (1, 2, 3)]
+    return [block] + [lax.ppermute(block, "lon", across_y(k)) for k in (1, 3, 2)]
+
+
+def join_kernel(parts_ref, joined_ref):
+    parts, _, width = parts_ref.shape
+    for x in range(parts):
+        joined_ref[:, x * width : (x + 1) * width] = parts_ref[x]
 
 
 def joined_rows(along_x):
-    return jnp.concatenate([along_x[x] for x in range(X)], axis=1)
+    parts, count, width = along_x.shape
+    return pl.pallas_call(
+        join_kernel,
+        out_shape=jax.ShapeDtypeStruct((count, parts * width), along_x.dtype),
+        in_specs=[pl.BlockSpec(memory_space=pltpu.VMEM)],
+        out_specs=pl.BlockSpec(memory_space=pltpu.VMEM),
+        compiler_params=pltpu.CompilerParams(vmem_limit_bytes=12 * 1024 * 1024),
+        cost_estimate=pl.CostEstimate(flops=0, bytes_accessed=2 * 2 * along_x.size, transcendentals=0),
+    )(along_x)
 
 
 def channel_order():
     lon = lax.axis_index("lon")
-    blocks = [(y, z_hi, side) for side in range(2) for z_hi in range(2) for y in range(Y)]
+    blocks = [(k, z_hi, side) for z_hi, side in ((0, 0), (0, 1), (1, 0), (1, 1)) for k in (0, 1, 3, 2)]
     row, z_hi, side = (jnp.asarray(np.repeat(np.array(v), 40)) for v in zip(*blocks))
     within = jnp.asarray(np.tile(np.arange(40), LONS))
-    row = lax.rem(lon // 4 + row, Y)
-    return lon_index(row, z_hi, (lon % 2) ^ side) * 40 + within
+    return lon_index((lon // 4) ^ row, z_hi, (lon % 2) ^ side) * 40 + within
 
 
 def lon_halos(columns):
@@ -117,13 +137,24 @@
     columns = latents.transpose(2, 0, 1, 3)
     far, near = lon_halos(columns)
     low, high = gather_z(spatial_kernel)
-    high = jnp.concatenate(over_y(high))
+    _, temporal_kernel = lax.optimization_barrier((low, temporal_kernel))
+    high = doubled_over_y(high)
     low = joined_rows(over_x(low))
-    _, _, temporal_kernel = lax.optimization_barrier((low, high, temporal_kernel))
     low = over_y(low)
     high = over_x(high)
     far, near, columns, _ = lax.optimization_barrier((far, near, columns, low[1]))
+    other_high = joined_rows(lax.ppermute(high, "lon", CORES))
+
+    before = jnp.where(core == 1, near, far)
+    after = jnp.where(core == 1, far, near)
+    wide = jnp.concatenate([before[None], columns, after[None]], axis=0)
+    earlier, later = frame_halos(wide)
+    inner_taps = tap_rows(wide, lon_cols, lat_rows)
+    earlier, later, *low = lax.optimization_barrier((earlier, later, *low))
     low = jnp.concatenate(low)
+    other_low = lax.ppermute(low, "lon", CORES)
+    halo_taps = tap_rows(jnp.concatenate([earlier, later], axis=1), lon_cols, lat_rows)
+    taps = jnp.concatenate([inner_taps, halo_taps], axis=0)
 
     order = channel_order()[:, None] == lax.broadcasted_iota(jnp.int32, (channels, channels), 1)
     ordered = [
@@ -133,31 +164,16 @@
     ordered = jnp.concatenate(ordered, axis=0)
     bias = jnp.sum(jnp.where(order, spatial_bias[None, :], 0.0), axis=1)
 
-    before = jnp.where(core == 1, near, far)
-    after = jnp.where(core == 1, far, near)
-    wide = jnp.concatenate([before[None], columns, after[None]], axis=0)
-    inner_rows = tap_rows(wide, lon_cols, lat_rows)
-    earlier, later = frame_halos(wide)
-
-    other_low = lax.ppermute(low, "lon", CORES)
-    other_high = joined_rows(lax.ppermute(high, "lon", CORES))
-    middle = jnp.concatenate([joined_rows(high), other_low])
-    groups = (low, middle, other_high)
-    ends = np.cumsum([rows.shape[0] for rows in groups])
-    biases = [bias[end - rows.shape[0] : end] for rows, end in zip(groups, ends)]
-    inner = [active(inner_rows, rows, part) for rows, part in zip(groups[:2], biases)]
-    earlier, later, inner[1] = lax.optimization_barrier((earlier, later, inner[1]))
-    outer_rows = tap_rows(jnp.concatenate([earlier, later], axis=1), lon_cols, lat_rows)
-    outer = [active(outer_rows, rows, part) for rows, part in zip(groups, biases)]
-    inner.append(active(inner_rows, groups[2], biases[2]))
-
-    inner = jnp.concatenate(inner, axis=-1).astype(jnp.bfloat16)
-    inner = inner.reshape(lon_cols, frames, lat_rows, channels)
-    outer = jnp.concatenate(outer, axis=-1).astype(jnp.bfloat16)
-    outer = outer.reshape(lon_cols, 2, lat_rows, channels)
+    early = jnp.concatenate([low, other_low, joined_rows(high)])
+    split = early.shape[0]
+    hidden = [active(taps, early, bias[:split]), active(taps, other_high, bias[split:])]
+    hidden = jnp.concatenate(hidden, axis=-1).astype(jnp.bfloat16)
+    inner_size = lon_cols * frames * lat_rows
+    inner = hidden[:inner_size].reshape(lon_cols, frames, lat_rows, channels)
+    halo = hidden[inner_size:].reshape(lon_cols, 2, lat_rows, channels)
     frame = lax.axis_index("frame")
-    first = jnp.where(frame == 0, 0, outer[:, :1])
-    final = jnp.where(frame == FRAMES_AXIS - 1, 0, outer[:, 1:])
+    first = jnp.where(frame == 0, 0, halo[:, :1])
+    final = jnp.where(frame == FRAMES_AXIS - 1, 0, halo[:, 1:])
     hidden = jnp.concatenate([first, inner, final], axis=1)
 
     stacked = jnp.concatenate([hidden[:, k : k + frames] for k in range(3)], axis=-1)

time: 177 us -> 147 us (0.83)
  the two profiles are of different devices: /device:TPU:11 before, /device:TPU:481 now
where the time goes in v4:
time: 147 us; the launch traced here: 146 us
  starting transfers between devices  64.8 us (44%)
  matrix products  25 us (17%)
  waiting for transfers between devices  24.7 us (17%)
  local copies, waits for them, and re-layouts  24.1 us (16%)
  other arithmetic  5.92 us (4%)
    ppermute x1, waiting for transfers between devices, frame_halos(): later = lax.ppermute(wide[:, :1], 'frame', down)  21.4 us
    unnamed x49, local copies, waits for them, and re-layouts  12.2 us
    dot_general x2, matrix products, active(): lax.dot_general(rows, kernel_rows, (((1,), (1,)), ((), ())), preferred_el...  12 us
    ppermute x1, starting transfers between devices, lon_halos(): lax.ppermute(jnp.where(core == 1, columns[-1], columns[0]), 'lon', FAR)  11.8 us
    ppermute x3, starting transfers between devices, over_y(): lax.ppermute(block, 'lon', across_y(k))  8.97 us
    dot_general x3, matrix products, body(): jnp.dot(order.astype(jnp.bfloat16), temporal_kernel[k * channels:(k + 1)...  8.95 us
    all_to_all x1, starting transfers between devices, gather_z(): lax.all_to_all(copies(shard, 16), ('lon', 'frame'), 0, 0, axis_index_grou...  8.29 us
    all_to_all x2, starting transfers between devices, over_x(): lax.all_to_all(copies(block, X), 'frame', 0, 0, axis_index_groups=x_group...  8.25 us
  transfers between devices with their start and end apart: 14, of which 2 were waited for; matrix products, arithmetic and copies ran while one was open for 28% of the time, Pallas kernels for 0%

profile of v4, /device:TPU:481, one launch (start us, length us, event | category | flops | bytes accessed | tf_op | source)
XLA Modules:
  0.0 146.2 jit_solution(17013975965537477847)
XLA Ops:
  0.0 1.5 %broadcast_in_dim.26 = bf16[16,40,180]{2,1,0:T(8,128)(2,1)} broadcast(bf16[40,180]{1,0:T(8,128)(2,1)} %bitcast.100), dimensions={1,2} | broadcast | bytes 244800 | tf_op jit(solution)/shard_map/broadcast_in_dim | solution.py:50
  1.6 8.3 %all-to-all-start = ((bf16[16,40,180]{2,1,0:T(8,128)(2,1)}), bf16[16,40,180]{2,1,0:T(8,128)(2,1)S(1)}, u32[]{:S(2)}, u32[]{:S(2)}) async-start(bf16[16,40,180]{2,1,0:T(8,128)(2,1)} %broadcast_in_dim.26), calls=%async_computation | async-start | bytes 655360 | tf_op jit(solution)/shard_map/all_to_all | solution.py:56
  9.8 1.2 copy.29
  11.1 0.8 select_bitcast_fusion.2
  11.9 11.8 %collective-permute-start = (bf16[5,32,640]{2,1,0:T(8,128)(2,1)}, bf16[5,32,640]{2,1,0:T(8,128)(2,1)S(1)}, u32[]{:S(2)}, u32[]{:S(2)}) collective-permute-start(bf16[5,32,640]{2,1,0:T(8,128)(2,1)} %get-tuple-element.38), channel_id=1, source_target_pairs={{0,480},{32,64},{64,32},{96,128},{128,96},{160,192},{192,160},{224... | collective-permute-start | bytes 614408 | tf_op jit(solution)/shard_map/ppermute | solution.py:104
  23.7 1.9 %collective-permute-start.1 = (bf16[5,32,640]{2,1,0:T(8,128)(2,1)}, bf16[5,32,640]{2,1,0:T(8,128)(2,1)}, u32[]{:S(2)}, u32[]{:S(2)}) collective-permute-start(bf16[5,32,640]{2,1,0:T(8,128)(2,1)} %get-tuple-element.37), channel_id=1, source_target_pairs={{0,32},{32,0},{64,96},{96,64},{128,160},{160,128},{192,224},{224,1... | collective-permute-start | bytes 614408 | tf_op jit(solution)/shard_map/ppermute | solution.py:105
  25.7 0.3 select_reduce_fusion
  26.1 3.2 %all-to-all-done = bf16[16,40,180]{2,1,0:T(8,128)(2,1)S(1)} async-done(((bf16[16,40,180]{2,1,0:T(8,128)(2,1)}), bf16[16,40,180]{2,1,0:T(8,128)(2,1)S(1)}, u32[]{:S(2)}, u32[]{:S(2)}) %all-to-all-start) | async-done | bytes 230432 | tf_op jit(solution)/shard_map/all_to_all | solution.py:56
  29.5 0.8 broadcast_in_dim.28
  30.3 4.0 %all-to-all-start.1 = ((bf16[4,40,1440]{2,1,0:T(8,128)(2,1)}), bf16[4,40,1440]{2,1,0:T(8,128)(2,1)S(1)}, u32[]{:S(2)}, u32[]{:S(2)}) async-start(bf16[4,40,1440]{2,1,0:T(8,128)(2,1)} %broadcast_in_dim.28), calls=%async_computation.1 | async-start | bytes 983040 | tf_op jit(solution)/shard_map/all_to_all | solution.py:64
  34.5 3.2 %collective-permute-start.8 = (bf16[40,1440]{1,0:T(8,128)(2,1)S(1)}, bf16[40,1440]{1,0:T(8,128)(2,1)S(1)}, u32[]{:S(2)}, u32[]{:S(2)}) collective-permute-start(bf16[40,1440]{1,0:T(8,128)(2,1)S(1)} %concatenate.72), channel_id=1, source_target_pairs={{128,0},{160,32},{192,64},{224,96},{0,128},{32,160},{64,192},{96,2... | collective-permute-start | bytes 345608 | tf_op jit(solution)/shard_map/ppermute | solution.py:68
  37.7 3.0 %fusion.14 = bf16[640,640]{1,0:T(8,128)(2,1)} fusion(bf16[1920,640]{1,0:T(8,128)(2,1)} %param.12, s32[640]{0:T(1024)S(1)} %multiply_add_fusion), kind=kOutput, calls=%fused_computation.20 | convolution fusion | flops 524697600 | bytes 1640960 | tf_op jit(solution)/shard_map/dot_general | solution.py:161
  40.7 3.0 %fusion.15 = bf16[640,640]{1,0:T(8,128)(2,1)} fusion(bf16[1920,640]{1,0:T(8,128)(2,1)} %param.12, s32[640]{0:T(1024)S(1)} %multiply_add_fusion), kind=kOutput, calls=%fused_computation.21 | convolution fusion | flops 524697600 | bytes 1640960 | tf_op jit(solution)/shard_map/dot_general | solution.py:161
  43.7 3.8 %collective-permute-start.9 = (bf16[80,1440]{1,0:T(8,128)(2,1)S(1)}, bf16[80,1440]{1,0:T(8,128)(2,1)S(1)}, u32[]{:S(2)}, u32[]{:S(2)}) collective-permute-start(bf16[80,1440]{1,0:T(8,128)(2,1)S(1)} %pad_maximum_fusion.18), channel_id=1, source_target_pairs={{384,0},{416,32},{448,64},{480,96},{256,128},{288,160},{320,192},{... | collective-permute-start | bytes 691208 | tf_op jit(solution)/shard_map/ppermute | solution.py:69
  47.7 2.3 %collective-permute-start.2 = (bf16[40,5760]{1,0:T(8,128)(2,1)S(1)}, bf16[40,5760]{1,0:T(8,128)(2,1)}, u32[]{:S(2)}, u32[]{:S(2)}) collective-permute-start(bf16[40,5760]{1,0:T(8,128)(2,1)S(1)} %shard_map.91), channel_id=1, source_target_pairs={{128,0},{160,32},{192,64},{224,96},{0,128},{32,160},{64,192},{96,2... | collective-permute-start | bytes 1382408 | tf_op jit(solution)/shard_map/ppermute | solution.py:73
  50.0 3.0 %fusion.13 = bf16[640,640]{1,0:T(8,128)(2,1)} fusion(bf16[1920,640]{1,0:T(8,128)(2,1)} %param.12, s32[640]{0:T(1024)S(1)} %multiply_add_fusion), kind=kOutput, calls=%fused_computation.19 | convolution fusion | flops 524697600 | bytes 1640960 | tf_op jit(solution)/shard_map/dot_general | solution.py:161
  53.0 2.5 %collective-permute-start.5 = (bf16[40,5760]{1,0:T(8,128)(2,1)S(1)}, bf16[40,5760]{1,0:T(8,128)(2,1)}, u32[]{:S(2)}, u32[]{:S(2)}) collective-permute-start(bf16[40,5760]{1,0:T(8,128)(2,1)S(1)} %shard_map.91), channel_id=1, source_target_pairs={{384,0},{416,32},{448,64},{480,96},{256,128},{288,160},{320,192},{... | collective-permute-start | bytes 1382408 | tf_op jit(solution)/shard_map/ppermute | solution.py:73
  55.5 4.1 %collective-permute-start.6 = (bf16[40,5760]{1,0:T(8,128)(2,1)S(1)}, bf16[40,5760]{1,0:T(8,128)(2,1)}, u32[]{:S(2)}, u32[]{:S(2)}) collective-permute-start(bf16[40,5760]{1,0:T(8,128)(2,1)S(1)} %shard_map.91), channel_id=1, source_target_pairs={{256,0},{288,32},{320,64},{352,96},{384,128},{416,160},{448,192},{... | collective-permute-start | bytes 1382408 | tf_op jit(solution)/shard_map/ppermute | solution.py:73
  59.7 1.4 broadcast_in_dim.51
  61.1 4.2 %all-to-all-start.2 = ((bf16[4,160,1440]{2,1,0:T(8,128)(2,1)}), bf16[4,160,1440]{2,1,0:T(8,128)(2,1)S(1)}, u32[]{:S(2)}, u32[]{:S(2)}) async-start(bf16[4,160,1440]{2,1,0:T(8,128)(2,1)} %broadcast_in_dim.51), calls=%async_computation.2 | async-start | bytes 3932160 | tf_op jit(solution)/shard_map/all_to_all | solution.py:64
  65.4 1.0 select_bitcast_fusion.1
  66.4 0.2 pad_maximum_fusion.8
  66.6 0.9 pad_slice_fusion
  67.6 0.2 pad_maximum_fusion.12
  67.7 7.9 %collective-permute-start.3 = (bf16[6,1,32,640]{3,2,1,0:T(8,128)(2,1)S(1)}, bf16[6,1,32,640]{3,2,1,0:T(8,128)(2,1)S(1)}, u32[]{:S(2)}, u32[]{:S(2)}) collective-permute-start(bf16[6,1,32,640]{3,2,1,0:T(8,128)(2,1)S(1)} %get-tuple-element.32), channel_id=1, source_target_pairs={{0,1},{1,2},{2,3},{3,4},{4,5},{5,6},{6,7},{7,8},{8,9},{9,10},{10,1... | collective-permute-start | bytes 737288 | tf_op jit(solution)/shard_map/ppermute | solution.py:112
  75.7 1.9 %collective-permute-start.4 = (bf16[6,1,32,640]{3,2,1,0:T(8,128)(2,1)S(1)}, bf16[6,1,32,640]{3,2,1,0:T(8,128)(2,1)S(1)}, u32[]{:S(2)}, u32[]{:S(2)}) collective-permute-start(bf16[6,1,32,640]{3,2,1,0:T(8,128)(2,1)S(1)} %get-tuple-element.31), channel_id=1, source_target_pairs={{1,0},{2,1},{3,2},{4,3},{5,4},{6,5},{7,6},{8,7},{9,8},{10,9},{11,1... | collective-permute-start | bytes 737288 | tf_op jit(solution)/shard_map/ppermute | solution.py:113
  78.8 21.4 %collective-permute-done.4 = bf16[6,1,32,640]{3,2,1,0:T(8,128)(2,1)S(1)} collective-permute-done((bf16[6,1,32,640]{3,2,1,0:T(8,128)(2,1)S(1)}, bf16[6,1,32,640]{3,2,1,0:T(8,128)(2,1)S(1)}, u32[]{:S(2)}, u32[]{:S(2)}) %collective-permute-start.4) | collective-permute-done | bytes 245792 | tf_op jit(solution)/shard_map/ppermute | solution.py:113
  100.2 0.9 constant_dynamic-update-slice_fusion.25
  101.1 1.9 %constant_dynamic-update-slice_fusion.24 = bf16[480,5760]{1,0:T(8,128)(2,1)} fusion(bf16[480,5760]{1,0:T(8,128)(2,1)} %constant_dynamic-update-slice_fusion.25, bf16[40,5760]{1,0:T(8,128)(2,1)} %collective-permute-done.2), kind=kLoop, calls=%fused_computation.84 | loop fusion | bytes 921600
  102.9 2.6 %pad_maximum_fusion.3 = bf16[160,5760]{1,0:T(8,128)(2,1)} fusion(bf16[40,5760]{1,0:T(8,128)(2,1)} %collective-permute-done.6, bf16[40,5760]{1,0:T(8,128)(2,1)} %collective-permute-done.5, bf16[40,5760]{1,0:T(8,128)(2,1)} %collective-permute-done.2, bf16[40,5760]{1,0:T(8,128)(2,1)S(1)} %shard_map.91), kind=kLoop, calls=%fused_computation.14 | loop fusion | flops 7372800 | bytes 3686400 | tf_op jit(solution)/shard_map/concatenate | solution.py:154
  105.6 6.2 %collective-permute-start.7 = (bf16[160,5760]{1,0:T(8,128)(2,1)}, bf16[160,5760]{1,0:T(8,128)(2,1)}, u32[]{:S(2)}, u32[]{:S(2)}) collective-permute-start(bf16[160,5760]{1,0:T(8,128)(2,1)} %pad_maximum_fusion.3), channel_id=1, source_target_pairs={{0,32},{32,0},{64,96},{96,64},{128,160},{160,128},{192,224},{224,1... | collective-permute-start | bytes 5529608 | tf_op jit(solution)/shard_map/ppermute | solution.py:155
  111.9 0.5 pad_slice_fusion.6
  112.8 2.2 %constant_dynamic-update-slice_fusion.23 = bf16[480,5760]{1,0:T(8,128)(2,1)} fusion(bf16[480,5760]{1,0:T(8,128)(2,1)} %constant_dynamic-update-slice_fusion.24, bf16[40,5760]{1,0:T(8,128)(2,1)} %collective-permute-done.5), kind=kLoop, calls=%fused_computation.83 | loop fusion | bytes 921600
  115.0 1.8 %constant_dynamic-update-slice_fusion.22 = bf16[480,5760]{1,0:T(8,128)(2,1)} fusion(bf16[480,5760]{1,0:T(8,128)(2,1)} %constant_dynamic-update-slice_fusion.23, bf16[40,5760]{1,0:T(8,128)(2,1)} %collective-permute-done.6), kind=kLoop, calls=%fused_computation.82 | loop fusion | bytes 921600
  116.8 0.4 shard_map.92
  117.3 2.5 %collective-permute-start.10 = (bf16[4,160,1440]{2,1,0:T(8,128)(2,1)S(1)}, bf16[4,160,1440]{2,1,0:T(8,128)(2,1)S(1)}, u32[]{:S(2)}, u32[]{:S(2)}) collective-permute-start(bf16[4,160,1440]{2,1,0:T(8,128)(2,1)S(1)} %all-to-all-done.2.parts_ref), channel_id=1, source_target_pairs={{0,32},{32,0},{64,96},{96,64},{128,160},{160,128},{192,224},{224,1... | collective-permute-start | bytes 5529608 | tf_op jit(solution)/shard_map/ppermute | solution.py:146
  119.8 2.9 %constant_dynamic-update-slice_fusion.21 = bf16[480,5760]{1,0:T(8,128)(2,1)} fusion(bf16[480,5760]{1,0:T(8,128)(2,1)} %constant_dynamic-update-slice_fusion.22, bf16[160,5760]{1,0:T(8,128)(2,1)} %collective-permute-done.7), kind=kLoop, calls=%fused_computation.81 | loop fusion | bytes 3686400
  122.7 1.5 constant_dynamic-update-slice_fusion.20
  124.2 8.6 %multiply_convert_fusion = bf16[896,480]{0,1:T(8,128)(2,1)S(1)} fusion(bf16[480,5760]{1,0:T(8,128)(2,1)} %constant_dynamic-update-slice_fusion.20, bf16[256,5760]{1,0:T(8,128)(2,1)S(1)} %copy-done.5, bf16[640,5760]{1,0:T(8,128)(2,1)S(1)} %copy-done.3, f32[480]{0:T(512)S(1)} %slice-done), kind=kOutput, calls=%fused_computation.15 | convolution fusion | flops 4977745920 | bytes 16713600 | tf_op jit(solution)/shard_map/dot_general | solution.py:128
  132.8 0.4 shard_map.93
  133.2 3.3 %multiply_convert_fusion.1 = bf16[896,160]{0,1:T(8,128)(2,1)S(1)} fusion(bf16[160,5760]{1,0:T(8,128)(2,1)S(1)} %shard_map.93, bf16[256,5760]{1,0:T(8,128)(2,1)S(1)} %copy-done.5, bf16[640,5760]{1,0:T(8,128)(2,1)S(1)} %copy-done.3, f32[160]{0:T(256)S(1)} %slice.195), kind=kOutput, calls=%fused_computation.44 | convolution fusion | flops 1673011200 | bytes 12452480 | tf_op jit(solution)/shard_map/dot_general | solution.py:128
  136.7 0.2 copy.23
  136.9 0.9 copy.24
  138.1 1.3 copy.25
  139.4 0.9 copy.26
  140.4 4.1 %fusion.17 = f32[640,640]{1,0:T(8,128)S(1)} fusion(bf16[640,640]{1,0:T(8,128)(2,1)} %fusion.13, bf16[640,640]{1,0:T(8,128)(2,1)} %fusion.14, bf16[640,640]{1,0:T(8,128)(2,1)} %fusion.15, bf16[640,640]{0,1:T(8,128)(2,1)S(1)} %copy.26, bf16[640,640]{0,1:T(8,128)(2,1)S(1)} %copy-done.1, bf16[640,640]{0,1:T(8,128)(2,1)} %copy.25, f32[640]{0:T(1024)S(1)} %copy-done.12), kind=kOutput, calls=%fused_computation.30 | convolution fusion | flops 1588019200 | bytes 6556160 | tf_op jit(solution)/shard_map/dot_general | solution.py:180
  144.5 0.5 fusion.28
  144.9 1.3 copy.27
  (73 shorter events, 2.5 us)
Async XLA Ops:
  0.0 25.6 %copy-start.8 = (s32[640]{0:T(1024)S(1)}, s32[640]{0:T(1024)}, u32[]{:S(2)}) copy-start(s32[640]{0:T(1024)} %constant.67.clone) | copy-start | bytes 7684
  0.0 25.6 %copy-start.9 = (s32[640]{0:T(1024)S(1)}, s32[640]{0:T(1024)}, u32[]{:S(2)}) copy-start(s32[640]{0:T(1024)} %constant.69.clone) | copy-start | bytes 7684
  0.0 25.7 %copy-start.10 = (s32[640]{0:T(1024)S(1)}, s32[640]{0:T(1024)}, u32[]{:S(2)}) copy-start(s32[640]{0:T(1024)} %constant.70.clone) | copy-start | bytes 7684
  0.0 25.7 %copy-start.11 = (s32[640]{0:T(1024)S(1)}, s32[640]{0:T(1024)}, u32[]{:S(2)}) copy-start(s32[640]{0:T(1024)} %constant.77) | copy-start | bytes 7684
  0.0 25.7 %copy-start.7 = (f32[640]{0:T(1024)S(1)}, f32[640]{0:T(1024)}, u32[]{:S(2)}) copy-start(f32[640]{0:T(1024)} %param.11) | copy-start | bytes 7684
  1.6 27.8 %all-to-all-start = ((bf16[16,40,180]{2,1,0:T(8,128)(2,1)}), bf16[16,40,180]{2,1,0:T(8,128)(2,1)S(1)}, u32[]{:S(2)}, u32[]{:S(2)}) async-start(bf16[16,40,180]{2,1,0:T(8,128)(2,1)} %broadcast_in_dim.26), calls=%async_computation | async-start | bytes 655360 | tf_op jit(solution)/shard_map/all_to_all | solution.py:56
  11.9 53.5 %collective-permute-start = (bf16[5,32,640]{2,1,0:T(8,128)(2,1)}, bf16[5,32,640]{2,1,0:T(8,128)(2,1)S(1)}, u32[]{:S(2)}, u32[]{:S(2)}) collective-permute-start(bf16[5,32,640]{2,1,0:T(8,128)(2,1)} %get-tuple-element.38), channel_id=1, source_target_pairs={{0,480},{32,64},{64,32},{96,128},{128,96},{160,192},{192,160},{224... | collective-permute-start | bytes 614408 | tf_op jit(solution)/shard_map/ppermute | solution.py:104
  23.7 41.7 %collective-permute-start.1 = (bf16[5,32,640]{2,1,0:T(8,128)(2,1)}, bf16[5,32,640]{2,1,0:T(8,128)(2,1)}, u32[]{:S(2)}, u32[]{:S(2)}) collective-permute-start(bf16[5,32,640]{2,1,0:T(8,128)(2,1)} %get-tuple-element.37), channel_id=1, source_target_pairs={{0,32},{32,0},{64,96},{96,64},{128,160},{160,128},{192,224},{224,1... | collective-permute-start | bytes 614408 | tf_op jit(solution)/shard_map/ppermute | solution.py:105
  26.0 14.6 %copy-start.6 = (f32[640]{0:T(1024)}, f32[640]{0:T(1024)S(1)}, u32[]{:S(2)}) copy-start(f32[640]{0:T(1024)S(1)} %select_reduce_fusion) | copy-start | bytes 7684
  30.3 17.2 %all-to-all-start.1 = ((bf16[4,40,1440]{2,1,0:T(8,128)(2,1)}), bf16[4,40,1440]{2,1,0:T(8,128)(2,1)S(1)}, u32[]{:S(2)}, u32[]{:S(2)}) async-start(bf16[4,40,1440]{2,1,0:T(8,128)(2,1)} %broadcast_in_dim.28), calls=%async_computation.1 | async-start | bytes 983040 | tf_op jit(solution)/shard_map/all_to_all | solution.py:64
  34.5 9.2 %collective-permute-start.8 = (bf16[40,1440]{1,0:T(8,128)(2,1)S(1)}, bf16[40,1440]{1,0:T(8,128)(2,1)S(1)}, u32[]{:S(2)}, u32[]{:S(2)}) collective-permute-start(bf16[40,1440]{1,0:T(8,128)(2,1)S(1)} %concatenate.72), channel_id=1, source_target_pairs={{128,0},{160,32},{192,64},{224,96},{0,128},{32,160},{64,192},{96,2... | collective-permute-start | bytes 345608 | tf_op jit(solution)/shard_map/ppermute | solution.py:68
  43.7 11.8 %collective-permute-start.9 = (bf16[80,1440]{1,0:T(8,128)(2,1)S(1)}, bf16[80,1440]{1,0:T(8,128)(2,1)S(1)}, u32[]{:S(2)}, u32[]{:S(2)}) collective-permute-start(bf16[80,1440]{1,0:T(8,128)(2,1)S(1)} %pad_maximum_fusion.18), channel_id=1, source_target_pairs={{384,0},{416,32},{448,64},{480,96},{256,128},{288,160},{320,192},{... | collective-permute-start | bytes 691208 | tf_op jit(solution)/shard_map/ppermute | solution.py:69
  47.7 17.7 %collective-permute-start.2 = (bf16[40,5760]{1,0:T(8,128)(2,1)S(1)}, bf16[40,5760]{1,0:T(8,128)(2,1)}, u32[]{:S(2)}, u32[]{:S(2)}) collective-permute-start(bf16[40,5760]{1,0:T(8,128)(2,1)S(1)} %shard_map.91), channel_id=1, source_target_pairs={{128,0},{160,32},{192,64},{224,96},{0,128},{32,160},{64,192},{96,2... | collective-permute-start | bytes 1382408 | tf_op jit(solution)/shard_map/ppermute | solution.py:73
  53.0 25.8 %collective-permute-start.5 = (bf16[40,5760]{1,0:T(8,128)(2,1)S(1)}, bf16[40,5760]{1,0:T(8,128)(2,1)}, u32[]{:S(2)}, u32[]{:S(2)}) collective-permute-start(bf16[40,5760]{1,0:T(8,128)(2,1)S(1)} %shard_map.91), channel_id=1, source_target_pairs={{384,0},{416,32},{448,64},{480,96},{256,128},{288,160},{320,192},{... | collective-permute-start | bytes 1382408 | tf_op jit(solution)/shard_map/ppermute | solution.py:73
  55.5 23.2 %collective-permute-start.6 = (bf16[40,5760]{1,0:T(8,128)(2,1)S(1)}, bf16[40,5760]{1,0:T(8,128)(2,1)}, u32[]{:S(2)}, u32[]{:S(2)}) collective-permute-start(bf16[40,5760]{1,0:T(8,128)(2,1)S(1)} %shard_map.91), channel_id=1, source_target_pairs={{256,0},{288,32},{320,64},{352,96},{384,128},{416,160},{448,192},{... | collective-permute-start | bytes 1382408 | tf_op jit(solution)/shard_map/ppermute | solution.py:73
  61.1 55.7 %all-to-all-start.2 = ((bf16[4,160,1440]{2,1,0:T(8,128)(2,1)}), bf16[4,160,1440]{2,1,0:T(8,128)(2,1)S(1)}, u32[]{:S(2)}, u32[]{:S(2)}) async-start(bf16[4,160,1440]{2,1,0:T(8,128)(2,1)} %broadcast_in_dim.51), calls=%async_computation.2 | async-start | bytes 3932160 | tf_op jit(solution)/shard_map/all_to_all | solution.py:64
  67.7 11.0 %collective-permute-start.3 = (bf16[6,1,32,640]{3,2,1,0:T(8,128)(2,1)S(1)}, bf16[6,1,32,640]{3,2,1,0:T(8,128)(2,1)S(1)}, u32[]{:S(2)}, u32[]{:S(2)}) collective-permute-start(bf16[6,1,32,640]{3,2,1,0:T(8,128)(2,1)S(1)} %get-tuple-element.32), channel_id=1, source_target_pairs={{0,1},{1,2},{2,3},{3,4},{4,5},{5,6},{6,7},{7,8},{8,9},{9,10},{10,1... | collective-permute-start | bytes 737288 | tf_op jit(solution)/shard_map/ppermute | solution.py:112
  75.7 24.6 %collective-permute-start.4 = (bf16[6,1,32,640]{3,2,1,0:T(8,128)(2,1)S(1)}, bf16[6,1,32,640]{3,2,1,0:T(8,128)(2,1)S(1)}, u32[]{:S(2)}, u32[]{:S(2)}) collective-permute-start(bf16[6,1,32,640]{3,2,1,0:T(8,128)(2,1)S(1)} %get-tuple-element.31), channel_id=1, source_target_pairs={{1,0},{2,1},{3,2},{4,3},{5,4},{6,5},{7,6},{8,7},{9,8},{10,9},{11,1... | collective-permute-start | bytes 737288 | tf_op jit(solution)/shard_map/ppermute | solution.py:113
  78.7 36.3 %copy-start.2 = (bf16[640,5760]{1,0:T(8,128)(2,1)}, bf16[640,5760]{1,0:T(8,128)(2,1)S(1)}, u32[]{:S(2)}) copy-start(bf16[640,5760]{1,0:T(8,128)(2,1)S(1)} %constant_dynamic-update-slice_fusion) | copy-start | bytes 22118404
  105.6 14.2 %collective-permute-start.7 = (bf16[160,5760]{1,0:T(8,128)(2,1)}, bf16[160,5760]{1,0:T(8,128)(2,1)}, u32[]{:S(2)}, u32[]{:S(2)}) collective-permute-start(bf16[160,5760]{1,0:T(8,128)(2,1)} %pad_maximum_fusion.3), channel_id=1, source_target_pairs={{0,32},{32,0},{64,96},{96,64},{128,160},{160,128},{192,224},{224,1... | collective-permute-start | bytes 5529608 | tf_op jit(solution)/shard_map/ppermute | solution.py:155
  112.8 2.2 %copy-start.4 = (bf16[256,5760]{1,0:T(8,128)(2,1)}, bf16[256,5760]{1,0:T(8,128)(2,1)S(1)}, u32[]{:S(2)}) copy-start(bf16[256,5760]{1,0:T(8,128)(2,1)S(1)} %constant_dynamic-update-slice_fusion.11) | copy-start | bytes 8847364
  116.8 7.3 %copy-start.5 = (bf16[256,5760]{1,0:T(8,128)(2,1)S(1)}, bf16[256,5760]{1,0:T(8,128)(2,1)}, u32[]{:S(2)}) copy-start(bf16[256,5760]{1,0:T(8,128)(2,1)} %copy-done.4) | copy-start | bytes 8847364
  116.8 7.3 %slice-start = ((f32[640]{0:T(1024)}), f32[480]{0:T(512)S(1)}, s32[]{:S(2)}) async-start(f32[640]{0:T(1024)} %copy-done.6), calls=%async_computation.3 | async-start | bytes 4096 | tf_op jit(solution)/shard_map/slice | solution.py:169
  117.3 6.9 %copy-start.3 = (bf16[640,5760]{1,0:T(8,128)(2,1)S(1)}, bf16[640,5760]{1,0:T(8,128)(2,1)}, u32[]{:S(2)}) copy-start(bf16[640,5760]{1,0:T(8,128)(2,1)} %copy-done.2) | copy-start | bytes 22118404
  117.3 15.5 %collective-permute-start.10 = (bf16[4,160,1440]{2,1,0:T(8,128)(2,1)S(1)}, bf16[4,160,1440]{2,1,0:T(8,128)(2,1)S(1)}, u32[]{:S(2)}, u32[]{:S(2)}) collective-permute-start(bf16[4,160,1440]{2,1,0:T(8,128)(2,1)S(1)} %all-to-all-done.2.parts_ref), channel_id=1, source_target_pairs={{0,32},{32,0},{64,96},{96,64},{128,160},{160,128},{192,224},{224,1... | collective-permute-start | bytes 5529608 | tf_op jit(solution)/shard_map/ppermute | solution.py:146
  136.7 1.2 copy-start
  137.9 2.4 %copy-start.12 = (f32[640]{0:T(1024)S(1)}, f32[640]{0:T(1024)}, u32[]{:S(2)}) copy-start(f32[640]{0:T(1024)} %param.13) | copy-start | bytes 7684
  138.1 2.3 %copy-start.1 = (bf16[640,640]{0,1:T(8,128)(2,1)S(1)}, bf16[640,640]{0,1:T(8,128)(2,1)}, u32[]{:S(2)}) copy-start(bf16[640,640]{0,1:T(8,128)(2,1)} %copy-done) | copy-start | bytes 2457604

commit v5 on v4

v5 whole, which is shorter than its diff:
```python
import functools

import jax
import jax.numpy as jnp
import numpy as np
from jax import lax
from jax.experimental import pallas as pl
from jax.experimental.pallas import tpu as pltpu
from jax.sharding import PartitionSpec as P

LONS = 16
FRAMES_AXIS = 32
Y = 4
X = 4
Z_LO = 8


def lon_index(y, z_hi, core):
    return y * 4 + z_hi * 2 + core


def frame_index(x, z_lo):
    return x * Z_LO + z_lo


def z_groups():
    return [
        [
            lon_index(y, z_hi, core) * FRAMES_AXIS + frame_index(x, z_lo)
            for z_hi in range(2)
            for z_lo in range(Z_LO)
        ]
        for x in range(X)
        for y in range(Y)
        for core in range(2)
    ]


def x_groups():
    return [[frame_index(x, z_lo) for x in range(X)] for z_lo in range(Z_LO)]


def across_y(k):
    return [((y ^ k) * 4 + r, y * 4 + r) for y in range(Y) for r in range(4)]


NEAR_FIRST = (0, 1, 3, 2)
CORES = [(i, i ^ 1) for i in range(LONS)]


def far_steps():
    first, second = [], []
    for lon in range(LONS):
        y, z_hi, core = lon // 4, lon // 2 % 2, lon % 2
        target = (lon + 1) % LONS if core else (lon - 1) % LONS
        for frame in range(FRAMES_AXIS):
            x, z_lo = frame // Z_LO, frame % Z_LO
            z = (z_hi * Z_LO + z_lo + (4 if core else 12)) % 16
            relay = lon_index(y, z // Z_LO, core) * FRAMES_AXIS + frame_index(x, z % Z_LO)
            first.append((lon * FRAMES_AXIS + frame, relay))
            second.append((relay, target * FRAMES_AXIS + frame))
    return first, second


def across_x(k):
    return [
        (frame_index(x ^ k, z_lo), frame_index(x, z_lo)) for x in range(X) for z_lo in range(Z_LO)
    ]


def copies(piece, count):
    return jnp.broadcast_to(piece[None], (count,) + piece.shape)


def gather_z(spatial_kernel):
    shard = spatial_kernel.T
    cols, rows = shard.shape
    along_z = lax.all_to_all(
        copies(shard, 16), ("lon", "frame"), 0, 0, axis_index_groups=z_groups()
    )
    along_z = along_z.reshape(2, Z_LO, cols, rows)
    return [jnp.concatenate([along_z[h, z] for z in range(Z_LO)], axis=1) for h in range(2)]


def over_x(block):
    return lax.all_to_all(copies(block, X), "frame", 0, 0, axis_index_groups=x_groups())


def doubled_over_y(block):
    block = jnp.concatenate([block, lax.ppermute(block, "lon", across_y(1))])
    return jnp.concatenate([block, lax.ppermute(block, "lon", across_y(3))])


def over_y(block):
    return [block] + [lax.ppermute(block, "lon", across_y(k)) for k in NEAR_FIRST[1:]]


def piecewise_over_x(block):
    return [block] + [lax.ppermute(block, "frame", across_x(k)) for k in NEAR_FIRST[1:]]


def joined_x(along_x):
    return jnp.concatenate([along_x[x] for x in range(X)], axis=1)


def channel_order():
    lon = lax.axis_index("lon")
    blocks = [(k, z_hi, side) for z_hi, side in ((0, 0), (0, 1), (1, 0), (1, 1)) for k in NEAR_FIRST]
    row, z_hi, side = (jnp.asarray(np.repeat(np.array(v), 40)) for v in zip(*blocks))
    within = jnp.asarray(np.tile(np.arange(40), LONS))
    return lon_index((lon // 4) ^ row, z_hi, (lon % 2) ^ side) * 40 + within


def lon_halos(columns):
    core = lax.axis_index("lon") % 2
    first, _ = far_steps()
    far = lax.ppermute(jnp.where(core == 1, columns[-1], columns[0]), ("lon", "frame"), first)
    near = lax.ppermute(jnp.where(core == 1, columns[0], columns[-1]), "lon", CORES)
    return far, near


def frame_halos(wide):
    up = [(i, i + 1) for i in range(FRAMES_AXIS - 1)]
    down = [(i + 1, i) for i in range(FRAMES_AXIS - 1)]
    earlier = lax.ppermute(wide[:, -1:], "frame", up)
    later = lax.ppermute(wide[:, :1], "frame", down)
    return earlier, later


VMEM = pl.BlockSpec(memory_space=pltpu.VMEM)
SMEM = pl.BlockSpec(memory_space=pltpu.SMEM)
ANY = pl.BlockSpec(memory_space=pl.ANY)


def params(mebibytes):
    return pltpu.CompilerParams(vmem_limit_bytes=mebibytes * 2**20)


def order_kernel(order_ref, kernel_ref, out_ref):
    channels = order_ref.shape[0]
    for k in range(3):
        part = slice(k * channels, (k + 1) * channels)
        moved = jnp.dot(order_ref[...], kernel_ref[part], preferred_element_type=jnp.float32)
        out_ref[part] = moved.astype(jnp.bfloat16)


def shift_rows(planes_ref, taps_ref, lat_rows):
    planes, rows, channels = planes_ref.shape
    row = lax.rem(lax.broadcasted_iota(jnp.int32, (rows, channels), 0), lat_rows)

    def plane(p, carry):
        here = planes_ref[p]
        wider = here.astype(jnp.float32)
        above = jnp.where(row == 0, 0.0, pltpu.roll(wider, 1, 0))
        below = jnp.where(row == lat_rows - 1, 0.0, pltpu.roll(wider, rows - 1, 0))
        taps_ref[0, p] = above.astype(jnp.bfloat16)
        taps_ref[1, p] = here
        taps_ref[2, p] = below.astype(jnp.bfloat16)
        return carry

    lax.fori_loop(0, planes, plane, 0)


def join_rows(parts_ref, joined_ref):
    parts, _, width = parts_ref.shape
    for x in range(parts):
        joined_ref[:, x * width : (x + 1) * width] = parts_ref[x]


def silu(v):
    return v * jax.nn.sigmoid(v)


def block_kernel(
    lat_rows, flags_ref, planes_any, low_any, other_low_any, h0, h1, h2, h3, o0, o1, o2, o3,
    kernel_any, bias_ref, tbias_ref, out_ref, planes_ref, low_ref, other_low_ref, high_ref,
    other_high_ref, kernel_ref, taps_ref, joined_ref, other_joined_ref, sems,
):
    x = lax.axis_index("frame") // Z_LO
    pairs = [(planes_any, planes_ref)]
    pairs += [(part, high_ref.at[x ^ k]) for k, part in zip(NEAR_FIRST, (h0, h1, h2, h3))]
    pairs += [(part, other_high_ref.at[x ^ k]) for k, part in zip(NEAR_FIRST, (o0, o1, o2, o3))]
    pairs += [(low_any, low_ref), (other_low_any, other_low_ref), (kernel_any, kernel_ref)]
    moves = [
        pltpu.make_async_copy(source, target, sems.at[i])
        for i, (source, target) in enumerate(pairs)
    ]
    for move in moves:
        move.start()
    moves[0].wait()
    shift_rows(planes_ref, taps_ref, lat_rows)
    for move in moves[1:5]:
        move.wait()
    join_rows(high_ref, joined_ref)
    for move in moves[5:9]:
        move.wait()
    join_rows(other_high_ref, other_joined_ref)
    moves[9].wait()
    moves[10].wait()

    planes, rows, channels = planes_ref.shape
    columns, inner = planes - 2, rows - 2 * lat_rows
    total = None
    for a in range(3):
        taps = [taps_ref[a, b : b + columns].reshape(columns * rows, channels) for b in range(3)]
        part = slice(3 * a * channels, 3 * (a + 1) * channels)
        weights = [r[:, part] for r in (low_ref, other_low_ref, joined_ref, other_joined_ref)]
        term = lax.dot_general(
            jnp.concatenate(taps, axis=1),
            jnp.concatenate(weights, axis=0),
            (((1,), (1,)), ((), ())),
            preferred_element_type=jnp.float32,
        )
        total = term if total is None else total + term
    active = silu(total + bias_ref[...])
    row = lax.rem(lax.broadcasted_iota(jnp.int32, active.shape, 0), rows)
    outside = (row < lat_rows) & (flags_ref[0] == 1)
    outside = outside | ((row >= rows - lat_rows) & (flags_ref[1] == 1))
    hidden = jnp.where(outside, 0.0, active).astype(jnp.bfloat16).reshape(columns, rows, channels)
    stacked = [
        hidden[:, k * lat_rows : k * lat_rows + inner].reshape(columns * inner, channels)
        for k in range(3)
    ]
    moves[11].wait()
    mixed = jnp.dot(
        jnp.concatenate(stacked, axis=1), kernel_ref[...], preferred_element_type=jnp.float32
    )
    mixed = silu(mixed + tbias_ref[...]).reshape(columns, inner, channels)
    here = planes_ref[1 : planes - 1, lat_rows : lat_rows + inner].astype(jnp.float32)
    out_ref[...] = (here + mixed).astype(jnp.bfloat16)


def block(flags, planes, low, other_low, high, other_high, kernel, bias, tbias, lat_rows):
    count, rows, channels = planes.shape
    inner = rows - 2 * lat_rows
    moved = (planes, low, other_low, *high, *other_high, kernel)
    parts = (len(high), *high[0].shape)
    shapes = (planes.shape, low.shape, low.shape, parts, parts, kernel.shape)
    shapes += ((3, *planes.shape), low.shape, low.shape)
    flops = (count - 2) * 2 * channels * channels * (9 * rows + 3 * inner)
    return pl.pallas_call(
        functools.partial(block_kernel, lat_rows),
        out_shape=jax.ShapeDtypeStruct((count - 2, inner, channels), jnp.bfloat16),
        in_specs=[SMEM] + [ANY] * len(moved) + [VMEM, VMEM],
        out_specs=VMEM,
        scratch_shapes=[pltpu.VMEM(s, jnp.bfloat16) for s in shapes]
        + [pltpu.SemaphoreType.DMA((len(moved),))],
        compiler_params=params(34),
        cost_estimate=pl.CostEstimate(flops=flops, bytes_accessed=2**24, transcendentals=0),
    )(flags, *moved, bias, tbias)


def reordered(order, kernel):
    return pl.pallas_call(
        order_kernel,
        out_shape=jax.ShapeDtypeStruct(kernel.shape, jnp.bfloat16),
        in_specs=[VMEM, VMEM],
        out_specs=VMEM,
        compiler_params=params(16),
        cost_estimate=pl.CostEstimate(
            flops=2 * kernel.size * order.shape[0], bytes_accessed=2**23, transcendentals=0
        ),
    )(order, kernel)


def body(latents, spatial_kernel, spatial_bias, temporal_kernel, temporal_bias):
    frames, lat_rows, lon_cols, channels = latents.shape
    core = lax.axis_index("lon") % 2
    columns = latents.transpose(2, 0, 1, 3)
    far, near = lon_halos(columns)
    low, high = gather_z(spatial_kernel)
    far, near, low, high = lax.optimization_barrier((far, near, low, high))
    far = lax.ppermute(far, ("lon", "frame"), far_steps()[1])
    high = doubled_over_y(high)
    low = joined_x(over_x(low))
    far, near, columns, temporal_kernel, low, high = lax.optimization_barrier(
        (far, near, columns, temporal_kernel, low, high)
    )
    low = over_y(low)
    high = piecewise_over_x(high)
    before = jnp.where(core == 1, near, far)
    after = jnp.where(core == 1, far, near)
    wide = jnp.concatenate([before[None], columns, after[None]], axis=0)
    earlier, later = frame_halos(wide)
    other_own = lax.ppermute(high[0], "lon", CORES)
    low = jnp.concatenate(low)
    order = channel_order()[:, None] == lax.broadcasted_iota(jnp.int32, (channels, channels), 1)
    bias = jnp.sum(jnp.where(order, spatial_bias[None, :], 0.0), axis=1)
    ordered = reordered(order.astype(jnp.bfloat16), temporal_kernel)
    earlier, later, low, ordered, bias, *_ = lax.optimization_barrier(
        (earlier, later, low, ordered, bias, *high)
    )
    other_high = [other_own] + [lax.ppermute(part, "lon", CORES) for part in high[1:]]
    planes = jnp.concatenate([earlier, wide, later], axis=1)
    planes = planes.reshape(lon_cols + 2, (frames + 2) * lat_rows, channels)
    other_low = lax.ppermute(low, "lon", CORES)

    frame = lax.axis_index("frame")
    flags = jnp.stack([frame == 0, frame == FRAMES_AXIS - 1]).astype(jnp.int32)
    result = block(
        flags, planes, low, other_low, high, other_high, ordered, bias[None],
        temporal_bias[None], lat_rows,
    )
    return result.reshape(lon_cols, frames, lat_rows, channels).transpose(1, 2, 0, 3)


def solution(mesh):
    placed = (P("frame", None, "lon", None), P("frame", "lon"), P(), P(), P())
    return jax.shard_map(
        body, mesh=mesh, in_specs=placed, out_specs=P("frame", None, "lon", None), check_vma=False
    )
```

time: 147 us -> 153 us (1.041)
  the two profiles are of different devices: /device:TPU:481 before, /device:TPU:7 now
where the time goes in v5:
time: 153 us; the launch traced here: 152 us
  starting transfers between devices  83.3 us (54%)
  waiting for transfers between devices  35.8 us (23%)
  Pallas kernels  19 us (12%)
  local copies, waits for them, and re-layouts  8.05 us (5%)
  other arithmetic  4.93 us (3%)
    pallas_call x1, Pallas kernels, block(): pl.pallas_call(functools.partial(block_kernel, lat_rows), out_shape=jax.S...  16.7 us
    all_to_all x1, starting transfers between devices, gather_z(): lax.all_to_all(copies(shard, 16), ('lon', 'frame'), 0, 0, axis_index_grou...  14.9 us
    ppermute x1, starting transfers between devices, body(): far = lax.ppermute(far, ('lon', 'frame'), far_steps()[1])  11.6 us
    ppermute x1, waiting for transfers between devices, lon_halos(): lax.ppermute(jnp.where(core == 1, columns[-1], columns[0]), ('lon', 'fram...  10.2 us
    ppermute x1, waiting for transfers between devices, frame_halos(): earlier = lax.ppermute(wide[:, -1:], 'frame', up)  9.82 us
    ppermute x3, starting transfers between devices, piecewise_over_x(): lax.ppermute(block, 'frame', across_x(k))  8.7 us
    ppermute x3, starting transfers between devices, over_y(): lax.ppermute(block, 'lon', across_y(k))  8.37 us
    ppermute x1, starting transfers between devices, lon_halos(): lax.ppermute(jnp.where(core == 1, columns[-1], columns[0]), ('lon', 'fram...  7.45 us
  transfers between devices with their start and end apart: 20, of which 6 were waited for; matrix products, arithmetic and copies ran while one was open for 6% of the time, Pallas kernels for 2%

profile of v5, /device:TPU:7, one launch (start us, length us, event | category | flops | bytes accessed | tf_op | source)
XLA Modules:
  0.0 151.6 jit_solution(733138435372427708)
XLA Ops:
  0.0 0.0 copy-start.11
  0.0 1.5 broadcast_in_dim.38
  1.5 14.9 %all-to-all-start = ((bf16[16,40,180]{2,1,0:T(8,128)(2,1)}), bf16[16,40,180]{2,1,0:T(8,128)(2,1)S(1)}, u32[]{:S(2)}, u32[]{:S(2)}) async-start(bf16[16,40,180]{2,1,0:T(8,128)(2,1)} %broadcast_in_dim.38), calls=%async_computation | async-start | bytes 655360 | tf_op jit(solution)/shard_map/all_to_all | solution.py:78
  16.5 1.2 copy.20
  17.7 0.0 copy-start.3
  17.8 2.9 %collective-permute-start.1 = (bf16[5,32,640]{2,1,0:T(8,128)(2,1)S(1)}, bf16[5,32,640]{2,1,0:T(8,128)(2,1)S(1)}, u32[]{:S(2)}, u32[]{:S(2)}) collective-permute-start(bf16[5,32,640]{2,1,0:T(8,128)(2,1)S(1)} %get-tuple-element.37), channel_id=1, source_target_pairs={{0,32},{32,0},{64,96},{96,64},{128,160},{160,128},{192,224},{224,1... | collective-permute-start | bytes 614408 | tf_op jit(solution)/shard_map/ppermute | solution.py:118
  20.7 7.4 %collective-permute-start = (bf16[5,32,640]{2,1,0:T(8,128)(2,1)S(1)}, bf16[5,32,640]{2,1,0:T(8,128)(2,1)}, u32[]{:S(2)}, u32[]{:S(2)}) collective-permute-start(bf16[5,32,640]{2,1,0:T(8,128)(2,1)S(1)} %get-tuple-element.38), channel_id=1, source_target_pairs={{0,68},{1,69},{2,70},{3,71},{4,0},{5,1},{6,2},{7,3},{8,76},{9,77},... | collective-permute-start | bytes 614408 | tf_op jit(solution)/shard_map/ppermute | solution.py:117
  28.2 0.0 copy-start.6
  28.2 0.2 fusion.order_ref
  28.4 3.3 %all-to-all-done = bf16[16,40,180]{2,1,0:T(8,128)(2,1)S(1)} async-done(((bf16[16,40,180]{2,1,0:T(8,128)(2,1)}), bf16[16,40,180]{2,1,0:T(8,128)(2,1)S(1)}, u32[]{:S(2)}, u32[]{:S(2)}) %all-to-all-start) | async-done | bytes 230432 | tf_op jit(solution)/shard_map/all_to_all | solution.py:78
  31.7 0.1 concatenate.26
  31.9 0.1 concatenate.25
  32.0 10.2 %collective-permute-done = bf16[5,32,640]{2,1,0:T(8,128)(2,1)} collective-permute-done((bf16[5,32,640]{2,1,0:T(8,128)(2,1)S(1)}, bf16[5,32,640]{2,1,0:T(8,128)(2,1)}, u32[]{:S(2)}, u32[]{:S(2)}) %collective-permute-start) | collective-permute-done | bytes 204832 | tf_op jit(solution)/shard_map/ppermute | solution.py:117
  42.3 3.2 %collective-permute-start.3 = (bf16[40,1440]{1,0:T(8,128)(2,1)S(1)}, bf16[40,1440]{1,0:T(8,128)(2,1)S(1)}, u32[]{:S(2)}, u32[]{:S(2)}) collective-permute-start(bf16[40,1440]{1,0:T(8,128)(2,1)S(1)} %concatenate.26), channel_id=1, source_target_pairs={{128,0},{160,32},{192,64},{224,96},{0,128},{32,160},{64,192},{96,2... | collective-permute-start | bytes 345608 | tf_op jit(solution)/shard_map/ppermute | solution.py:90
  45.5 0.8 broadcast_in_dim.39
  46.3 4.2 %all-to-all-start.1 = ((bf16[4,40,1440]{2,1,0:T(8,128)(2,1)}), bf16[4,40,1440]{2,1,0:T(8,128)(2,1)S(1)}, u32[]{:S(2)}, u32[]{:S(2)}) async-start(bf16[4,40,1440]{2,1,0:T(8,128)(2,1)} %broadcast_in_dim.39), calls=%async_computation.1 | async-start | bytes 983040 | tf_op jit(solution)/shard_map/all_to_all | solution.py:86
  50.5 0.3 select_reduce_fusion
  50.8 11.6 %collective-permute-start.2 = (bf16[5,32,640]{2,1,0:T(8,128)(2,1)}, bf16[5,32,640]{2,1,0:T(8,128)(2,1)}, u32[]{:S(2)}, u32[]{:S(2)}) collective-permute-start(bf16[5,32,640]{2,1,0:T(8,128)(2,1)} %collective-permute-done), channel_id=1, source_target_pairs={{68,480},{69,481},{70,482},{71,483},{0,484},{1,485},{2,486},{3,487... | collective-permute-start | bytes 614408 | tf_op jit(solution)/shard_map/ppermute | solution.py:273
  62.5 4.4 %collective-permute-start.4 = (bf16[80,1440]{1,0:T(8,128)(2,1)S(1)}, bf16[80,1440]{1,0:T(8,128)(2,1)S(1)}, u32[]{:S(2)}, u32[]{:S(2)}) collective-permute-start(bf16[80,1440]{1,0:T(8,128)(2,1)S(1)} %pad_maximum_fusion.6), channel_id=1, source_target_pairs={{384,0},{416,32},{448,64},{480,96},{256,128},{288,160},{320,192},{... | collective-permute-start | bytes 691208 | tf_op jit(solution)/shard_map/ppermute | solution.py:91
  67.0 1.1 concatenate.27
  68.1 6.0 %collective-permute-done.4 = bf16[80,1440]{1,0:T(8,128)(2,1)S(1)} collective-permute-done((bf16[80,1440]{1,0:T(8,128)(2,1)S(1)}, bf16[80,1440]{1,0:T(8,128)(2,1)S(1)}, u32[]{:S(2)}, u32[]{:S(2)}) %collective-permute-start.4) | collective-permute-done | bytes 230432 | tf_op jit(solution)/shard_map/ppermute | solution.py:91
  74.1 2.9 %collective-permute-start.9 = (bf16[40,5760]{1,0:T(8,128)(2,1)}, bf16[40,5760]{1,0:T(8,128)(2,1)S(1)}, u32[]{:S(2)}, u32[]{:S(2)}) collective-permute-start(bf16[40,5760]{1,0:T(8,128)(2,1)} %concatenate.27), channel_id=1, source_target_pairs={{256,0},{288,32},{320,64},{352,96},{384,128},{416,160},{448,192},{... | collective-permute-start | bytes 1382408 | tf_op jit(solution)/shard_map/ppermute | solution.py:95
  77.0 2.7 %collective-permute-start.8 = (bf16[40,5760]{1,0:T(8,128)(2,1)}, bf16[40,5760]{1,0:T(8,128)(2,1)S(1)}, u32[]{:S(2)}, u32[]{:S(2)}) collective-permute-start(bf16[40,5760]{1,0:T(8,128)(2,1)} %concatenate.27), channel_id=1, source_target_pairs={{384,0},{416,32},{448,64},{480,96},{256,128},{288,160},{320,192},{... | collective-permute-start | bytes 1382408 | tf_op jit(solution)/shard_map/ppermute | solution.py:95
  79.7 2.8 %collective-permute-start.7 = (bf16[40,5760]{1,0:T(8,128)(2,1)}, bf16[40,5760]{1,0:T(8,128)(2,1)S(1)}, u32[]{:S(2)}, u32[]{:S(2)}) collective-permute-start(bf16[40,5760]{1,0:T(8,128)(2,1)} %concatenate.27), channel_id=1, source_target_pairs={{128,0},{160,32},{192,64},{224,96},{0,128},{32,160},{64,192},{96,2... | collective-permute-start | bytes 1382408 | tf_op jit(solution)/shard_map/ppermute | solution.py:95
  82.5 3.1 %collective-permute-start.12 = (bf16[160,1440]{1,0:T(8,128)(2,1)S(1)}, bf16[160,1440]{1,0:T(8,128)(2,1)S(1)}, u32[]{:S(2)}, u32[]{:S(2)}) collective-permute-start(bf16[160,1440]{1,0:T(8,128)(2,1)S(1)} %pad_maximum_fusion.2.h0), channel_id=1, source_target_pairs={{16,0},{17,1},{18,2},{19,3},{20,4},{21,5},{22,6},{23,7},{24,8},{25... | collective-permute-start | bytes 1382408 | tf_op jit(solution)/shard_map/ppermute | solution.py:99
  85.6 3.7 %collective-permute-start.11 = (bf16[160,1440]{1,0:T(8,128)(2,1)S(1)}, bf16[160,1440]{1,0:T(8,128)(2,1)S(1)}, u32[]{:S(2)}, u32[]{:S(2)}) collective-permute-start(bf16[160,1440]{1,0:T(8,128)(2,1)S(1)} %pad_maximum_fusion.2.h0), channel_id=1, source_target_pairs={{24,0},{25,1},{26,2},{27,3},{28,4},{29,5},{30,6},{31,7},{16,8},{17... | collective-permute-start | bytes 1382408 | tf_op jit(solution)/shard_map/ppermute | solution.py:99
  89.3 1.1 select_bitcast_fusion.1
  90.4 0.1 pad_maximum_fusion.3
  90.5 2.3 %shard_map.91.kernel_any = bf16[1920,640]{1,0:T(8,128)(2,1)S(1)} custom-call(bf16[640,640]{1,0:T(8,128)(2,1)S(1)} %fusion.order_ref, bf16[1920,640]{1,0:T(8,128)(2,1)S(1)} %copy-done), custom_call_target="tpu_custom_call" | custom-call | flops 1572864000 | bytes 8388608 | tf_op jit(solution)/shard_map/pallas_call | solution.py:254
  92.8 1.4 copy-done.1
  94.3 1.9 %collective-permute-start.10 = (bf16[160,1440]{1,0:T(8,128)(2,1)S(1)}, bf16[160,1440]{1,0:T(8,128)(2,1)}, u32[]{:S(2)}, u32[]{:S(2)}) collective-permute-start(bf16[160,1440]{1,0:T(8,128)(2,1)S(1)} %pad_maximum_fusion.2.h0), channel_id=1, source_target_pairs={{8,0},{9,1},{10,2},{11,3},{12,4},{13,5},{14,6},{15,7},{0,8},{1,9},... | collective-permute-start | bytes 1382408 | tf_op jit(solution)/shard_map/ppermute | solution.py:99
  96.2 3.9 %collective-permute-done.8 = bf16[40,5760]{1,0:T(8,128)(2,1)S(1)} collective-permute-done((bf16[40,5760]{1,0:T(8,128)(2,1)}, bf16[40,5760]{1,0:T(8,128)(2,1)S(1)}, u32[]{:S(2)}, u32[]{:S(2)}) %collective-permute-start.8) | collective-permute-done | bytes 460832 | tf_op jit(solution)/shard_map/ppermute | solution.py:95
  100.1 2.5 %collective-permute-start.6 = (bf16[6,1,32,640]{3,2,1,0:T(8,128)(2,1)S(1)}, bf16[6,1,32,640]{3,2,1,0:T(8,128)(2,1)}, u32[]{:S(2)}, u32[]{:S(2)}) collective-permute-start(bf16[6,1,32,640]{3,2,1,0:T(8,128)(2,1)S(1)} %get-tuple-element.35), channel_id=1, source_target_pairs={{1,0},{2,1},{3,2},{4,3},{5,4},{6,5},{7,6},{8,7},{9,8},{10,9},{11,1... | collective-permute-start | bytes 737288 | tf_op jit(solution)/shard_map/ppermute | solution.py:126
  102.6 0.0 copy-start.7
  102.6 2.8 %collective-permute-start.5 = (bf16[6,1,32,640]{3,2,1,0:T(8,128)(2,1)S(1)}, bf16[6,1,32,640]{3,2,1,0:T(8,128)(2,1)}, u32[]{:S(2)}, u32[]{:S(2)}) collective-permute-start(bf16[6,1,32,640]{3,2,1,0:T(8,128)(2,1)S(1)} %get-tuple-element.36), channel_id=1, source_target_pairs={{0,1},{1,2},{2,3},{3,4},{4,5},{5,6},{6,7},{7,8},{8,9},{9,10},{10,1... | collective-permute-start | bytes 737288 | tf_op jit(solution)/shard_map/ppermute | solution.py:125
  105.4 1.2 pad_maximum_fusion.low_any
  106.6 2.5 %collective-permute-done.6 = bf16[6,1,32,640]{3,2,1,0:T(8,128)(2,1)} collective-permute-done((bf16[6,1,32,640]{3,2,1,0:T(8,128)(2,1)S(1)}, bf16[6,1,32,640]{3,2,1,0:T(8,128)(2,1)}, u32[]{:S(2)}, u32[]{:S(2)}) %collective-permute-start.6) | collective-permute-done | bytes 245792 | tf_op jit(solution)/shard_map/ppermute | solution.py:126
  109.1 9.8 %collective-permute-done.5 = bf16[6,1,32,640]{3,2,1,0:T(8,128)(2,1)} collective-permute-done((bf16[6,1,32,640]{3,2,1,0:T(8,128)(2,1)S(1)}, bf16[6,1,32,640]{3,2,1,0:T(8,128)(2,1)}, u32[]{:S(2)}, u32[]{:S(2)}) %collective-permute-start.5) | collective-permute-done | bytes 245792 | tf_op jit(solution)/shard_map/ppermute | solution.py:125
  118.9 3.5 %collective-permute-start.13 = (bf16[160,5760]{1,0:T(8,128)(2,1)S(1)}, bf16[160,5760]{1,0:T(8,128)(2,1)}, u32[]{:S(2)}, u32[]{:S(2)}) collective-permute-start(bf16[160,5760]{1,0:T(8,128)(2,1)S(1)} %pad_maximum_fusion.low_any), channel_id=1, source_target_pairs={{0,32},{32,0},{64,96},{96,64},{128,160},{160,128},{192,224},{224,1... | collective-permute-start | bytes 5529608 | tf_op jit(solution)/shard_map/ppermute | solution.py:296
  122.4 1.9 %collective-permute-start.14 = (bf16[160,1440]{1,0:T(8,128)(2,1)S(1)}, bf16[160,1440]{1,0:T(8,128)(2,1)}, u32[]{:S(2)}, u32[]{:S(2)}) collective-permute-start(bf16[160,1440]{1,0:T(8,128)(2,1)S(1)} %pad_maximum_fusion.2.h0), channel_id=1, source_target_pairs={{0,32},{32,0},{64,96},{96,64},{128,160},{160,128},{192,224},{224,1... | collective-permute-start | bytes 1382408 | tf_op jit(solution)/shard_map/ppermute | solution.py:285
  124.3 2.4 %collective-permute-start.17 = (bf16[160,1440]{1,0:T(8,128)(2,1)S(1)}, bf16[160,1440]{1,0:T(8,128)(2,1)}, u32[]{:S(2)}, u32[]{:S(2)}) collective-permute-start(bf16[160,1440]{1,0:T(8,128)(2,1)S(1)} %collective-permute-done.12.h3), channel_id=1, source_target_pairs={{0,32},{32,0},{64,96},{96,64},{128,160},{160,128},{192,224},{224,1... | collective-permute-start | bytes 1382408 | tf_op jit(solution)/shard_map/ppermute | solution.py:293
  126.7 1.9 %collective-permute-start.16 = (bf16[160,1440]{1,0:T(8,128)(2,1)S(1)}, bf16[160,1440]{1,0:T(8,128)(2,1)}, u32[]{:S(2)}, u32[]{:S(2)}) collective-permute-start(bf16[160,1440]{1,0:T(8,128)(2,1)S(1)} %collective-permute-done.11.h2), channel_id=1, source_target_pairs={{0,32},{32,0},{64,96},{96,64},{128,160},{160,128},{192,224},{224,1... | collective-permute-start | bytes 1382408 | tf_op jit(solution)/shard_map/ppermute | solution.py:293
  128.7 2.6 %collective-permute-start.15 = (bf16[160,1440]{1,0:T(8,128)(2,1)}, bf16[160,1440]{1,0:T(8,128)(2,1)}, u32[]{:S(2)}, u32[]{:S(2)}) collective-permute-start(bf16[160,1440]{1,0:T(8,128)(2,1)} %collective-permute-done.10.h1), channel_id=1, source_target_pairs={{0,32},{32,0},{64,96},{96,64},{128,160},{160,128},{192,224},{224,1... | collective-permute-start | bytes 1382408 | tf_op jit(solution)/shard_map/ppermute | solution.py:293
  131.3 0.1 add_convert_fusion.flags_ref
  131.4 1.9 %pad_maximum_fusion.1 = bf16[6,7,32,640]{3,2,1,0:T(8,128)(2,1)S(1)} fusion(bf16[6,1,32,640]{3,2,1,0:T(8,128)(2,1)} %collective-permute-done.6, bf16[1,5,32,640]{3,2,1,0:T(8,128)(2,1)} %copy-done.4, bf16[4,5,32,640]{3,2,1,0:T(8,128)(2,1)} %bitcast.64, bf16[1,5,32,640]{3,2,1,0:T(8,128)(2,1)S(1)} %get-tuple-element.43, ...), kind=kLoop, calls=%fused_computation.1 | loop fusion | flops 3440640 | bytes 3440640 | tf_op jit(solution)/shard_map/concatenate | solution.py:294
  133.3 0.3 copy-done.2
  133.6 16.7 %shard_map.92 = bf16[4,160,640]{2,1,0:T(8,128)(2,1)S(1)} custom-call(s32[2]{0:T(128)S(1)} %add_convert_fusion.flags_ref, bf16[6,224,640]{2,1,0:T(8,128)(2,1)S(1)} %bitcast.60, bf16[160,5760]{1,0:T(8,128)(2,1)S(1)} %pad_maximum_fusion.low_any, bf16[160,5760]{1,0:T(8,128)(2,1)} %collective-permute-done.13.other_low_any, ...), custom_call_target="tpu_custom_call" | custom-call | flops 8178892800 | bytes 16777216 | tf_op jit(solution)/shard_map/pallas_call | solution.py:241
  150.3 1.3 copy.19
  (40 shorter events, 0.3 us)
Async XLA Ops:
  0.0 28.1 %copy-start.8 = (s32[640]{0:T(1024)S(1)}, s32[640]{0:T(1024)}, u32[]{:S(2)}) copy-start(s32[640]{0:T(1024)} %constant.64) | copy-start | bytes 7684
  0.0 28.1 %copy-start.9 = (s32[640]{0:T(1024)S(1)}, s32[640]{0:T(1024)}, u32[]{:S(2)}) copy-start(s32[640]{0:T(1024)} %constant.61.clone) | copy-start | bytes 7684
  0.0 28.1 %copy-start.10 = (s32[640]{0:T(1024)S(1)}, s32[640]{0:T(1024)}, u32[]{:S(2)}) copy-start(s32[640]{0:T(1024)} %constant.60.clone) | copy-start | bytes 7684
  0.0 28.1 %copy-start.11 = (s32[640]{0:T(1024)S(1)}, s32[640]{0:T(1024)}, u32[]{:S(2)}) copy-start(s32[640]{0:T(1024)} %constant.58.clone) | copy-start | bytes 7684
  1.5 30.2 %all-to-all-start = ((bf16[16,40,180]{2,1,0:T(8,128)(2,1)}), bf16[16,40,180]{2,1,0:T(8,128)(2,1)S(1)}, u32[]{:S(2)}, u32[]{:S(2)}) async-start(bf16[16,40,180]{2,1,0:T(8,128)(2,1)} %broadcast_in_dim.38), calls=%async_computation | async-start | bytes 655360 | tf_op jit(solution)/shard_map/all_to_all | solution.py:78
  17.7 72.8 %copy-start.3 = (bf16[5,32,4,640]{3,1,0,2:T(8,128)(2,1)}, bf16[5,32,4,640]{3,1,0,2:T(8,128)(2,1)S(1)}, u32[]{:S(2)}) copy-start(bf16[5,32,4,640]{3,1,0,2:T(8,128)(2,1)S(1)} %copy.20) | copy-start | bytes 2457604
  17.8 14.2 %collective-permute-start.1 = (bf16[5,32,640]{2,1,0:T(8,128)(2,1)S(1)}, bf16[5,32,640]{2,1,0:T(8,128)(2,1)S(1)}, u32[]{:S(2)}, u32[]{:S(2)}) collective-permute-start(bf16[5,32,640]{2,1,0:T(8,128)(2,1)S(1)} %get-tuple-element.37), channel_id=1, source_target_pairs={{0,32},{32,0},{64,96},{96,64},{128,160},{160,128},{192,224},{224,1... | collective-permute-start | bytes 614408 | tf_op jit(solution)/shard_map/ppermute | solution.py:118
  20.7 21.6 %collective-permute-start = (bf16[5,32,640]{2,1,0:T(8,128)(2,1)S(1)}, bf16[5,32,640]{2,1,0:T(8,128)(2,1)}, u32[]{:S(2)}, u32[]{:S(2)}) collective-permute-start(bf16[5,32,640]{2,1,0:T(8,128)(2,1)S(1)} %get-tuple-element.38), channel_id=1, source_target_pairs={{0,68},{1,69},{2,70},{3,71},{4,0},{5,1},{6,2},{7,3},{8,76},{9,77},... | collective-permute-start | bytes 614408 | tf_op jit(solution)/shard_map/ppermute | solution.py:117
  28.2 22.3 %copy-start.6 = (f32[640]{0:T(1024)S(1)}, f32[640]{0:T(1024)}, u32[]{:S(2)}) copy-start(f32[640]{0:T(1024)} %param.11) | copy-start | bytes 7684
  32.0 14.3 %copy-start.5 = (bf16[5,32,640]{2,1,0:T(8,128)(2,1)}, bf16[5,32,640]{2,1,0:T(8,128)(2,1)S(1)}, u32[]{:S(2)}) copy-start(bf16[5,32,640]{2,1,0:T(8,128)(2,1)S(1)} %collective-permute-done.1) | copy-start | bytes 614404
  42.3 20.2 %collective-permute-start.3 = (bf16[40,1440]{1,0:T(8,128)(2,1)S(1)}, bf16[40,1440]{1,0:T(8,128)(2,1)S(1)}, u32[]{:S(2)}, u32[]{:S(2)}) collective-permute-start(bf16[40,1440]{1,0:T(8,128)(2,1)S(1)} %concatenate.26), channel_id=1, source_target_pairs={{128,0},{160,32},{192,64},{224,96},{0,128},{32,160},{64,192},{96,2... | collective-permute-start | bytes 345608 | tf_op jit(solution)/shard_map/ppermute | solution.py:90
  46.3 20.7 %all-to-all-start.1 = ((bf16[4,40,1440]{2,1,0:T(8,128)(2,1)}), bf16[4,40,1440]{2,1,0:T(8,128)(2,1)S(1)}, u32[]{:S(2)}, u32[]{:S(2)}) async-start(bf16[4,40,1440]{2,1,0:T(8,128)(2,1)} %broadcast_in_dim.39), calls=%async_computation.1 | async-start | bytes 983040 | tf_op jit(solution)/shard_map/all_to_all | solution.py:86
  50.8 23.3 %collective-permute-start.2 = (bf16[5,32,640]{2,1,0:T(8,128)(2,1)}, bf16[5,32,640]{2,1,0:T(8,128)(2,1)}, u32[]{:S(2)}, u32[]{:S(2)}) collective-permute-start(bf16[5,32,640]{2,1,0:T(8,128)(2,1)} %collective-permute-done), channel_id=1, source_target_pairs={{68,480},{69,481},{70,482},{71,483},{0,484},{1,485},{2,486},{3,487... | collective-permute-start | bytes 614408 | tf_op jit(solution)/shard_map/ppermute | solution.py:273
  62.5 11.5 %collective-permute-start.4 = (bf16[80,1440]{1,0:T(8,128)(2,1)S(1)}, bf16[80,1440]{1,0:T(8,128)(2,1)S(1)}, u32[]{:S(2)}, u32[]{:S(2)}) collective-permute-start(bf16[80,1440]{1,0:T(8,128)(2,1)S(1)} %pad_maximum_fusion.6), channel_id=1, source_target_pairs={{384,0},{416,32},{448,64},{480,96},{256,128},{288,160},{320,192},{... | collective-permute-start | bytes 691208 | tf_op jit(solution)/shard_map/ppermute | solution.py:91
  68.1 22.4 %copy-start = (bf16[1920,640]{1,0:T(8,128)(2,1)S(1)}, bf16[1920,640]{1,0:T(8,128)(2,1)}, u32[]{:S(2)}) copy-start(bf16[1920,640]{1,0:T(8,128)(2,1)} %kernel_ref) | copy-start | bytes 7372804
  74.1 20.2 %collective-permute-start.9 = (bf16[40,5760]{1,0:T(8,128)(2,1)}, bf16[40,5760]{1,0:T(8,128)(2,1)S(1)}, u32[]{:S(2)}, u32[]{:S(2)}) collective-permute-start(bf16[40,5760]{1,0:T(8,128)(2,1)} %concatenate.27), channel_id=1, source_target_pairs={{256,0},{288,32},{320,64},{352,96},{384,128},{416,160},{448,192},{... | collective-permute-start | bytes 1382408 | tf_op jit(solution)/shard_map/ppermute | solution.py:95
  77.0 23.1 %collective-permute-start.8 = (bf16[40,5760]{1,0:T(8,128)(2,1)}, bf16[40,5760]{1,0:T(8,128)(2,1)S(1)}, u32[]{:S(2)}, u32[]{:S(2)}) collective-permute-start(bf16[40,5760]{1,0:T(8,128)(2,1)} %concatenate.27), channel_id=1, source_target_pairs={{384,0},{416,32},{448,64},{480,96},{256,128},{288,160},{320,192},{... | collective-permute-start | bytes 1382408 | tf_op jit(solution)/shard_map/ppermute | solution.py:95
  79.7 22.9 %collective-permute-start.7 = (bf16[40,5760]{1,0:T(8,128)(2,1)}, bf16[40,5760]{1,0:T(8,128)(2,1)S(1)}, u32[]{:S(2)}, u32[]{:S(2)}) collective-permute-start(bf16[40,5760]{1,0:T(8,128)(2,1)} %concatenate.27), channel_id=1, source_target_pairs={{128,0},{160,32},{192,64},{224,96},{0,128},{32,160},{64,192},{96,2... | collective-permute-start | bytes 1382408 | tf_op jit(solution)/shard_map/ppermute | solution.py:95
  82.5 36.4 %collective-permute-start.12 = (bf16[160,1440]{1,0:T(8,128)(2,1)S(1)}, bf16[160,1440]{1,0:T(8,128)(2,1)S(1)}, u32[]{:S(2)}, u32[]{:S(2)}) collective-permute-start(bf16[160,1440]{1,0:T(8,128)(2,1)S(1)} %pad_maximum_fusion.2.h0), channel_id=1, source_target_pairs={{16,0},{17,1},{18,2},{19,3},{20,4},{21,5},{22,6},{23,7},{24,8},{25... | collective-permute-start | bytes 1382408 | tf_op jit(solution)/shard_map/ppermute | solution.py:99
  85.6 33.3 %collective-permute-start.11 = (bf16[160,1440]{1,0:T(8,128)(2,1)S(1)}, bf16[160,1440]{1,0:T(8,128)(2,1)S(1)}, u32[]{:S(2)}, u32[]{:S(2)}) collective-permute-start(bf16[160,1440]{1,0:T(8,128)(2,1)S(1)} %pad_maximum_fusion.2.h0), channel_id=1, source_target_pairs={{24,0},{25,1},{26,2},{27,3},{28,4},{29,5},{30,6},{31,7},{16,8},{17... | collective-permute-start | bytes 1382408 | tf_op jit(solution)/shard_map/ppermute | solution.py:99
  90.4 12.2 %copy-start.4 = (bf16[1,5,32,640]{3,2,1,0:T(8,128)(2,1)}, bf16[1,5,32,640]{3,2,1,0:T(8,128)(2,1)S(1)}, u32[]{:S(2)}) copy-start(bf16[1,5,32,640]{3,2,1,0:T(8,128)(2,1)S(1)} %get-tuple-element.44) | copy-start | bytes 614404
  92.8 1.4 copy-start.1
  94.3 24.6 %collective-permute-start.10 = (bf16[160,1440]{1,0:T(8,128)(2,1)S(1)}, bf16[160,1440]{1,0:T(8,128)(2,1)}, u32[]{:S(2)}, u32[]{:S(2)}) collective-permute-start(bf16[160,1440]{1,0:T(8,128)(2,1)S(1)} %pad_maximum_fusion.2.h0), channel_id=1, source_target_pairs={{8,0},{9,1},{10,2},{11,3},{12,4},{13,5},{14,6},{15,7},{0,8},{1,9},... | collective-permute-start | bytes 1382408 | tf_op jit(solution)/shard_map/ppermute | solution.py:99
  100.1 9.0 %collective-permute-start.6 = (bf16[6,1,32,640]{3,2,1,0:T(8,128)(2,1)S(1)}, bf16[6,1,32,640]{3,2,1,0:T(8,128)(2,1)}, u32[]{:S(2)}, u32[]{:S(2)}) collective-permute-start(bf16[6,1,32,640]{3,2,1,0:T(8,128)(2,1)S(1)} %get-tuple-element.35), channel_id=1, source_target_pairs={{1,0},{2,1},{3,2},{4,3},{5,4},{6,5},{7,6},{8,7},{9,8},{10,9},{11,1... | collective-permute-start | bytes 737288 | tf_op jit(solution)/shard_map/ppermute | solution.py:126
  102.6 28.7 %copy-start.7 = (f32[640]{0:T(1024)S(1)}, f32[640]{0:T(1024)}, u32[]{:S(2)}) copy-start(f32[640]{0:T(1024)} %param.13) | copy-start | bytes 7684
  102.6 16.3 %collective-permute-start.5 = (bf16[6,1,32,640]{3,2,1,0:T(8,128)(2,1)S(1)}, bf16[6,1,32,640]{3,2,1,0:T(8,128)(2,1)}, u32[]{:S(2)}, u32[]{:S(2)}) collective-permute-start(bf16[6,1,32,640]{3,2,1,0:T(8,128)(2,1)S(1)} %get-tuple-element.36), channel_id=1, source_target_pairs={{0,1},{1,2},{2,3},{3,4},{4,5},{5,6},{6,7},{7,8},{8,9},{9,10},{10,1... | collective-permute-start | bytes 737288 | tf_op jit(solution)/shard_map/ppermute | solution.py:125
  118.9 14.4 %collective-permute-start.13 = (bf16[160,5760]{1,0:T(8,128)(2,1)S(1)}, bf16[160,5760]{1,0:T(8,128)(2,1)}, u32[]{:S(2)}, u32[]{:S(2)}) collective-permute-start(bf16[160,5760]{1,0:T(8,128)(2,1)S(1)} %pad_maximum_fusion.low_any), channel_id=1, source_target_pairs={{0,32},{32,0},{64,96},{96,64},{128,160},{160,128},{192,224},{224,1... | collective-permute-start | bytes 5529608 | tf_op jit(solution)/shard_map/ppermute | solution.py:296
  122.4 10.9 %collective-permute-start.14 = (bf16[160,1440]{1,0:T(8,128)(2,1)S(1)}, bf16[160,1440]{1,0:T(8,128)(2,1)}, u32[]{:S(2)}, u32[]{:S(2)}) collective-permute-start(bf16[160,1440]{1,0:T(8,128)(2,1)S(1)} %pad_maximum_fusion.2.h0), channel_id=1, source_target_pairs={{0,32},{32,0},{64,96},{96,64},{128,160},{160,128},{192,224},{224,1... | collective-permute-start | bytes 1382408 | tf_op jit(solution)/shard_map/ppermute | solution.py:285
  124.3 9.0 %collective-permute-start.17 = (bf16[160,1440]{1,0:T(8,128)(2,1)S(1)}, bf16[160,1440]{1,0:T(8,128)(2,1)}, u32[]{:S(2)}, u32[]{:S(2)}) collective-permute-start(bf16[160,1440]{1,0:T(8,128)(2,1)S(1)} %collective-permute-done.12.h3), channel_id=1, source_target_pairs={{0,32},{32,0},{64,96},{96,64},{128,160},{160,128},{192,224},{224,1... | collective-permute-start | bytes 1382408 | tf_op jit(solution)/shard_map/ppermute | solution.py:293
  126.7 6.5 %collective-permute-start.16 = (bf16[160,1440]{1,0:T(8,128)(2,1)S(1)}, bf16[160,1440]{1,0:T(8,128)(2,1)}, u32[]{:S(2)}, u32[]{:S(2)}) collective-permute-start(bf16[160,1440]{1,0:T(8,128)(2,1)S(1)} %collective-permute-done.11.h2), channel_id=1, source_target_pairs={{0,32},{32,0},{64,96},{96,64},{128,160},{160,128},{192,224},{224,1... | collective-permute-start | bytes 1382408 | tf_op jit(solution)/shard_map/ppermute | solution.py:293
  128.7 4.6 %collective-permute-start.15 = (bf16[160,1440]{1,0:T(8,128)(2,1)}, bf16[160,1440]{1,0:T(8,128)(2,1)}, u32[]{:S(2)}, u32[]{:S(2)}) collective-permute-start(bf16[160,1440]{1,0:T(8,128)(2,1)} %collective-permute-done.10.h1), channel_id=1, source_target_pairs={{0,32},{32,0},{64,96},{96,64},{128,160},{160,128},{192,224},{224,1... | collective-permute-start | bytes 1382408 | tf_op jit(solution)/shard_map/ppermute | solution.py:293
  131.4 2.2 %copy-start.2 = (bf16[1920,640]{1,0:T(8,128)(2,1)S(1)}, bf16[1920,640]{1,0:T(8,128)(2,1)}, u32[]{:S(2)}) copy-start(bf16[1920,640]{1,0:T(8,128)(2,1)} %copy-done.1) | copy-start | bytes 7372804

commit v6 on v5

v6 whole, which is shorter than its diff:
```python
import functools

import jax
import jax.numpy as jnp
import numpy as np
from jax import lax
from jax.experimental import pallas as pl
from jax.experimental.pallas import tpu as pltpu
from jax.sharding import PartitionSpec as P

LONS = 16
FRAMES_AXIS = 32
Y = 4
X = 4
Z_LO = 8


def lon_index(y, z_hi, core):
    return y * 4 + z_hi * 2 + core


def frame_index(x, z_lo):
    return x * Z_LO + z_lo


def z_groups():
    return [
        [
            lon_index(y, z_hi, core) * FRAMES_AXIS + frame_index(x, z_lo)
            for z_hi in range(2)
            for z_lo in range(Z_LO)
        ]
        for x in range(X)
        for y in range(Y)
        for core in range(2)
    ]


def x_groups():
    return [[frame_index(x, z_lo) for x in range(X)] for z_lo in range(Z_LO)]


def across_y(k):
    return [((y ^ k) * 4 + r, y * 4 + r) for y in range(Y) for r in range(4)]


NEAR_FIRST = (0, 1, 3, 2)
CORES = [(i, i ^ 1) for i in range(LONS)]
FAR = [(i, (i + 1) % LONS if i % 2 else (i - 1) % LONS) for i in range(LONS)]


def copies(piece, count):
    return jnp.broadcast_to(piece[None], (count,) + piece.shape)


def gather_z(spatial_kernel):
    shard = spatial_kernel.T
    cols, rows = shard.shape
    along_z = lax.all_to_all(
        copies(shard, 16), ("lon", "frame"), 0, 0, axis_index_groups=z_groups()
    )
    along_z = along_z.reshape(2, Z_LO, cols, rows).transpose(0, 2, 1, 3)
    return along_z.reshape(2 * cols, Z_LO * rows)


def over_x(block):
    return lax.all_to_all(copies(block, X), "frame", 0, 0, axis_index_groups=x_groups())


def over_y(block):
    return [block] + [lax.ppermute(block, "lon", across_y(k)) for k in NEAR_FIRST[1:]]


def joined_x(along_x):
    return jnp.concatenate([along_x[x] for x in range(X)], axis=1)


def channel_order():
    lon = lax.axis_index("lon")
    blocks = [(k, side, z_hi) for k in NEAR_FIRST for side in range(2) for z_hi in range(2)]
    row, side, z_hi = (jnp.asarray(np.repeat(np.array(v), 40)) for v in zip(*blocks))
    within = jnp.asarray(np.tile(np.arange(40), LONS))
    return lon_index((lon // 4) ^ row, z_hi, (lon % 2) ^ side) * 40 + within


def lon_halos(columns):
    core = lax.axis_index("lon") % 2
    far = lax.ppermute(jnp.where(core == 1, columns[-1], columns[0]), "lon", FAR)
    near = lax.ppermute(jnp.where(core == 1, columns[0], columns[-1]), "lon", CORES)
    return far, near


def frame_halos(wide):
    up = [(i, i + 1) for i in range(FRAMES_AXIS - 1)]
    down = [(i + 1, i) for i in range(FRAMES_AXIS - 1)]
    earlier = lax.ppermute(wide[:, -1:], "frame", up)
    later = lax.ppermute(wide[:, :1], "frame", down)
    return earlier, later


VMEM = pl.BlockSpec(memory_space=pltpu.VMEM)
SMEM = pl.BlockSpec(memory_space=pltpu.SMEM)
ANY = pl.BlockSpec(memory_space=pl.ANY)


def params(mebibytes):
    return pltpu.CompilerParams(vmem_limit_bytes=mebibytes * 2**20)


def order_kernel(order_ref, kernel_ref, out_ref):
    channels = order_ref.shape[0]
    for k in range(3):
        part = slice(k * channels, (k + 1) * channels)
        moved = jnp.dot(order_ref[...], kernel_ref[part], preferred_element_type=jnp.float32)
        out_ref[part] = moved.astype(jnp.bfloat16)


def shift_rows(planes_ref, taps_ref, lat_rows):
    planes, rows, channels = planes_ref.shape
    row = lax.rem(lax.broadcasted_iota(jnp.int32, (rows, channels), 0), lat_rows)

    def plane(p, carry):
        here = planes_ref[p]
        wider = here.astype(jnp.float32)
        above = jnp.where(row == 0, 0.0, pltpu.roll(wider, 1, 0))
        below = jnp.where(row == lat_rows - 1, 0.0, pltpu.roll(wider, rows - 1, 0))
        taps_ref[0, p] = above.astype(jnp.bfloat16)
        taps_ref[1, p] = here
        taps_ref[2, p] = below.astype(jnp.bfloat16)
        return carry

    lax.fori_loop(0, planes, plane, 0)


def silu(v):
    return v * jax.nn.sigmoid(v)


def block_kernel(
    lat_rows, flags_ref, planes_any, w0, w1, w2, w3, w4, w5, w6, w7, kernel_any, bias_ref, tbias_ref,
    out_ref, planes_ref, weights_ref, kernel_ref, taps_ref, sems,
):
    pieces = (w0, w1, w2, w3, w4, w5, w6, w7)
    count = weights_ref.shape[0] // len(pieces)
    pairs = [(planes_any, planes_ref)]
    pairs += [(w, weights_ref.at[pl.ds(i * count, count)]) for i, w in enumerate(pieces)]
    pairs += [(kernel_any, kernel_ref)]
    moves = [
        pltpu.make_async_copy(source, target, sems.at[i])
        for i, (source, target) in enumerate(pairs)
    ]
    for move in moves:
        move.start()
    moves[0].wait()
    shift_rows(planes_ref, taps_ref, lat_rows)
    for move in moves[1:-1]:
        move.wait()

    planes, rows, channels = planes_ref.shape
    columns, inner = planes - 2, rows - 2 * lat_rows
    total = None
    for a in range(3):
        taps = [taps_ref[a, b : b + columns].reshape(columns * rows, channels) for b in range(3)]
        term = lax.dot_general(
            jnp.concatenate(taps, axis=1),
            weights_ref[:, 3 * a * channels : 3 * (a + 1) * channels],
            (((1,), (1,)), ((), ())),
            preferred_element_type=jnp.float32,
        )
        total = term if total is None else total + term
    active = silu(total + bias_ref[...])
    row = lax.rem(lax.broadcasted_iota(jnp.int32, active.shape, 0), rows)
    outside = (row < lat_rows) & (flags_ref[0] == 1)
    outside = outside | ((row >= rows - lat_rows) & (flags_ref[1] == 1))
    hidden = jnp.where(outside, 0.0, active).astype(jnp.bfloat16).reshape(columns, rows, channels)
    stacked = [
        hidden[:, k * lat_rows : k * lat_rows + inner].reshape(columns * inner, channels)
        for k in range(3)
    ]
    moves[-1].wait()
    mixed = jnp.dot(
        jnp.concatenate(stacked, axis=1), kernel_ref[...], preferred_element_type=jnp.float32
    )
    mixed = silu(mixed + tbias_ref[...]).reshape(columns, inner, channels)
    here = planes_ref[1 : planes - 1, lat_rows : lat_rows + inner].astype(jnp.float32)
    out_ref[...] = (here + mixed).astype(jnp.bfloat16)


def block(flags, planes, weights, kernel, bias, tbias, lat_rows):
    count, rows, channels = planes.shape
    inner = rows - 2 * lat_rows
    moved = (planes, *weights, kernel)
    joined = (len(weights) * weights[0].shape[0], weights[0].shape[1])
    shapes = (planes.shape, joined, kernel.shape, (3, *planes.shape))
    flops = (count - 2) * 2 * channels * channels * (9 * rows + 3 * inner)
    return pl.pallas_call(
        functools.partial(block_kernel, lat_rows),
        out_shape=jax.ShapeDtypeStruct((count - 2, inner, channels), jnp.bfloat16),
        in_specs=[SMEM] + [ANY] * len(moved) + [VMEM, VMEM],
        out_specs=VMEM,
        scratch_shapes=[pltpu.VMEM(s, jnp.bfloat16) for s in shapes]
        + [pltpu.SemaphoreType.DMA((len(moved),))],
        compiler_params=params(34),
        cost_estimate=pl.CostEstimate(flops=flops, bytes_accessed=2**24, transcendentals=0),
    )(flags, *moved, bias, tbias)


def reordered(order, kernel):
    return pl.pallas_call(
        order_kernel,
        out_shape=jax.ShapeDtypeStruct(kernel.shape, jnp.bfloat16),
        in_specs=[VMEM, VMEM],
        out_specs=VMEM,
        compiler_params=params(16),
        cost_estimate=pl.CostEstimate(
            flops=2 * 10**10, bytes_accessed=2**23, transcendentals=0
        ),
    )(order, kernel)


def body(latents, spatial_kernel, spatial_bias, temporal_kernel, temporal_bias):
    frames, lat_rows, lon_cols, channels = latents.shape
    core = lax.axis_index("lon") % 2
    columns = latents.transpose(2, 0, 1, 3)
    far, near = lon_halos(columns)
    along_z = gather_z(spatial_kernel)
    _, temporal_kernel = lax.optimization_barrier((along_z, temporal_kernel))
    order = channel_order()[:, None] == lax.broadcasted_iota(jnp.int32, (channels, channels), 1)
    bias = jnp.sum(jnp.where(order, spatial_bias[None, :], 0.0), axis=1)
    ordered = [
        jnp.dot(order.astype(jnp.bfloat16), temporal_kernel[k * channels : (k + 1) * channels])
        for k in range(3)
    ]
    ordered = jnp.concatenate(ordered, axis=0)
    mine = joined_x(over_x(along_z))
    pieces = over_y(mine)
    others = [lax.ppermute(mine, "lon", CORES)]
    far, near, columns, _ = lax.optimization_barrier((far, near, columns, mine))
    before = jnp.where(core == 1, near, far)
    after = jnp.where(core == 1, far, near)
    wide = jnp.concatenate([before[None], columns, after[None]], axis=0)
    earlier, later = frame_halos(wide)
    earlier, later, ordered, pieces[-1] = lax.optimization_barrier(
        (earlier, later, ordered, pieces[-1])
    )
    others += [lax.ppermute(piece, "lon", CORES) for piece in pieces[1:]]
    weights = [piece for pair in zip(pieces, others) for piece in pair]
    planes = jnp.concatenate([earlier, wide, later], axis=1)
    planes = planes.reshape(lon_cols + 2, (frames + 2) * lat_rows, channels)

    frame = lax.axis_index("frame")
    flags = jnp.stack([frame == 0, frame == FRAMES_AXIS - 1]).astype(jnp.int32)
    result = block(
        flags, planes, weights, ordered, bias[None], temporal_bias[None], lat_rows
    )
    return result.reshape(lon_cols, frames, lat_rows, channels).transpose(1, 2, 0, 3)


def solution(mesh):
    placed = (P("frame", None, "lon", None), P("frame", "lon"), P(), P(), P())
    return jax.shard_map(
        body, mesh=mesh, in_specs=placed, out_specs=P("frame", None, "lon", None), check_vma=False
    )
```

time: 153 us -> 141 us (0.922)
  the two profiles are of different devices: /device:TPU:7 before, /device:TPU:289 now
where the time goes in v6:
time: 141 us; the launch traced here: 140 us
  starting transfers between devices  53.8 us (38%)
  waiting for transfers between devices  48.7 us (35%)
  Pallas kernels  16.4 us (12%)
  matrix products  8.03 us (6%)
  local copies, waits for them, and re-layouts  7.8 us (6%)
  other arithmetic  4.58 us (3%)
    all_to_all x1, waiting for transfers between devices, gather_z(): lax.all_to_all(copies(shard, 16), ('lon', 'frame'), 0, 0, axis_index_grou...  20.8 us
    ppermute x3, waiting for transfers between devices, over_y(): lax.ppermute(block, 'lon', across_y(k))  18.2 us
    pallas_call x1, Pallas kernels, block(): pl.pallas_call(functools.partial(block_kernel, lat_rows), out_shape=jax.S...  16.4 us
    all_to_all x1, starting transfers between devices, gather_z(): lax.all_to_all(copies(shard, 16), ('lon', 'frame'), 0, 0, axis_index_grou...  11 us
    ppermute x3, starting transfers between devices, over_y(): lax.ppermute(block, 'lon', across_y(k))  9.66 us
    ppermute x3, starting transfers between devices, body(): others += [lax.ppermute(piece, 'lon', CORES) for piece in pieces[1:]]  9.09 us
    dot_general x3, matrix products, body(): jnp.dot(order.astype(jnp.bfloat16), temporal_kernel[k * channels:(k + 1)...  8.03 us
    all_to_all x1, waiting for transfers between devices, over_x(): lax.all_to_all(copies(block, X), 'frame', 0, 0, axis_index_groups=x_group...  7.82 us
  transfers between devices with their start and end apart: 13, of which 4 were waited for; matrix products, arithmetic and copies ran while one was open for 13% of the time, Pallas kernels for 0%

profile of v6, /device:TPU:289, one launch (start us, length us, event | category | flops | bytes accessed | tf_op | source)
XLA Modules:
  0.0 139.7 jit_solution(3006895751036083715)
XLA Ops:
  0.0 1.5 %broadcast_in_dim.39 = bf16[16,40,180]{2,1,0:T(8,128)(2,1)} broadcast(bf16[40,180]{1,0:T(8,128)(2,1)} %bitcast.38), dimensions={1,2} | broadcast | bytes 244800 | tf_op jit(solution)/shard_map/broadcast_in_dim | solution.py:53
  1.5 11.0 %all-to-all-start = ((bf16[16,40,180]{2,1,0:T(8,128)(2,1)}), bf16[16,40,180]{2,1,0:T(8,128)(2,1)S(1)}, u32[]{:S(2)}, u32[]{:S(2)}) async-start(bf16[16,40,180]{2,1,0:T(8,128)(2,1)} %broadcast_in_dim.39), calls=%async_computation | async-start | bytes 655360 | tf_op jit(solution)/shard_map/all_to_all | solution.py:59
  12.5 1.2 copy.26
  13.7 0.0 copy-start
  13.7 0.9 select_bitcast_fusion.2
  14.6 3.1 %collective-permute-start.1 = (bf16[5,32,640]{2,1,0:T(8,128)(2,1)}, bf16[5,32,640]{2,1,0:T(8,128)(2,1)}, u32[]{:S(2)}, u32[]{:S(2)}) collective-permute-start(bf16[5,32,640]{2,1,0:T(8,128)(2,1)} %get-tuple-element.25), channel_id=1, source_target_pairs={{0,32},{32,0},{64,96},{96,64},{128,160},{160,128},{192,224},{224,1... | collective-permute-start | bytes 614408 | tf_op jit(solution)/shard_map/ppermute | solution.py:89
  17.7 4.0 %collective-permute-start = (bf16[5,32,640]{2,1,0:T(8,128)(2,1)}, bf16[5,32,640]{2,1,0:T(8,128)(2,1)}, u32[]{:S(2)}, u32[]{:S(2)}) collective-permute-start(bf16[5,32,640]{2,1,0:T(8,128)(2,1)} %get-tuple-element.26), channel_id=1, source_target_pairs={{0,480},{32,64},{64,32},{96,128},{128,96},{160,192},{192,160},{224... | collective-permute-start | bytes 614408 | tf_op jit(solution)/shard_map/ppermute | solution.py:88
  21.8 20.8 %all-to-all-done = bf16[16,40,180]{2,1,0:T(8,128)(2,1)S(1)} async-done(((bf16[16,40,180]{2,1,0:T(8,128)(2,1)}), bf16[16,40,180]{2,1,0:T(8,128)(2,1)S(1)}, u32[]{:S(2)}, u32[]{:S(2)}) %all-to-all-start) | async-done | bytes 230432 | tf_op jit(solution)/shard_map/all_to_all | solution.py:59
  42.6 0.1 copy.21
  42.7 0.3 broadcast_in_dim.40
  43.0 0.0 copy-start.9
  43.0 0.0 copy-start.10
  43.0 0.0 copy-start.11
  43.0 0.0 copy-start.12
  43.0 1.0 broadcast_in_dim.41
  44.1 4.0 %all-to-all-start.1 = ((bf16[4,80,1440]{2,1,0:T(8,128)(2,1)}), bf16[4,80,1440]{2,1,0:T(8,128)(2,1)S(1)}, u32[]{:S(2)}, u32[]{:S(2)}) async-start(bf16[4,80,1440]{2,1,0:T(8,128)(2,1)} %broadcast_in_dim.41), calls=%async_computation.1 | async-start | bytes 1966080 | tf_op jit(solution)/shard_map/all_to_all | solution.py:67
  48.1 3.0 %fusion = bf16[640,640]{1,0:T(8,128)(2,1)} fusion(bf16[1920,640]{1,0:T(8,128)(2,1)} %param.12, s32[640]{0:T(1024)S(1)} %multiply_add_fusion), kind=kOutput, calls=%fused_computation.4 | convolution fusion | flops 524697600 | bytes 1640960 | tf_op jit(solution)/shard_map/dot_general | solution.py:231
  51.1 3.0 %fusion.1 = bf16[640,640]{1,0:T(8,128)(2,1)} fusion(bf16[1920,640]{1,0:T(8,128)(2,1)} %param.12, s32[640]{0:T(1024)S(1)} %multiply_add_fusion), kind=kOutput, calls=%fused_computation.5 | convolution fusion | flops 524697600 | bytes 1640960 | tf_op jit(solution)/shard_map/dot_general | solution.py:231
  54.1 7.8 %all-to-all-done.1 = bf16[4,80,1440]{2,1,0:T(8,128)(2,1)S(1)} async-done(((bf16[4,80,1440]{2,1,0:T(8,128)(2,1)}), bf16[4,80,1440]{2,1,0:T(8,128)(2,1)S(1)}, u32[]{:S(2)}, u32[]{:S(2)}) %all-to-all-start.1) | async-done | bytes 921632 | tf_op jit(solution)/shard_map/all_to_all | solution.py:67
  61.9 0.8 slice_bitcast_fusion
  62.7 1.5 %concatenate.12.w0 = bf16[80,5760]{1,0:T(8,128)(2,1)S(1)} concatenate(bf16[80,1440]{1,0:T(8,128)(2,1)} %get-tuple-element.24, bf16[80,1440]{1,0:T(8,128)(2,1)S(1)} %get-tuple-element.23, bf16[80,1440]{1,0:T(8,128)(2,1)S(1)} %get-tuple-element.22, bf16[80,1440]{1,0:T(8,128)(2,1)S(1)} %get-tuple-element.21), dimensions={1} | concatenate | bytes 1843200 | tf_op jit(solution)/shard_map/concatenate | solution.py:75
  64.2 4.6 %collective-permute-start.8 = (bf16[80,5760]{1,0:T(8,128)(2,1)S(1)}, bf16[80,5760]{1,0:T(8,128)(2,1)}, u32[]{:S(2)}, u32[]{:S(2)}) collective-permute-start(bf16[80,5760]{1,0:T(8,128)(2,1)S(1)} %concatenate.12.w0), channel_id=1, source_target_pairs={{384,0},{416,32},{448,64},{480,96},{256,128},{288,160},{320,192},{... | collective-permute-start | bytes 2764808 | tf_op jit(solution)/shard_map/ppermute | solution.py:71
  68.9 1.9 %collective-permute-start.6 = (bf16[80,5760]{1,0:T(8,128)(2,1)S(1)}, bf16[80,5760]{1,0:T(8,128)(2,1)}, u32[]{:S(2)}, u32[]{:S(2)}) collective-permute-start(bf16[80,5760]{1,0:T(8,128)(2,1)S(1)} %concatenate.12.w0), channel_id=1, source_target_pairs={{128,0},{160,32},{192,64},{224,96},{0,128},{32,160},{64,192},{96,2... | collective-permute-start | bytes 2764808 | tf_op jit(solution)/shard_map/ppermute | solution.py:71
  70.8 3.1 %collective-permute-start.4 = (bf16[80,5760]{1,0:T(8,128)(2,1)S(1)}, bf16[80,5760]{1,0:T(8,128)(2,1)}, u32[]{:S(2)}, u32[]{:S(2)}) collective-permute-start(bf16[80,5760]{1,0:T(8,128)(2,1)S(1)} %concatenate.12.w0), channel_id=1, source_target_pairs={{256,0},{288,32},{320,64},{352,96},{384,128},{416,160},{448,192},{... | collective-permute-start | bytes 2764808 | tf_op jit(solution)/shard_map/ppermute | solution.py:71
  73.9 2.1 %fusion.2 = bf16[640,640]{1,0:T(8,128)(2,1)S(1)} fusion(bf16[1920,640]{1,0:T(8,128)(2,1)} %param.12, s32[640]{0:T(1024)S(1)} %multiply_add_fusion), kind=kOutput, calls=%fused_computation.6 | convolution fusion | flops 524697600 | bytes 1640960 | tf_op jit(solution)/shard_map/dot_general | solution.py:231
  76.0 0.0 collective-permute-done.1
  76.0 1.2 select_bitcast_fusion.1
  77.2 0.1 pad_maximum_fusion.2
  77.3 1.9 %collective-permute-start.3 = (bf16[6,1,32,640]{3,2,1,0:T(8,128)(2,1)S(1)}, bf16[6,1,32,640]{3,2,1,0:T(8,128)(2,1)S(1)}, u32[]{:S(2)}, u32[]{:S(2)}) collective-permute-start(bf16[6,1,32,640]{3,2,1,0:T(8,128)(2,1)S(1)} %get-tuple-element.19), channel_id=1, source_target_pairs={{1,0},{2,1},{3,2},{4,3},{5,4},{6,5},{7,6},{8,7},{9,8},{10,9},{11,1... | collective-permute-start | bytes 737288 | tf_op jit(solution)/shard_map/ppermute | solution.py:97
  79.3 0.0 copy-start.8
  79.3 0.0 copy-start.7
  79.3 3.4 %collective-permute-start.2 = (bf16[6,1,32,640]{3,2,1,0:T(8,128)(2,1)S(1)}, bf16[6,1,32,640]{3,2,1,0:T(8,128)(2,1)S(1)}, u32[]{:S(2)}, u32[]{:S(2)}) collective-permute-start(bf16[6,1,32,640]{3,2,1,0:T(8,128)(2,1)S(1)} %get-tuple-element.20), channel_id=1, source_target_pairs={{0,1},{1,2},{2,3},{3,4},{4,5},{5,6},{6,7},{7,8},{8,9},{9,10},{10,1... | collective-permute-start | bytes 737288 | tf_op jit(solution)/shard_map/ppermute | solution.py:96
  82.7 0.2 pad_maximum_fusion.kernel_any
  82.9 1.8 %collective-permute-done.3 = bf16[6,1,32,640]{3,2,1,0:T(8,128)(2,1)S(1)} collective-permute-done((bf16[6,1,32,640]{3,2,1,0:T(8,128)(2,1)S(1)}, bf16[6,1,32,640]{3,2,1,0:T(8,128)(2,1)S(1)}, u32[]{:S(2)}, u32[]{:S(2)}) %collective-permute-start.3) | collective-permute-done | bytes 245792 | tf_op jit(solution)/shard_map/ppermute | solution.py:97
  84.7 7.6 %collective-permute-start.5 = (bf16[80,5760]{1,0:T(8,128)(2,1)S(1)}, bf16[80,5760]{1,0:T(8,128)(2,1)}, u32[]{:S(2)}, u32[]{:S(2)}) collective-permute-start(bf16[80,5760]{1,0:T(8,128)(2,1)S(1)} %concatenate.12.w0), channel_id=1, source_target_pairs={{0,32},{32,0},{64,96},{96,64},{128,160},{160,128},{192,224},{224,1... | collective-permute-start | bytes 2764808 | tf_op jit(solution)/shard_map/ppermute | solution.py:237
  92.3 0.0 collective-permute-done.2
  92.3 18.2 %collective-permute-done.4.w6 = bf16[80,5760]{1,0:T(8,128)(2,1)} collective-permute-done((bf16[80,5760]{1,0:T(8,128)(2,1)S(1)}, bf16[80,5760]{1,0:T(8,128)(2,1)}, u32[]{:S(2)}, u32[]{:S(2)}) %collective-permute-start.4) | collective-permute-done | bytes 921632 | tf_op jit(solution)/shard_map/ppermute | solution.py:71
  110.5 0.0 collective-permute-done.8.w4
  110.5 4.6 %collective-permute-start.9 = (bf16[80,5760]{1,0:T(8,128)(2,1)}, bf16[80,5760]{1,0:T(8,128)(2,1)}, u32[]{:S(2)}, u32[]{:S(2)}) collective-permute-start(bf16[80,5760]{1,0:T(8,128)(2,1)} %collective-permute-done.8.w4), channel_id=1, source_target_pairs={{0,32},{32,0},{64,96},{96,64},{128,160},{160,128},{192,224},{224,1... | collective-permute-start | bytes 2764808 | tf_op jit(solution)/shard_map/ppermute | solution.py:246
  115.1 1.9 %collective-permute-start.7 = (bf16[80,5760]{1,0:T(8,128)(2,1)}, bf16[80,5760]{1,0:T(8,128)(2,1)}, u32[]{:S(2)}, u32[]{:S(2)}) collective-permute-start(bf16[80,5760]{1,0:T(8,128)(2,1)} %collective-permute-done.6.w2), channel_id=1, source_target_pairs={{0,32},{32,0},{64,96},{96,64},{128,160},{160,128},{192,224},{224,1... | collective-permute-start | bytes 2764808 | tf_op jit(solution)/shard_map/ppermute | solution.py:246
  117.1 2.6 %collective-permute-start.10 = (bf16[80,5760]{1,0:T(8,128)(2,1)}, bf16[80,5760]{1,0:T(8,128)(2,1)}, u32[]{:S(2)}, u32[]{:S(2)}) collective-permute-start(bf16[80,5760]{1,0:T(8,128)(2,1)} %collective-permute-done.4.w6), channel_id=1, source_target_pairs={{0,32},{32,0},{64,96},{96,64},{128,160},{160,128},{192,224},{224,1... | collective-permute-start | bytes 2764808 | tf_op jit(solution)/shard_map/ppermute | solution.py:246
  119.7 0.3 select_reduce_fusion
  120.0 0.1 add_convert_fusion.flags_ref
  120.1 1.8 %pad_maximum_fusion.1 = bf16[6,7,32,640]{3,2,1,0:T(8,128)(2,1)S(1)} fusion(bf16[6,1,32,640]{3,2,1,0:T(8,128)(2,1)} %copy-done.5, bf16[1,5,32,640]{3,2,1,0:T(8,128)(2,1)} %copy-done.2, bf16[4,5,32,640]{3,2,1,0:T(8,128)(2,1)} %bitcast.36, bf16[1,5,32,640]{3,2,1,0:T(8,128)(2,1)} %copy-done.1, bf16[6,1,32,640]{3,2,1,0:T(8,128)(2,1)} %copy-done.6), kind=kLoop, calls=%fused_computation.1 | loop fusion | flops 3440640 | bytes 3440640 | tf_op jit(solution)/shard_map/concatenate | solution.py:248
  121.9 0.0 collective-permute-done.9.w5
  122.0 0.0 collective-permute-done.7.w3
  122.0 16.4 %shard_map.91 = bf16[4,160,640]{2,1,0:T(8,128)(2,1)S(1)} custom-call(s32[2]{0:T(128)S(1)} %add_convert_fusion.flags_ref, bf16[6,224,640]{2,1,0:T(8,128)(2,1)S(1)} %bitcast.32, bf16[80,5760]{1,0:T(8,128)(2,1)S(1)} %concatenate.12.w0, bf16[80,5760]{1,0:T(8,128)(2,1)} %collective-permute-done.5.w1, bf16[80,5760]{1,0:T(8,128)(2,1)} %collective-permute-done.6.w2, ...), custom_call_target="tpu_custom_call" | custom-call | flops 8178892800 | bytes 16777216 | tf_op jit(solution)/shard_map/pallas_call | solution.py:196
  138.4 1.3 copy.25
  (26 shorter events, 0.1 us)
Async XLA Ops:
  1.5 41.1 %all-to-all-start = ((bf16[16,40,180]{2,1,0:T(8,128)(2,1)}), bf16[16,40,180]{2,1,0:T(8,128)(2,1)S(1)}, u32[]{:S(2)}, u32[]{:S(2)}) async-start(bf16[16,40,180]{2,1,0:T(8,128)(2,1)} %broadcast_in_dim.39), calls=%async_computation | async-start | bytes 655360 | tf_op jit(solution)/shard_map/all_to_all | solution.py:59
  13.7 63.5 %copy-start = (bf16[5,32,4,640]{3,1,0,2:T(8,128)(2,1)}, bf16[5,32,4,640]{3,1,0,2:T(8,128)(2,1)S(1)}, u32[]{:S(2)}) copy-start(bf16[5,32,4,640]{3,1,0,2:T(8,128)(2,1)S(1)} %copy.26) | copy-start | bytes 2457604
  14.6 61.4 %collective-permute-start.1 = (bf16[5,32,640]{2,1,0:T(8,128)(2,1)}, bf16[5,32,640]{2,1,0:T(8,128)(2,1)}, u32[]{:S(2)}, u32[]{:S(2)}) collective-permute-start(bf16[5,32,640]{2,1,0:T(8,128)(2,1)} %get-tuple-element.25), channel_id=1, source_target_pairs={{0,32},{32,0},{64,96},{96,64},{128,160},{160,128},{192,224},{224,1... | collective-permute-start | bytes 614408 | tf_op jit(solution)/shard_map/ppermute | solution.py:89
  17.7 58.3 %collective-permute-start = (bf16[5,32,640]{2,1,0:T(8,128)(2,1)}, bf16[5,32,640]{2,1,0:T(8,128)(2,1)}, u32[]{:S(2)}, u32[]{:S(2)}) collective-permute-start(bf16[5,32,640]{2,1,0:T(8,128)(2,1)} %get-tuple-element.26), channel_id=1, source_target_pairs={{0,480},{32,64},{64,32},{96,128},{128,96},{160,192},{192,160},{224... | collective-permute-start | bytes 614408 | tf_op jit(solution)/shard_map/ppermute | solution.py:88
  43.0 5.1 %copy-start.9 = (s32[640]{0:T(1024)S(1)}, s32[640]{0:T(1024)}, u32[]{:S(2)}) copy-start(s32[640]{0:T(1024)} %constant.64) | copy-start | bytes 7684
  43.0 5.1 %copy-start.10 = (s32[640]{0:T(1024)S(1)}, s32[640]{0:T(1024)}, u32[]{:S(2)}) copy-start(s32[640]{0:T(1024)} %constant.61.clone) | copy-start | bytes 7684
  43.0 5.1 %copy-start.11 = (s32[640]{0:T(1024)S(1)}, s32[640]{0:T(1024)}, u32[]{:S(2)}) copy-start(s32[640]{0:T(1024)} %constant.59.clone) | copy-start | bytes 7684
  43.0 5.1 %copy-start.12 = (s32[640]{0:T(1024)S(1)}, s32[640]{0:T(1024)}, u32[]{:S(2)}) copy-start(s32[640]{0:T(1024)} %constant.58.clone) | copy-start | bytes 7684
  44.1 17.8 %all-to-all-start.1 = ((bf16[4,80,1440]{2,1,0:T(8,128)(2,1)}), bf16[4,80,1440]{2,1,0:T(8,128)(2,1)S(1)}, u32[]{:S(2)}, u32[]{:S(2)}) async-start(bf16[4,80,1440]{2,1,0:T(8,128)(2,1)} %broadcast_in_dim.41), calls=%async_computation.1 | async-start | bytes 1966080 | tf_op jit(solution)/shard_map/all_to_all | solution.py:67
  64.2 46.3 %collective-permute-start.8 = (bf16[80,5760]{1,0:T(8,128)(2,1)S(1)}, bf16[80,5760]{1,0:T(8,128)(2,1)}, u32[]{:S(2)}, u32[]{:S(2)}) collective-permute-start(bf16[80,5760]{1,0:T(8,128)(2,1)S(1)} %concatenate.12.w0), channel_id=1, source_target_pairs={{384,0},{416,32},{448,64},{480,96},{256,128},{288,160},{320,192},{... | collective-permute-start | bytes 2764808 | tf_op jit(solution)/shard_map/ppermute | solution.py:71
  68.9 46.2 %collective-permute-start.6 = (bf16[80,5760]{1,0:T(8,128)(2,1)S(1)}, bf16[80,5760]{1,0:T(8,128)(2,1)}, u32[]{:S(2)}, u32[]{:S(2)}) collective-permute-start(bf16[80,5760]{1,0:T(8,128)(2,1)S(1)} %concatenate.12.w0), channel_id=1, source_target_pairs={{128,0},{160,32},{192,64},{224,96},{0,128},{32,160},{64,192},{96,2... | collective-permute-start | bytes 2764808 | tf_op jit(solution)/shard_map/ppermute | solution.py:71
  70.8 39.7 %collective-permute-start.4 = (bf16[80,5760]{1,0:T(8,128)(2,1)S(1)}, bf16[80,5760]{1,0:T(8,128)(2,1)}, u32[]{:S(2)}, u32[]{:S(2)}) collective-permute-start(bf16[80,5760]{1,0:T(8,128)(2,1)S(1)} %concatenate.12.w0), channel_id=1, source_target_pairs={{256,0},{288,32},{320,64},{352,96},{384,128},{416,160},{448,192},{... | collective-permute-start | bytes 2764808 | tf_op jit(solution)/shard_map/ppermute | solution.py:71
  76.0 6.7 %copy-start.3 = (bf16[640,640]{1,0:T(8,128)(2,1)S(1)}, bf16[640,640]{1,0:T(8,128)(2,1)}, u32[]{:S(2)}) copy-start(bf16[640,640]{1,0:T(8,128)(2,1)} %fusion) | copy-start | bytes 2457604
  76.0 6.7 %copy-start.4 = (bf16[640,640]{1,0:T(8,128)(2,1)S(1)}, bf16[640,640]{1,0:T(8,128)(2,1)}, u32[]{:S(2)}) copy-start(bf16[640,640]{1,0:T(8,128)(2,1)} %fusion.1) | copy-start | bytes 2457604
  77.2 2.0 %copy-start.1 = (bf16[1,5,32,640]{3,2,1,0:T(8,128)(2,1)}, bf16[1,5,32,640]{3,2,1,0:T(8,128)(2,1)S(1)}, u32[]{:S(2)}) copy-start(bf16[1,5,32,640]{3,2,1,0:T(8,128)(2,1)S(1)} %get-tuple-element.27) | copy-start | bytes 614404
  77.2 2.0 %copy-start.2 = (bf16[1,5,32,640]{3,2,1,0:T(8,128)(2,1)}, bf16[1,5,32,640]{3,2,1,0:T(8,128)(2,1)S(1)}, u32[]{:S(2)}) copy-start(bf16[1,5,32,640]{3,2,1,0:T(8,128)(2,1)S(1)} %get-tuple-element.28) | copy-start | bytes 614404
  77.3 7.3 %collective-permute-start.3 = (bf16[6,1,32,640]{3,2,1,0:T(8,128)(2,1)S(1)}, bf16[6,1,32,640]{3,2,1,0:T(8,128)(2,1)S(1)}, u32[]{:S(2)}, u32[]{:S(2)}) collective-permute-start(bf16[6,1,32,640]{3,2,1,0:T(8,128)(2,1)S(1)} %get-tuple-element.19), channel_id=1, source_target_pairs={{1,0},{2,1},{3,2},{4,3},{5,4},{6,5},{7,6},{8,7},{9,8},{10,9},{11,1... | collective-permute-start | bytes 737288 | tf_op jit(solution)/shard_map/ppermute | solution.py:97
  79.3 40.4 %copy-start.8 = (f32[640]{0:T(1024)S(1)}, f32[640]{0:T(1024)}, u32[]{:S(2)}) copy-start(f32[640]{0:T(1024)} %param.13) | copy-start | bytes 7684
  79.3 40.4 %copy-start.7 = (f32[640]{0:T(1024)S(1)}, f32[640]{0:T(1024)}, u32[]{:S(2)}) copy-start(f32[640]{0:T(1024)} %param.11) | copy-start | bytes 7684
  79.3 13.0 %collective-permute-start.2 = (bf16[6,1,32,640]{3,2,1,0:T(8,128)(2,1)S(1)}, bf16[6,1,32,640]{3,2,1,0:T(8,128)(2,1)S(1)}, u32[]{:S(2)}, u32[]{:S(2)}) collective-permute-start(bf16[6,1,32,640]{3,2,1,0:T(8,128)(2,1)S(1)} %get-tuple-element.20), channel_id=1, source_target_pairs={{0,1},{1,2},{2,3},{3,4},{4,5},{5,6},{6,7},{7,8},{8,9},{9,10},{10,1... | collective-permute-start | bytes 737288 | tf_op jit(solution)/shard_map/ppermute | solution.py:96
  84.7 30.5 %copy-start.5 = (bf16[6,1,32,640]{3,2,1,0:T(8,128)(2,1)}, bf16[6,1,32,640]{3,2,1,0:T(8,128)(2,1)S(1)}, u32[]{:S(2)}) copy-start(bf16[6,1,32,640]{3,2,1,0:T(8,128)(2,1)S(1)} %collective-permute-done.3) | copy-start | bytes 737284
  84.7 37.3 %collective-permute-start.5 = (bf16[80,5760]{1,0:T(8,128)(2,1)S(1)}, bf16[80,5760]{1,0:T(8,128)(2,1)}, u32[]{:S(2)}, u32[]{:S(2)}) collective-permute-start(bf16[80,5760]{1,0:T(8,128)(2,1)S(1)} %concatenate.12.w0), channel_id=1, source_target_pairs={{0,32},{32,0},{64,96},{96,64},{128,160},{160,128},{192,224},{224,1... | collective-permute-start | bytes 2764808 | tf_op jit(solution)/shard_map/ppermute | solution.py:237
  92.3 24.8 %copy-start.6 = (bf16[6,1,32,640]{3,2,1,0:T(8,128)(2,1)}, bf16[6,1,32,640]{3,2,1,0:T(8,128)(2,1)S(1)}, u32[]{:S(2)}) copy-start(bf16[6,1,32,640]{3,2,1,0:T(8,128)(2,1)S(1)} %collective-permute-done.2) | copy-start | bytes 737284
  110.5 11.4 %collective-permute-start.9 = (bf16[80,5760]{1,0:T(8,128)(2,1)}, bf16[80,5760]{1,0:T(8,128)(2,1)}, u32[]{:S(2)}, u32[]{:S(2)}) collective-permute-start(bf16[80,5760]{1,0:T(8,128)(2,1)} %collective-permute-done.8.w4), channel_id=1, source_target_pairs={{0,32},{32,0},{64,96},{96,64},{128,160},{160,128},{192,224},{224,1... | collective-permute-start | bytes 2764808 | tf_op jit(solution)/shard_map/ppermute | solution.py:246
  115.1 6.8 %collective-permute-start.7 = (bf16[80,5760]{1,0:T(8,128)(2,1)}, bf16[80,5760]{1,0:T(8,128)(2,1)}, u32[]{:S(2)}, u32[]{:S(2)}) collective-permute-start(bf16[80,5760]{1,0:T(8,128)(2,1)} %collective-permute-done.6.w2), channel_id=1, source_target_pairs={{0,32},{32,0},{64,96},{96,64},{128,160},{160,128},{192,224},{224,1... | collective-permute-start | bytes 2764808 | tf_op jit(solution)/shard_map/ppermute | solution.py:246
  117.1 4.9 %collective-permute-start.10 = (bf16[80,5760]{1,0:T(8,128)(2,1)}, bf16[80,5760]{1,0:T(8,128)(2,1)}, u32[]{:S(2)}, u32[]{:S(2)}) collective-permute-start(bf16[80,5760]{1,0:T(8,128)(2,1)} %collective-permute-done.4.w6), channel_id=1, source_target_pairs={{0,32},{32,0},{64,96},{96,64},{128,160},{160,128},{192,224},{224,1... | collective-permute-start | bytes 2764808 | tf_op jit(solution)/shard_map/ppermute | solution.py:246

commit v7 on v6

--- a/solution.py
+++ b/solution.py
@@ -44,7 +44,7 @@
     return [((y ^ k) * 4 + r, y * 4 + r) for y in range(Y) for r in range(4)]
 
 
-NEAR_FIRST = (0, 1, 3, 2)
+NEAR_FIRST = (0, 2, 1, 3)
 CORES = [(i, i ^ 1) for i in range(LONS)]
 FAR = [(i, (i + 1) % LONS if i % 2 else (i - 1) % LONS) for i in range(LONS)]
 
@@ -105,14 +105,6 @@
 
 def params(mebibytes):
     return pltpu.CompilerParams(vmem_limit_bytes=mebibytes * 2**20)
-
-
-def order_kernel(order_ref, kernel_ref, out_ref):
-    channels = order_ref.shape[0]
-    for k in range(3):
-        part = slice(k * channels, (k + 1) * channels)
-        moved = jnp.dot(order_ref[...], kernel_ref[part], preferred_element_type=jnp.float32)
-        out_ref[part] = moved.astype(jnp.bfloat16)
 
 
 def shift_rows(planes_ref, taps_ref, lat_rows):
@@ -142,8 +134,16 @@
 ):
     pieces = (w0, w1, w2, w3, w4, w5, w6, w7)
     count = weights_ref.shape[0] // len(pieces)
+    third = weights_ref.shape[1] // 3
     pairs = [(planes_any, planes_ref)]
-    pairs += [(w, weights_ref.at[pl.ds(i * count, count)]) for i, w in enumerate(pieces)]
+    pairs += [
+        (
+            w.at[:, pl.ds(a * third, third)],
+            weights_ref.at[pl.ds(i * count, count), pl.ds(a * third, third)],
+        )
+        for a in range(3)
+        for i, w in enumerate(pieces)
+    ]
     pairs += [(kernel_any, kernel_ref)]
     moves = [
         pltpu.make_async_copy(source, target, sems.at[i])
@@ -153,13 +153,13 @@
         move.start()
     moves[0].wait()
     shift_rows(planes_ref, taps_ref, lat_rows)
-    for move in moves[1:-1]:
-        move.wait()
 
     planes, rows, channels = planes_ref.shape
     columns, inner = planes - 2, rows - 2 * lat_rows
     total = None
     for a in range(3):
+        for move in moves[1 + a * len(pieces) : 1 + (a + 1) * len(pieces)]:
+            move.wait()
         taps = [taps_ref[a, b : b + columns].reshape(columns * rows, channels) for b in range(3)]
         term = lax.dot_general(
             jnp.concatenate(taps, axis=1),
@@ -199,23 +199,10 @@
         in_specs=[SMEM] + [ANY] * len(moved) + [VMEM, VMEM],
         out_specs=VMEM,
         scratch_shapes=[pltpu.VMEM(s, jnp.bfloat16) for s in shapes]
-        + [pltpu.SemaphoreType.DMA((len(moved),))],
+        + [pltpu.SemaphoreType.DMA((3 * len(weights) + 2,))],
         compiler_params=params(34),
         cost_estimate=pl.CostEstimate(flops=flops, bytes_accessed=2**24, transcendentals=0),
     )(flags, *moved, bias, tbias)
-
-
-def reordered(order, kernel):
-    return pl.pallas_call(
-        order_kernel,
-        out_shape=jax.ShapeDtypeStruct(kernel.shape, jnp.bfloat16),
-        in_specs=[VMEM, VMEM],
-        out_specs=VMEM,
-        compiler_params=params(16),
-        cost_estimate=pl.CostEstimate(
-            flops=2 * 10**10, bytes_accessed=2**23, transcendentals=0
-        ),
-    )(order, kernel)
 
 
 def body(latents, spatial_kernel, spatial_bias, temporal_kernel, temporal_bias):
@@ -240,12 +227,10 @@
     after = jnp.where(core == 1, far, near)
     wide = jnp.concatenate([before[None], columns, after[None]], axis=0)
     earlier, later = frame_halos(wide)
-    earlier, later, ordered, pieces[-1] = lax.optimization_barrier(
-        (earlier, later, ordered, pieces[-1])
-    )
+    planes = jnp.concatenate([earlier, wide, later], axis=1)
+    planes, ordered, pieces[3] = lax.optimization_barrier((planes, ordered, pieces[3]))
     others += [lax.ppermute(piece, "lon", CORES) for piece in pieces[1:]]
     weights = [piece for pair in zip(pieces, others) for piece in pair]
-    planes = jnp.concatenate([earlier, wide, later], axis=1)
     planes = planes.reshape(lon_cols + 2, (frames + 2) * lat_rows, channels)
 
     frame = lax.axis_index("frame")

time: 141 us -> 146 us (1.035)
  waiting for transfers between devices: 48.7 us -> 55.6 us
  starting transfers between devices: 53.8 us -> 51.6 us
  local copies, waits for them, and re-layouts: 7.8 us -> 9.42 us
    ppermute x3, waiting for transfers between devices: 18.2 us -> 23.6 us  [over_y(): lax.ppermute(block, 'lon', across_y(k))]
    ppermute x1, starting transfers between devices: 7.59 us -> 4.96 us  [body(): others = [lax.ppermute(mine, 'lon', CORES)]]
    ppermute x3, waiting for transfers between devices: 0.01 us -> 1.76 us  [body(): others += [lax.ppermute(piece, 'lon', CORES) for piece in pieces[1:]]]
    ppermute x1, waiting for transfers between devices: 1.76 us -> 0.01 us  [frame_halos(): later = lax.ppermute(wide[:, :1], 'frame', down)]
    ppermute x1, waiting for transfers between devices: 0.01 us -> 1.62 us  [frame_halos(): earlier = lax.ppermute(wide[:, -1:], 'frame', up)]
    ppermute x1, starting transfers between devices: 1.92 us -> 3.5 us  [frame_halos(): later = lax.ppermute(wide[:, :1], 'frame', down)]
  transfers between devices with their start and end apart: 13 -> 13, of which waited for: 4 -> 5; matrix products, arithmetic and copies ran while one was open for 13% -> 12% of each run, Pallas kernels for 0% -> 0%
where the time goes in v7:
time: 146 us; the launch traced here: 145 us
  waiting for transfers between devices  55.6 us (38%)
  starting transfers between devices  51.6 us (35%)
  Pallas kernels  15.9 us (11%)
  local copies, waits for them, and re-layouts  9.42 us (6%)
  matrix products  8.07 us (6%)
  other arithmetic  4.32 us (3%)
    ppermute x3, waiting for transfers between devices, over_y(): lax.ppermute(block, 'lon', across_y(k))  23.6 us
    all_to_all x1, waiting for transfers between devices, gather_z(): lax.all_to_all(copies(shard, 16), ('lon', 'frame'), 0, 0, axis_index_grou...  20.8 us
    pallas_call x1, Pallas kernels, block(): pl.pallas_call(functools.partial(block_kernel, lat_rows), out_shape=jax.S...  15.9 us
    all_to_all x1, starting transfers between devices, gather_z(): lax.all_to_all(copies(shard, 16), ('lon', 'frame'), 0, 0, axis_index_grou...  11 us
    ppermute x3, starting transfers between devices, over_y(): lax.ppermute(block, 'lon', across_y(k))  9.66 us
    ppermute x3, starting transfers between devices, body(): others += [lax.ppermute(piece, 'lon', CORES) for piece in pieces[1:]]  9.43 us
    dot_general x3, matrix products, body(): jnp.dot(order.astype(jnp.bfloat16), temporal_kernel[k * channels:(k + 1)...  8.07 us
    all_to_all x1, waiting for transfers between devices, over_x(): lax.all_to_all(copies(block, X), 'frame', 0, 0, axis_index_groups=x_group...  7.77 us
  transfers between devices with their start and end apart: 13, of which 5 were waited for; matrix products, arithmetic and copies ran while one was open for 12% of the time, Pallas kernels for 0%

profile of v7, /device:TPU:289, one launch (start us, length us, event | category | flops | bytes accessed | tf_op | source)
XLA Modules:
  0.0 145.3 jit_solution(15602052095683366700)
XLA Ops:
  0.0 1.5 %broadcast_in_dim.39 = bf16[16,40,180]{2,1,0:T(8,128)(2,1)} broadcast(bf16[40,180]{1,0:T(8,128)(2,1)} %bitcast.38), dimensions={1,2} | broadcast | bytes 244800 | tf_op jit(solution)/shard_map/broadcast_in_dim | solution.py:53
  1.5 11.0 %all-to-all-start = ((bf16[16,40,180]{2,1,0:T(8,128)(2,1)}), bf16[16,40,180]{2,1,0:T(8,128)(2,1)S(1)}, u32[]{:S(2)}, u32[]{:S(2)}) async-start(bf16[16,40,180]{2,1,0:T(8,128)(2,1)} %broadcast_in_dim.39), calls=%async_computation | async-start | bytes 655360 | tf_op jit(solution)/shard_map/all_to_all | solution.py:59
  12.5 1.2 copy.26
  13.7 0.0 copy-start.1
  13.7 0.9 select_bitcast_fusion.2
  14.6 3.1 %collective-permute-start.1 = (bf16[5,32,640]{2,1,0:T(8,128)(2,1)}, bf16[5,32,640]{2,1,0:T(8,128)(2,1)}, u32[]{:S(2)}, u32[]{:S(2)}) collective-permute-start(bf16[5,32,640]{2,1,0:T(8,128)(2,1)} %get-tuple-element.23), channel_id=1, source_target_pairs={{0,32},{32,0},{64,96},{96,64},{128,160},{160,128},{192,224},{224,1... | collective-permute-start | bytes 614408 | tf_op jit(solution)/shard_map/ppermute | solution.py:89
  17.8 4.0 %collective-permute-start = (bf16[5,32,640]{2,1,0:T(8,128)(2,1)}, bf16[5,32,640]{2,1,0:T(8,128)(2,1)}, u32[]{:S(2)}, u32[]{:S(2)}) collective-permute-start(bf16[5,32,640]{2,1,0:T(8,128)(2,1)} %get-tuple-element.24), channel_id=1, source_target_pairs={{0,480},{32,64},{64,32},{96,128},{128,96},{160,192},{192,160},{224... | collective-permute-start | bytes 614408 | tf_op jit(solution)/shard_map/ppermute | solution.py:88
  21.8 20.8 %all-to-all-done = bf16[16,40,180]{2,1,0:T(8,128)(2,1)S(1)} async-done(((bf16[16,40,180]{2,1,0:T(8,128)(2,1)}), bf16[16,40,180]{2,1,0:T(8,128)(2,1)S(1)}, u32[]{:S(2)}, u32[]{:S(2)}) %all-to-all-start) | async-done | bytes 230432 | tf_op jit(solution)/shard_map/all_to_all | solution.py:59
  42.6 0.1 copy.21
  42.7 0.3 broadcast_in_dim.40
  43.0 0.0 copy-start.7
  43.0 0.0 copy-start.8
  43.0 0.0 copy-start.9
  43.0 0.0 copy-start.10
  43.0 1.1 broadcast_in_dim.41
  44.1 4.0 %all-to-all-start.1 = ((bf16[4,80,1440]{2,1,0:T(8,128)(2,1)}), bf16[4,80,1440]{2,1,0:T(8,128)(2,1)S(1)}, u32[]{:S(2)}, u32[]{:S(2)}) async-start(bf16[4,80,1440]{2,1,0:T(8,128)(2,1)} %broadcast_in_dim.41), calls=%async_computation.1 | async-start | bytes 1966080 | tf_op jit(solution)/shard_map/all_to_all | solution.py:67
  48.1 3.0 %fusion = bf16[640,640]{1,0:T(8,128)(2,1)} fusion(bf16[1920,640]{1,0:T(8,128)(2,1)} %param.12, s32[640]{0:T(1024)S(1)} %multiply_add_fusion), kind=kOutput, calls=%fused_computation.4 | convolution fusion | flops 524697600 | bytes 1640960 | tf_op jit(solution)/shard_map/dot_general | solution.py:218
  51.2 3.0 %fusion.1 = bf16[640,640]{1,0:T(8,128)(2,1)} fusion(bf16[1920,640]{1,0:T(8,128)(2,1)} %param.12, s32[640]{0:T(1024)S(1)} %multiply_add_fusion), kind=kOutput, calls=%fused_computation.5 | convolution fusion | flops 524697600 | bytes 1640960 | tf_op jit(solution)/shard_map/dot_general | solution.py:218
  54.1 7.8 %all-to-all-done.1 = bf16[4,80,1440]{2,1,0:T(8,128)(2,1)S(1)} async-done(((bf16[4,80,1440]{2,1,0:T(8,128)(2,1)}), bf16[4,80,1440]{2,1,0:T(8,128)(2,1)S(1)}, u32[]{:S(2)}, u32[]{:S(2)}) %all-to-all-start.1) | async-done | bytes 921632 | tf_op jit(solution)/shard_map/all_to_all | solution.py:67
  61.9 0.9 slice_bitcast_fusion
  62.8 1.6 %concatenate.12.w0 = bf16[80,5760]{1,0:T(8,128)(2,1)S(1)} concatenate(bf16[80,1440]{1,0:T(8,128)(2,1)} %get-tuple-element.22, bf16[80,1440]{1,0:T(8,128)(2,1)} %get-tuple-element.21, bf16[80,1440]{1,0:T(8,128)(2,1)S(1)} %get-tuple-element.20, bf16[80,1440]{1,0:T(8,128)(2,1)S(1)} %get-tuple-element.19), dimensions={1} | concatenate | bytes 1843200 | tf_op jit(solution)/shard_map/concatenate | solution.py:75
  64.4 3.2 %collective-permute-start.8 = (bf16[80,5760]{1,0:T(8,128)(2,1)S(1)}, bf16[80,5760]{1,0:T(8,128)(2,1)}, u32[]{:S(2)}, u32[]{:S(2)}) collective-permute-start(bf16[80,5760]{1,0:T(8,128)(2,1)S(1)} %concatenate.12.w0), channel_id=1, source_target_pairs={{128,0},{160,32},{192,64},{224,96},{0,128},{32,160},{64,192},{96,2... | collective-permute-start | bytes 2764808 | tf_op jit(solution)/shard_map/ppermute | solution.py:71
  67.6 4.5 %collective-permute-start.6 = (bf16[80,5760]{1,0:T(8,128)(2,1)S(1)}, bf16[80,5760]{1,0:T(8,128)(2,1)}, u32[]{:S(2)}, u32[]{:S(2)}) collective-permute-start(bf16[80,5760]{1,0:T(8,128)(2,1)S(1)} %concatenate.12.w0), channel_id=1, source_target_pairs={{256,0},{288,32},{320,64},{352,96},{384,128},{416,160},{448,192},{... | collective-permute-start | bytes 2764808 | tf_op jit(solution)/shard_map/ppermute | solution.py:71
  72.1 1.9 %collective-permute-start.4 = (bf16[80,5760]{1,0:T(8,128)(2,1)S(1)}, bf16[80,5760]{1,0:T(8,128)(2,1)}, u32[]{:S(2)}, u32[]{:S(2)}) collective-permute-start(bf16[80,5760]{1,0:T(8,128)(2,1)S(1)} %concatenate.12.w0), channel_id=1, source_target_pairs={{384,0},{416,32},{448,64},{480,96},{256,128},{288,160},{320,192},{... | collective-permute-start | bytes 2764808 | tf_op jit(solution)/shard_map/ppermute | solution.py:71
  74.0 2.1 %fusion.2 = bf16[640,640]{1,0:T(8,128)(2,1)S(1)} fusion(bf16[1920,640]{1,0:T(8,128)(2,1)} %param.12, s32[640]{0:T(1024)S(1)} %multiply_add_fusion), kind=kOutput, calls=%fused_computation.6 | convolution fusion | flops 524697600 | bytes 1640960 | tf_op jit(solution)/shard_map/dot_general | solution.py:218
  76.2 0.0 collective-permute-done.1
  76.2 0.0 collective-permute-done
  76.2 1.2 select_bitcast_fusion.1
  77.4 0.1 pad_maximum_fusion.4
  77.5 1.9 %collective-permute-start.2 = (bf16[6,1,32,640]{3,2,1,0:T(8,128)(2,1)S(1)}, bf16[6,1,32,640]{3,2,1,0:T(8,128)(2,1)S(1)}, u32[]{:S(2)}, u32[]{:S(2)}) collective-permute-start(bf16[6,1,32,640]{3,2,1,0:T(8,128)(2,1)S(1)} %get-tuple-element.17), channel_id=1, source_target_pairs={{0,1},{1,2},{2,3},{3,4},{4,5},{5,6},{6,7},{7,8},{8,9},{9,10},{10,1... | collective-permute-start | bytes 737288 | tf_op jit(solution)/shard_map/ppermute | solution.py:96
  79.4 0.0 copy-start.2
  79.4 3.5 %collective-permute-start.3 = (bf16[6,1,32,640]{3,2,1,0:T(8,128)(2,1)S(1)}, bf16[6,1,32,640]{3,2,1,0:T(8,128)(2,1)S(1)}, u32[]{:S(2)}, u32[]{:S(2)}) collective-permute-start(bf16[6,1,32,640]{3,2,1,0:T(8,128)(2,1)S(1)} %get-tuple-element.18), channel_id=1, source_target_pairs={{1,0},{2,1},{3,2},{4,3},{5,4},{6,5},{7,6},{8,7},{9,8},{10,9},{11,1... | collective-permute-start | bytes 737288 | tf_op jit(solution)/shard_map/ppermute | solution.py:97
  82.9 0.2 pad_maximum_fusion.kernel_any
  83.2 0.0 copy-start.6
  83.2 0.0 copy-start.5
  83.2 1.6 %collective-permute-done.2 = bf16[6,1,32,640]{3,2,1,0:T(8,128)(2,1)S(1)} collective-permute-done((bf16[6,1,32,640]{3,2,1,0:T(8,128)(2,1)S(1)}, bf16[6,1,32,640]{3,2,1,0:T(8,128)(2,1)S(1)}, u32[]{:S(2)}, u32[]{:S(2)}) %collective-permute-start.2) | collective-permute-done | bytes 245792 | tf_op jit(solution)/shard_map/ppermute | solution.py:96
  84.8 5.0 %collective-permute-start.5 = (bf16[80,5760]{1,0:T(8,128)(2,1)S(1)}, bf16[80,5760]{1,0:T(8,128)(2,1)}, u32[]{:S(2)}, u32[]{:S(2)}) collective-permute-start(bf16[80,5760]{1,0:T(8,128)(2,1)S(1)} %concatenate.12.w0), channel_id=1, source_target_pairs={{0,32},{32,0},{64,96},{96,64},{128,160},{160,128},{192,224},{224,1... | collective-permute-start | bytes 2764808 | tf_op jit(solution)/shard_map/ppermute | solution.py:224
  89.8 1.5 %pad_maximum_fusion.1 = bf16[6,7,32,640]{3,2,1,0:T(8,128)(2,1)} fusion(bf16[6,1,32,640]{3,2,1,0:T(8,128)(2,1)S(1)} %collective-permute-done.3, bf16[1,5,32,640]{3,2,1,0:T(8,128)(2,1)S(1)} %get-tuple-element.26, bf16[4,5,32,640]{3,2,1,0:T(8,128)(2,1)S(1)} %bitcast.36, bf16[1,5,32,640]{3,2,1,0:T(8,128)(2,1)S(1)} %get-tuple-element.25, ...), kind=kLoop, calls=%fused_computation.1 | loop fusion | flops 3440640 | bytes 3440640 | tf_op jit(solution)/shard_map/concatenate | solution.py:230
  91.3 23.6 %collective-permute-done.4.w6 = bf16[80,5760]{1,0:T(8,128)(2,1)} collective-permute-done((bf16[80,5760]{1,0:T(8,128)(2,1)S(1)}, bf16[80,5760]{1,0:T(8,128)(2,1)}, u32[]{:S(2)}, u32[]{:S(2)}) %collective-permute-start.4) | collective-permute-done | bytes 921632 | tf_op jit(solution)/shard_map/ppermute | solution.py:71
  114.9 4.9 %collective-permute-start.9 = (bf16[80,5760]{1,0:T(8,128)(2,1)}, bf16[80,5760]{1,0:T(8,128)(2,1)}, u32[]{:S(2)}, u32[]{:S(2)}) collective-permute-start(bf16[80,5760]{1,0:T(8,128)(2,1)} %collective-permute-done.8.w4), channel_id=1, source_target_pairs={{0,32},{32,0},{64,96},{96,64},{128,160},{160,128},{192,224},{224,1... | collective-permute-start | bytes 2764808 | tf_op jit(solution)/shard_map/ppermute | solution.py:232
  119.8 1.9 %collective-permute-start.7 = (bf16[80,5760]{1,0:T(8,128)(2,1)}, bf16[80,5760]{1,0:T(8,128)(2,1)}, u32[]{:S(2)}, u32[]{:S(2)}) collective-permute-start(bf16[80,5760]{1,0:T(8,128)(2,1)} %collective-permute-done.6.w2), channel_id=1, source_target_pairs={{0,32},{32,0},{64,96},{96,64},{128,160},{160,128},{192,224},{224,1... | collective-permute-start | bytes 2764808 | tf_op jit(solution)/shard_map/ppermute | solution.py:232
  121.8 2.6 %collective-permute-start.10 = (bf16[80,5760]{1,0:T(8,128)(2,1)}, bf16[80,5760]{1,0:T(8,128)(2,1)}, u32[]{:S(2)}, u32[]{:S(2)}) collective-permute-start(bf16[80,5760]{1,0:T(8,128)(2,1)} %collective-permute-done.4.w6), channel_id=1, source_target_pairs={{0,32},{32,0},{64,96},{96,64},{128,160},{160,128},{192,224},{224,1... | collective-permute-start | bytes 2764808 | tf_op jit(solution)/shard_map/ppermute | solution.py:232
  124.4 0.3 select_reduce_fusion
  124.8 0.1 add_convert_fusion.flags_ref
  124.9 1.8 %collective-permute-done.10.w7 = bf16[80,5760]{1,0:T(8,128)(2,1)} collective-permute-done((bf16[80,5760]{1,0:T(8,128)(2,1)}, bf16[80,5760]{1,0:T(8,128)(2,1)}, u32[]{:S(2)}, u32[]{:S(2)}) %collective-permute-start.10) | collective-permute-done | bytes 921632 | tf_op jit(solution)/shard_map/ppermute | solution.py:232
  126.6 1.5 %copy-done = bf16[6,7,32,640]{3,2,1,0:T(8,128)(2,1)S(1)} copy-done((bf16[6,7,32,640]{3,2,1,0:T(8,128)(2,1)S(1)}, bf16[6,7,32,640]{3,2,1,0:T(8,128)(2,1)}, u32[]{:S(2)}) %copy-start) | copy-done | bytes 1720344
  128.1 15.9 %shard_map.91 = bf16[4,160,640]{2,1,0:T(8,128)(2,1)S(1)} custom-call(s32[2]{0:T(128)S(1)} %add_convert_fusion.flags_ref, bf16[6,224,640]{2,1,0:T(8,128)(2,1)S(1)} %bitcast.32, bf16[80,5760]{1,0:T(8,128)(2,1)S(1)} %concatenate.12.w0, bf16[80,5760]{1,0:T(8,128)(2,1)} %collective-permute-done.5.w1, bf16[80,5760]{1,0:T(8,128)(2,1)} %collective-permute-done.6.w2, ...), custom_call_target="tpu_custom_call" | custom-call | flops 8178892800 | bytes 16777216 | tf_op jit(solution)/shard_map/pallas_call | solution.py:196
  144.0 1.3 copy.25
  (22 shorter events, 0.1 us)
Async XLA Ops:
  1.5 41.1 %all-to-all-start = ((bf16[16,40,180]{2,1,0:T(8,128)(2,1)}), bf16[16,40,180]{2,1,0:T(8,128)(2,1)S(1)}, u32[]{:S(2)}, u32[]{:S(2)}) async-start(bf16[16,40,180]{2,1,0:T(8,128)(2,1)} %broadcast_in_dim.39), calls=%async_computation | async-start | bytes 655360 | tf_op jit(solution)/shard_map/all_to_all | solution.py:59
  13.7 63.6 %copy-start.1 = (bf16[5,32,4,640]{3,1,0,2:T(8,128)(2,1)}, bf16[5,32,4,640]{3,1,0,2:T(8,128)(2,1)S(1)}, u32[]{:S(2)}) copy-start(bf16[5,32,4,640]{3,1,0,2:T(8,128)(2,1)S(1)} %copy.26) | copy-start | bytes 2457604
  14.6 61.5 %collective-permute-start.1 = (bf16[5,32,640]{2,1,0:T(8,128)(2,1)}, bf16[5,32,640]{2,1,0:T(8,128)(2,1)}, u32[]{:S(2)}, u32[]{:S(2)}) collective-permute-start(bf16[5,32,640]{2,1,0:T(8,128)(2,1)} %get-tuple-element.23), channel_id=1, source_target_pairs={{0,32},{32,0},{64,96},{96,64},{128,160},{160,128},{192,224},{224,1... | collective-permute-start | bytes 614408 | tf_op jit(solution)/shard_map/ppermute | solution.py:89
  17.8 58.4 %collective-permute-start = (bf16[5,32,640]{2,1,0:T(8,128)(2,1)}, bf16[5,32,640]{2,1,0:T(8,128)(2,1)}, u32[]{:S(2)}, u32[]{:S(2)}) collective-permute-start(bf16[5,32,640]{2,1,0:T(8,128)(2,1)} %get-tuple-element.24), channel_id=1, source_target_pairs={{0,480},{32,64},{64,32},{96,128},{128,96},{160,192},{192,160},{224... | collective-permute-start | bytes 614408 | tf_op jit(solution)/shard_map/ppermute | solution.py:88
  43.0 5.1 %copy-start.7 = (s32[640]{0:T(1024)S(1)}, s32[640]{0:T(1024)}, u32[]{:S(2)}) copy-start(s32[640]{0:T(1024)} %constant.64) | copy-start | bytes 7684
  43.0 5.1 %copy-start.8 = (s32[640]{0:T(1024)S(1)}, s32[640]{0:T(1024)}, u32[]{:S(2)}) copy-start(s32[640]{0:T(1024)} %constant.61.clone) | copy-start | bytes 7684
  43.0 5.1 %copy-start.9 = (s32[640]{0:T(1024)S(1)}, s32[640]{0:T(1024)}, u32[]{:S(2)}) copy-start(s32[640]{0:T(1024)} %constant.59.clone) | copy-start | bytes 7684
  43.0 5.1 %copy-start.10 = (s32[640]{0:T(1024)S(1)}, s32[640]{0:T(1024)}, u32[]{:S(2)}) copy-start(s32[640]{0:T(1024)} %constant.58.clone) | copy-start | bytes 7684
  44.1 17.8 %all-to-all-start.1 = ((bf16[4,80,1440]{2,1,0:T(8,128)(2,1)}), bf16[4,80,1440]{2,1,0:T(8,128)(2,1)S(1)}, u32[]{:S(2)}, u32[]{:S(2)}) async-start(bf16[4,80,1440]{2,1,0:T(8,128)(2,1)} %broadcast_in_dim.41), calls=%async_computation.1 | async-start | bytes 1966080 | tf_op jit(solution)/shard_map/all_to_all | solution.py:67
  64.4 50.5 %collective-permute-start.8 = (bf16[80,5760]{1,0:T(8,128)(2,1)S(1)}, bf16[80,5760]{1,0:T(8,128)(2,1)}, u32[]{:S(2)}, u32[]{:S(2)}) collective-permute-start(bf16[80,5760]{1,0:T(8,128)(2,1)S(1)} %concatenate.12.w0), channel_id=1, source_target_pairs={{128,0},{160,32},{192,64},{224,96},{0,128},{32,160},{64,192},{96,2... | collective-permute-start | bytes 2764808 | tf_op jit(solution)/shard_map/ppermute | solution.py:71
  67.6 52.3 %collective-permute-start.6 = (bf16[80,5760]{1,0:T(8,128)(2,1)S(1)}, bf16[80,5760]{1,0:T(8,128)(2,1)}, u32[]{:S(2)}, u32[]{:S(2)}) collective-permute-start(bf16[80,5760]{1,0:T(8,128)(2,1)S(1)} %concatenate.12.w0), channel_id=1, source_target_pairs={{256,0},{288,32},{320,64},{352,96},{384,128},{416,160},{448,192},{... | collective-permute-start | bytes 2764808 | tf_op jit(solution)/shard_map/ppermute | solution.py:71
  72.1 42.8 %collective-permute-start.4 = (bf16[80,5760]{1,0:T(8,128)(2,1)S(1)}, bf16[80,5760]{1,0:T(8,128)(2,1)}, u32[]{:S(2)}, u32[]{:S(2)}) collective-permute-start(bf16[80,5760]{1,0:T(8,128)(2,1)S(1)} %concatenate.12.w0), channel_id=1, source_target_pairs={{384,0},{416,32},{448,64},{480,96},{256,128},{288,160},{320,192},{... | collective-permute-start | bytes 2764808 | tf_op jit(solution)/shard_map/ppermute | solution.py:71
  76.1 6.8 %copy-start.3 = (bf16[640,640]{1,0:T(8,128)(2,1)S(1)}, bf16[640,640]{1,0:T(8,128)(2,1)}, u32[]{:S(2)}) copy-start(bf16[640,640]{1,0:T(8,128)(2,1)} %fusion) | copy-start | bytes 2457604
  76.1 6.8 %copy-start.4 = (bf16[640,640]{1,0:T(8,128)(2,1)S(1)}, bf16[640,640]{1,0:T(8,128)(2,1)}, u32[]{:S(2)}) copy-start(bf16[640,640]{1,0:T(8,128)(2,1)} %fusion.1) | copy-start | bytes 2457604
  77.5 7.3 %collective-permute-start.2 = (bf16[6,1,32,640]{3,2,1,0:T(8,128)(2,1)S(1)}, bf16[6,1,32,640]{3,2,1,0:T(8,128)(2,1)S(1)}, u32[]{:S(2)}, u32[]{:S(2)}) collective-permute-start(bf16[6,1,32,640]{3,2,1,0:T(8,128)(2,1)S(1)} %get-tuple-element.17), channel_id=1, source_target_pairs={{0,1},{1,2},{2,3},{3,4},{4,5},{5,6},{6,7},{7,8},{8,9},{9,10},{10,1... | collective-permute-start | bytes 737288 | tf_op jit(solution)/shard_map/ppermute | solution.py:96
  79.4 10.4 %copy-start.2 = (bf16[5,32,4,640]{3,1,0,2:T(8,128)(2,1)S(1)}, bf16[5,32,4,640]{3,1,0,2:T(8,128)(2,1)}, u32[]{:S(2)}) copy-start(bf16[5,32,4,640]{3,1,0,2:T(8,128)(2,1)} %copy-done.1) | copy-start | bytes 2457604
  79.4 10.4 %collective-permute-start.3 = (bf16[6,1,32,640]{3,2,1,0:T(8,128)(2,1)S(1)}, bf16[6,1,32,640]{3,2,1,0:T(8,128)(2,1)S(1)}, u32[]{:S(2)}, u32[]{:S(2)}) collective-permute-start(bf16[6,1,32,640]{3,2,1,0:T(8,128)(2,1)S(1)} %get-tuple-element.18), channel_id=1, source_target_pairs={{1,0},{2,1},{3,2},{4,3},{5,4},{6,5},{7,6},{8,7},{9,8},{10,9},{11,1... | collective-permute-start | bytes 737288 | tf_op jit(solution)/shard_map/ppermute | solution.py:97
  83.2 41.2 %copy-start.6 = (f32[640]{0:T(1024)S(1)}, f32[640]{0:T(1024)}, u32[]{:S(2)}) copy-start(f32[640]{0:T(1024)} %param.13) | copy-start | bytes 7684
  83.2 41.2 %copy-start.5 = (f32[640]{0:T(1024)S(1)}, f32[640]{0:T(1024)}, u32[]{:S(2)}) copy-start(f32[640]{0:T(1024)} %param.11) | copy-start | bytes 7684
  84.8 40.1 %collective-permute-start.5 = (bf16[80,5760]{1,0:T(8,128)(2,1)S(1)}, bf16[80,5760]{1,0:T(8,128)(2,1)}, u32[]{:S(2)}, u32[]{:S(2)}) collective-permute-start(bf16[80,5760]{1,0:T(8,128)(2,1)S(1)} %concatenate.12.w0), channel_id=1, source_target_pairs={{0,32},{32,0},{64,96},{96,64},{128,160},{160,128},{192,224},{224,1... | collective-permute-start | bytes 2764808 | tf_op jit(solution)/shard_map/ppermute | solution.py:224
  114.9 9.9 %collective-permute-start.9 = (bf16[80,5760]{1,0:T(8,128)(2,1)}, bf16[80,5760]{1,0:T(8,128)(2,1)}, u32[]{:S(2)}, u32[]{:S(2)}) collective-permute-start(bf16[80,5760]{1,0:T(8,128)(2,1)} %collective-permute-done.8.w4), channel_id=1, source_target_pairs={{0,32},{32,0},{64,96},{96,64},{128,160},{160,128},{192,224},{224,1... | collective-permute-start | bytes 2764808 | tf_op jit(solution)/shard_map/ppermute | solution.py:232
  119.8 5.0 %collective-permute-start.7 = (bf16[80,5760]{1,0:T(8,128)(2,1)}, bf16[80,5760]{1,0:T(8,128)(2,1)}, u32[]{:S(2)}, u32[]{:S(2)}) collective-permute-start(bf16[80,5760]{1,0:T(8,128)(2,1)} %collective-permute-done.6.w2), channel_id=1, source_target_pairs={{0,32},{32,0},{64,96},{96,64},{128,160},{160,128},{192,224},{224,1... | collective-permute-start | bytes 2764808 | tf_op jit(solution)/shard_map/ppermute | solution.py:232
  121.8 4.8 %collective-permute-start.10 = (bf16[80,5760]{1,0:T(8,128)(2,1)}, bf16[80,5760]{1,0:T(8,128)(2,1)}, u32[]{:S(2)}, u32[]{:S(2)}) collective-permute-start(bf16[80,5760]{1,0:T(8,128)(2,1)} %collective-permute-done.4.w6), channel_id=1, source_target_pairs={{0,32},{32,0},{64,96},{96,64},{128,160},{160,128},{192,224},{224,1... | collective-permute-start | bytes 2764808 | tf_op jit(solution)/shard_map/ppermute | solution.py:232
  126.6 1.5 %copy-start = (bf16[6,7,32,640]{3,2,1,0:T(8,128)(2,1)S(1)}, bf16[6,7,32,640]{3,2,1,0:T(8,128)(2,1)}, u32[]{:S(2)}) copy-start(bf16[6,7,32,640]{3,2,1,0:T(8,128)(2,1)} %pad_maximum_fusion.1) | copy-start | bytes 5160964

commit v8 on v7

--- a/solution.py
+++ b/solution.py
@@ -44,7 +44,7 @@
     return [((y ^ k) * 4 + r, y * 4 + r) for y in range(Y) for r in range(4)]
 
 
-NEAR_FIRST = (0, 2, 1, 3)
+NEAR_FIRST = (0, 1, 3, 2)
 CORES = [(i, i ^ 1) for i in range(LONS)]
 FAR = [(i, (i + 1) % LONS if i % 2 else (i - 1) % LONS) for i in range(LONS)]
 
@@ -129,13 +129,18 @@
 
 
 def block_kernel(
-    lat_rows, flags_ref, planes_any, w0, w1, w2, w3, w4, w5, w6, w7, kernel_any, bias_ref, tbias_ref,
-    out_ref, planes_ref, weights_ref, kernel_ref, taps_ref, sems,
+    lat_rows, flags_ref, wide_any, earlier_any, later_any, w0, w1, w2, w3, w4, w5, w6, w7, kernel_any,
+    bias_ref, tbias_ref, out_ref, planes_ref, weights_ref, kernel_ref, taps_ref, sems,
 ):
     pieces = (w0, w1, w2, w3, w4, w5, w6, w7)
     count = weights_ref.shape[0] // len(pieces)
     third = weights_ref.shape[1] // 3
-    pairs = [(planes_any, planes_ref)]
+    held = planes_ref.shape[1]
+    pairs = [
+        (wide_any, planes_ref.at[:, pl.ds(lat_rows, held - 2 * lat_rows)]),
+        (earlier_any, planes_ref.at[:, pl.ds(0, lat_rows)]),
+        (later_any, planes_ref.at[:, pl.ds(held - lat_rows, lat_rows)]),
+    ]
     pairs += [
         (
             w.at[:, pl.ds(a * third, third)],
@@ -151,14 +156,15 @@
     ]
     for move in moves:
         move.start()
-    moves[0].wait()
+    for move in moves[:3]:
+        move.wait()
     shift_rows(planes_ref, taps_ref, lat_rows)
 
     planes, rows, channels = planes_ref.shape
     columns, inner = planes - 2, rows - 2 * lat_rows
     total = None
     for a in range(3):
-        for move in moves[1 + a * len(pieces) : 1 + (a + 1) * len(pieces)]:
+        for move in moves[3 + a * len(pieces) : 3 + (a + 1) * len(pieces)]:
             move.wait()
         taps = [taps_ref[a, b : b + columns].reshape(columns * rows, channels) for b in range(3)]
         term = lax.dot_general(
@@ -186,10 +192,11 @@
     out_ref[...] = (here + mixed).astype(jnp.bfloat16)
 
 
-def block(flags, planes, weights, kernel, bias, tbias, lat_rows):
-    count, rows, channels = planes.shape
-    inner = rows - 2 * lat_rows
-    moved = (planes, *weights, kernel)
+def block(flags, wide, earlier, later, weights, kernel, bias, tbias, lat_rows):
+    count, inner, channels = wide.shape
+    rows = inner + 2 * lat_rows
+    planes = jax.ShapeDtypeStruct((count, rows, channels), wide.dtype)
+    moved = (wide, earlier, later, *weights, kernel)
     joined = (len(weights) * weights[0].shape[0], weights[0].shape[1])
     shapes = (planes.shape, joined, kernel.shape, (3, *planes.shape))
     flops = (count - 2) * 2 * channels * channels * (9 * rows + 3 * inner)
@@ -199,7 +206,7 @@
         in_specs=[SMEM] + [ANY] * len(moved) + [VMEM, VMEM],
         out_specs=VMEM,
         scratch_shapes=[pltpu.VMEM(s, jnp.bfloat16) for s in shapes]
-        + [pltpu.SemaphoreType.DMA((3 * len(weights) + 2,))],
+        + [pltpu.SemaphoreType.DMA((3 * len(weights) + 4,))],
         compiler_params=params(34),
         cost_estimate=pl.CostEstimate(flops=flops, bytes_accessed=2**24, transcendentals=0),
     )(flags, *moved, bias, tbias)
@@ -222,21 +229,27 @@
     mine = joined_x(over_x(along_z))
     pieces = over_y(mine)
     others = [lax.ppermute(mine, "lon", CORES)]
-    far, near, columns, _ = lax.optimization_barrier((far, near, columns, mine))
+    far, near, columns, ordered, _ = lax.optimization_barrier((far, near, columns, ordered, mine))
     before = jnp.where(core == 1, near, far)
     after = jnp.where(core == 1, far, near)
     wide = jnp.concatenate([before[None], columns, after[None]], axis=0)
     earlier, later = frame_halos(wide)
-    planes = jnp.concatenate([earlier, wide, later], axis=1)
-    planes, ordered, pieces[3] = lax.optimization_barrier((planes, ordered, pieces[3]))
+    earlier, later, pieces[3] = lax.optimization_barrier((earlier, later, pieces[3]))
     others += [lax.ppermute(piece, "lon", CORES) for piece in pieces[1:]]
     weights = [piece for pair in zip(pieces, others) for piece in pair]
-    planes = planes.reshape(lon_cols + 2, (frames + 2) * lat_rows, channels)
 
     frame = lax.axis_index("frame")
     flags = jnp.stack([frame == 0, frame == FRAMES_AXIS - 1]).astype(jnp.int32)
     result = block(
-        flags, planes, weights, ordered, bias[None], temporal_bias[None], lat_rows
+        flags,
+        wide.reshape(lon_cols + 2, frames * lat_rows, channels),
+        earlier.reshape(lon_cols + 2, lat_rows, channels),
+        later.reshape(lon_cols + 2, lat_rows, channels),
+        weights,
+        ordered,
+        bias[None],
+        temporal_bias[None],
+        lat_rows,
     )
     return result.reshape(lon_cols, frames, lat_rows, channels).transpose(1, 2, 0, 3)
 

time: 146 us -> 135 us (0.925)
  the two profiles are of different devices: /device:TPU:289 before, /device:TPU:297 now
where the time goes in v8:
time: 135 us
  starting transfers between devices  52.6 us (39%)
  waiting for transfers between devices  44.5 us (33%)
  Pallas kernels  15.8 us (12%)
  local copies, waits for them, and re-layouts  8.62 us (6%)
  matrix products  6.83 us (5%)
  other arithmetic  5.78 us (4%)
    all_to_all x1, waiting for transfers between devices, gather_z(): lax.all_to_all(copies(shard, 16), ('lon', 'frame'), 0, 0, axis_index_grou...  21.5 us
    pallas_call x1, Pallas kernels, block(): pl.pallas_call(functools.partial(block_kernel, lat_rows), out_shape=jax.S...  15.8 us
    ppermute x3, waiting for transfers between devices, over_y(): lax.ppermute(block, 'lon', across_y(k))  13.4 us
    all_to_all x1, starting transfers between devices, gather_z(): lax.all_to_all(copies(shard, 16), ('lon', 'frame'), 0, 0, axis_index_grou...  11 us
    ppermute x3, starting transfers between devices, body(): others += [lax.ppermute(piece, 'lon', CORES) for piece in pieces[1:]]  11 us
    ppermute x3, starting transfers between devices, over_y(): lax.ppermute(block, 'lon', across_y(k))  9.11 us
    all_to_all x1, waiting for transfers between devices, over_x(): lax.all_to_all(copies(block, X), 'frame', 0, 0, axis_index_groups=x_group...  6.97 us
    dot_general x3, matrix products, body(): jnp.dot(order.astype(jnp.bfloat16), temporal_kernel[k * channels:(k + 1)...  6.83 us
  transfers between devices with their start and end apart: 13, of which 5 were waited for; matrix products, arithmetic and copies ran while one was open for 12% of the time, Pallas kernels for 0%

profile of v8, /device:TPU:297, one launch (start us, length us, event | category | flops | bytes accessed | tf_op | source)
XLA Modules:
  0.0 134.5 jit_solution(5707865037204232241)
XLA Ops:
  0.0 0.0 copy-start.13
  0.0 1.5 %broadcast_in_dim.39 = bf16[16,40,180]{2,1,0:T(8,128)(2,1)} broadcast(bf16[40,180]{1,0:T(8,128)(2,1)} %bitcast.47), dimensions={1,2} | broadcast | bytes 244800 | tf_op jit(solution)/shard_map/broadcast_in_dim | solution.py:53
  1.5 11.0 %all-to-all-start = ((bf16[16,40,180]{2,1,0:T(8,128)(2,1)}), bf16[16,40,180]{2,1,0:T(8,128)(2,1)S(1)}, u32[]{:S(2)}, u32[]{:S(2)}) async-start(bf16[16,40,180]{2,1,0:T(8,128)(2,1)} %broadcast_in_dim.39), calls=%async_computation | async-start | bytes 655360 | tf_op jit(solution)/shard_map/all_to_all | solution.py:59
  12.6 1.2 copy.33
  13.8 0.0 copy-start.4
  13.8 0.9 copy-done.4
  14.7 0.8 select_bitcast_fusion
  15.5 5.2 %collective-permute-start = (bf16[5,32,640]{2,1,0:T(8,128)(2,1)}, bf16[5,32,640]{2,1,0:T(8,128)(2,1)}, u32[]{:S(2)}, u32[]{:S(2)}) collective-permute-start(bf16[5,32,640]{2,1,0:T(8,128)(2,1)} %get-tuple-element.26), channel_id=1, source_target_pairs={{0,480},{32,64},{64,32},{96,128},{128,96},{160,192},{192,160},{224... | collective-permute-start | bytes 614408 | tf_op jit(solution)/shard_map/ppermute | solution.py:88
  20.7 1.9 %collective-permute-start.1 = (bf16[5,32,640]{2,1,0:T(8,128)(2,1)}, bf16[5,32,640]{2,1,0:T(8,128)(2,1)}, u32[]{:S(2)}, u32[]{:S(2)}) collective-permute-start(bf16[5,32,640]{2,1,0:T(8,128)(2,1)} %get-tuple-element.25), channel_id=1, source_target_pairs={{0,32},{32,0},{64,96},{96,64},{128,160},{160,128},{192,224},{224,1... | collective-permute-start | bytes 614408 | tf_op jit(solution)/shard_map/ppermute | solution.py:89
  22.7 21.5 %all-to-all-done = bf16[16,40,180]{2,1,0:T(8,128)(2,1)S(1)} async-done(((bf16[16,40,180]{2,1,0:T(8,128)(2,1)}), bf16[16,40,180]{2,1,0:T(8,128)(2,1)S(1)}, u32[]{:S(2)}, u32[]{:S(2)}) %all-to-all-start) | async-done | bytes 230432 | tf_op jit(solution)/shard_map/all_to_all | solution.py:59
  44.2 0.1 copy.24
  44.3 0.3 broadcast_in_dim.40
  44.6 1.0 broadcast_in_dim.41
  45.7 4.0 %all-to-all-start.1 = ((bf16[4,80,1440]{2,1,0:T(8,128)(2,1)}), bf16[4,80,1440]{2,1,0:T(8,128)(2,1)S(1)}, u32[]{:S(2)}, u32[]{:S(2)}) async-start(bf16[4,80,1440]{2,1,0:T(8,128)(2,1)} %broadcast_in_dim.41), calls=%async_computation.1 | async-start | bytes 1966080 | tf_op jit(solution)/shard_map/all_to_all | solution.py:67
  49.7 3.1 %fusion = bf16[640,640]{1,0:T(8,128)(2,1)} fusion(bf16[1920,640]{1,0:T(8,128)(2,1)} %param.12, s32[640]{0:T(1024)S(1)} %multiply_add_fusion), kind=kOutput, calls=%fused_computation.3 | convolution fusion | flops 524697600 | bytes 1640960 | tf_op jit(solution)/shard_map/dot_general | solution.py:225
  52.8 1.8 %fusion.1 = bf16[640,640]{1,0:T(8,128)(2,1)} fusion(bf16[1920,640]{1,0:T(8,128)(2,1)S(1)} %copy-done.14, s32[640]{0:T(1024)S(1)} %multiply_add_fusion), kind=kOutput, calls=%fused_computation.4 | convolution fusion | flops 524697600 | bytes 1642496 | tf_op jit(solution)/shard_map/dot_general | solution.py:225
  54.7 1.9 %fusion.2 = bf16[640,640]{1,0:T(8,128)(2,1)} fusion(bf16[1920,640]{1,0:T(8,128)(2,1)S(1)} %copy-done.14, s32[640]{0:T(1024)S(1)} %multiply_add_fusion), kind=kOutput, calls=%fused_computation.5 | convolution fusion | flops 524697600 | bytes 1642496 | tf_op jit(solution)/shard_map/dot_general | solution.py:225
  56.5 7.0 %all-to-all-done.1 = bf16[4,80,1440]{2,1,0:T(8,128)(2,1)S(1)} async-done(((bf16[4,80,1440]{2,1,0:T(8,128)(2,1)}), bf16[4,80,1440]{2,1,0:T(8,128)(2,1)S(1)}, u32[]{:S(2)}, u32[]{:S(2)}) %all-to-all-start.1) | async-done | bytes 921632 | tf_op jit(solution)/shard_map/all_to_all | solution.py:67
  63.5 0.1 slice_bitcast_fusion
  63.6 0.7 concatenate.19.w0
  64.3 0.0 copy-start.5
  64.3 3.7 %collective-permute-start.4 = (bf16[80,5760]{1,0:T(8,128)(2,1)S(1)}, bf16[80,5760]{1,0:T(8,128)(2,1)}, u32[]{:S(2)}, u32[]{:S(2)}) collective-permute-start(bf16[80,5760]{1,0:T(8,128)(2,1)S(1)} %concatenate.19.w0), channel_id=1, source_target_pairs={{256,0},{288,32},{320,64},{352,96},{384,128},{416,160},{448,192},{... | collective-permute-start | bytes 2764808 | tf_op jit(solution)/shard_map/ppermute | solution.py:71
  68.0 3.3 %collective-permute-start.6 = (bf16[80,5760]{1,0:T(8,128)(2,1)S(1)}, bf16[80,5760]{1,0:T(8,128)(2,1)}, u32[]{:S(2)}, u32[]{:S(2)}) collective-permute-start(bf16[80,5760]{1,0:T(8,128)(2,1)S(1)} %concatenate.19.w0), channel_id=1, source_target_pairs={{128,0},{160,32},{192,64},{224,96},{0,128},{32,160},{64,192},{96,2... | collective-permute-start | bytes 2764808 | tf_op jit(solution)/shard_map/ppermute | solution.py:71
  71.4 2.1 %collective-permute-start.8 = (bf16[80,5760]{1,0:T(8,128)(2,1)S(1)}, bf16[80,5760]{1,0:T(8,128)(2,1)}, u32[]{:S(2)}, u32[]{:S(2)}) collective-permute-start(bf16[80,5760]{1,0:T(8,128)(2,1)S(1)} %concatenate.19.w0), channel_id=1, source_target_pairs={{384,0},{416,32},{448,64},{480,96},{256,128},{288,160},{320,192},{... | collective-permute-start | bytes 2764808 | tf_op jit(solution)/shard_map/ppermute | solution.py:71
  73.5 1.9 %pad_maximum_fusion.kernel_any = bf16[1920,640]{1,0:T(8,128)(2,1)S(1)} fusion(bf16[640,640]{1,0:T(8,128)(2,1)} %fusion, bf16[640,640]{1,0:T(8,128)(2,1)} %fusion.1, bf16[640,640]{1,0:T(8,128)(2,1)} %fusion.2), kind=kLoop, calls=%fused_computation | loop fusion | flops 7372800 | bytes 4915200 | tf_op jit(solution)/shard_map/concatenate | solution.py:228
  75.3 0.0 copy-start.8
  75.3 0.0 copy-start.9
  75.3 0.0 collective-permute-done
  75.4 1.1 broadcast_select_fusion.1
  76.5 0.1 pad_maximum_fusion.2
  76.5 1.9 %collective-permute-start.2 = (bf16[6,1,32,640]{3,2,0,1:T(8,128)(2,1)S(1)}, bf16[6,1,32,640]{3,2,0,1:T(8,128)(2,1)S(1)}, u32[]{:S(2)}, u32[]{:S(2)}) collective-permute-start(bf16[6,1,32,640]{3,2,0,1:T(8,128)(2,1)S(1)} %get-tuple-element.20), channel_id=1, source_target_pairs={{0,1},{1,2},{2,3},{3,4},{4,5},{5,6},{6,7},{7,8},{8,9},{9,10},{10,1... | collective-permute-start | bytes 737288 | tf_op jit(solution)/shard_map/ppermute | solution.py:96
  78.4 3.4 %collective-permute-start.3 = (bf16[6,1,32,640]{3,2,0,1:T(8,128)(2,1)S(1)}, bf16[6,1,32,640]{3,2,0,1:T(8,128)(2,1)S(1)}, u32[]{:S(2)}, u32[]{:S(2)}) collective-permute-start(bf16[6,1,32,640]{3,2,0,1:T(8,128)(2,1)S(1)} %get-tuple-element.19), channel_id=1, source_target_pairs={{1,0},{2,1},{3,2},{4,3},{5,4},{6,5},{7,6},{8,7},{9,8},{10,9},{11,1... | collective-permute-start | bytes 737288 | tf_op jit(solution)/shard_map/ppermute | solution.py:97
  81.8 2.0 %collective-permute-done.2 = bf16[6,1,32,640]{3,2,0,1:T(8,128)(2,1)S(1)} collective-permute-done((bf16[6,1,32,640]{3,2,0,1:T(8,128)(2,1)S(1)}, bf16[6,1,32,640]{3,2,0,1:T(8,128)(2,1)S(1)}, u32[]{:S(2)}, u32[]{:S(2)}) %collective-permute-start.2) | collective-permute-done | bytes 245792 | tf_op jit(solution)/shard_map/ppermute | solution.py:96
  83.9 0.7 copy-done
  84.6 5.0 %collective-permute-start.5 = (bf16[80,5760]{1,0:T(8,128)(2,1)S(1)}, bf16[80,5760]{1,0:T(8,128)(2,1)}, u32[]{:S(2)}, u32[]{:S(2)}) collective-permute-start(bf16[80,5760]{1,0:T(8,128)(2,1)S(1)} %concatenate.19.w0), channel_id=1, source_target_pairs={{0,32},{32,0},{64,96},{96,64},{128,160},{160,128},{192,224},{224,1... | collective-permute-start | bytes 2764808 | tf_op jit(solution)/shard_map/ppermute | solution.py:231
  89.6 0.7 copy-done.2
  90.3 4.5 %collective-permute-start.10 = (bf16[80,5760]{1,0:T(8,128)(2,1)}, bf16[80,5760]{1,0:T(8,128)(2,1)}, u32[]{:S(2)}, u32[]{:S(2)}) collective-permute-start(bf16[80,5760]{1,0:T(8,128)(2,1)} %collective-permute-done.4.w6), channel_id=1, source_target_pairs={{0,32},{32,0},{64,96},{96,64},{128,160},{160,128},{192,224},{224,1... | collective-permute-start | bytes 2764808 | tf_op jit(solution)/shard_map/ppermute | solution.py:238
  94.8 13.4 %collective-permute-done.6.w2 = bf16[80,5760]{1,0:T(8,128)(2,1)} collective-permute-done((bf16[80,5760]{1,0:T(8,128)(2,1)S(1)}, bf16[80,5760]{1,0:T(8,128)(2,1)}, u32[]{:S(2)}, u32[]{:S(2)}) %collective-permute-start.6) | collective-permute-done | bytes 921632 | tf_op jit(solution)/shard_map/ppermute | solution.py:71
  108.2 4.4 %collective-permute-start.7 = (bf16[80,5760]{1,0:T(8,128)(2,1)}, bf16[80,5760]{1,0:T(8,128)(2,1)}, u32[]{:S(2)}, u32[]{:S(2)}) collective-permute-start(bf16[80,5760]{1,0:T(8,128)(2,1)} %collective-permute-done.6.w2), channel_id=1, source_target_pairs={{0,32},{32,0},{64,96},{96,64},{128,160},{160,128},{192,224},{224,1... | collective-permute-start | bytes 2764808 | tf_op jit(solution)/shard_map/ppermute | solution.py:238
  112.6 0.0 collective-permute-done.8.w4
  112.6 2.1 %collective-permute-start.9 = (bf16[80,5760]{1,0:T(8,128)(2,1)}, bf16[80,5760]{1,0:T(8,128)(2,1)}, u32[]{:S(2)}, u32[]{:S(2)}) collective-permute-start(bf16[80,5760]{1,0:T(8,128)(2,1)} %collective-permute-done.8.w4), channel_id=1, source_target_pairs={{0,32},{32,0},{64,96},{96,64},{128,160},{160,128},{192,224},{224,1... | collective-permute-start | bytes 2764808 | tf_op jit(solution)/shard_map/ppermute | solution.py:238
  114.8 0.3 select_reduce_fusion
  115.2 0.1 add_convert_fusion.flags_ref
  115.2 1.6 %pad_maximum_fusion.1.wide_any = bf16[6,160,640]{2,1,0:T(8,128)(2,1)S(1)} fusion(bf16[1,160,640]{2,1,0:T(8,128)(2,1)} %bitcast.45, bf16[4,160,640]{2,1,0:T(8,128)(2,1)} %bitcast.40, bf16[1,160,640]{2,1,0:T(8,128)(2,1)} %bitcast.43), kind=kLoop, calls=%fused_computation.6 | loop fusion | flops 1228800 | bytes 2457600 | tf_op jit(solution)/shard_map/concatenate | solution.py:235
  116.8 0.0 collective-permute-done.5.w1
  116.9 0.5 collective-permute-done.9.w5
  117.3 15.8 %shard_map.91 = bf16[4,160,640]{2,1,0:T(8,128)(2,1)S(1)} custom-call(s32[2]{0:T(128)S(1)} %add_convert_fusion.flags_ref, bf16[6,160,640]{2,1,0:T(8,128)(2,1)S(1)} %pad_maximum_fusion.1.wide_any, bf16[6,32,640]{2,1,0:T(8,128)(2,1)S(1)} %bitcast.37, bf16[6,32,640]{2,1,0:T(8,128)(2,1)S(1)} %bitcast.38, bf16[80,5760]{1,0:T(8,128)(2,1)S(1)} %concatenate.19.w0, ...), custom_call_target="tpu_custom_call" | custom-call | flops 8178892800 | bytes 16777216 | tf_op jit(solution)/shard_map/pallas_call | solution.py:203
  133.2 1.3 copy.32
  (30 shorter events, 0.1 us)
Async XLA Ops:
  0.0 22.7 %copy-start.10 = (s32[640]{0:T(1024)S(1)}, s32[640]{0:T(1024)}, u32[]{:S(2)}) copy-start(s32[640]{0:T(1024)} %constant.58.clone) | copy-start | bytes 7684
  0.0 22.7 %copy-start.11 = (s32[640]{0:T(1024)S(1)}, s32[640]{0:T(1024)}, u32[]{:S(2)}) copy-start(s32[640]{0:T(1024)} %constant.59.clone) | copy-start | bytes 7684
  0.0 22.7 %copy-start.12 = (s32[640]{0:T(1024)S(1)}, s32[640]{0:T(1024)}, u32[]{:S(2)}) copy-start(s32[640]{0:T(1024)} %constant.61.clone) | copy-start | bytes 7684
  0.0 22.7 %copy-start.13 = (s32[640]{0:T(1024)S(1)}, s32[640]{0:T(1024)}, u32[]{:S(2)}) copy-start(s32[640]{0:T(1024)} %constant.64) | copy-start | bytes 7684
  1.5 42.7 %all-to-all-start = ((bf16[16,40,180]{2,1,0:T(8,128)(2,1)}), bf16[16,40,180]{2,1,0:T(8,128)(2,1)S(1)}, u32[]{:S(2)}, u32[]{:S(2)}) async-start(bf16[16,40,180]{2,1,0:T(8,128)(2,1)} %broadcast_in_dim.39), calls=%async_computation | async-start | bytes 655360 | tf_op jit(solution)/shard_map/all_to_all | solution.py:59
  13.8 0.9 copy-start.4
  15.5 59.8 %collective-permute-start = (bf16[5,32,640]{2,1,0:T(8,128)(2,1)}, bf16[5,32,640]{2,1,0:T(8,128)(2,1)}, u32[]{:S(2)}, u32[]{:S(2)}) collective-permute-start(bf16[5,32,640]{2,1,0:T(8,128)(2,1)} %get-tuple-element.26), channel_id=1, source_target_pairs={{0,480},{32,64},{64,32},{96,128},{128,96},{160,192},{192,160},{224... | collective-permute-start | bytes 614408 | tf_op jit(solution)/shard_map/ppermute | solution.py:88
  20.7 54.6 %collective-permute-start.1 = (bf16[5,32,640]{2,1,0:T(8,128)(2,1)}, bf16[5,32,640]{2,1,0:T(8,128)(2,1)}, u32[]{:S(2)}, u32[]{:S(2)}) collective-permute-start(bf16[5,32,640]{2,1,0:T(8,128)(2,1)} %get-tuple-element.25), channel_id=1, source_target_pairs={{0,32},{32,0},{64,96},{96,64},{128,160},{160,128},{192,224},{224,1... | collective-permute-start | bytes 614408 | tf_op jit(solution)/shard_map/ppermute | solution.py:89
  45.7 17.8 %all-to-all-start.1 = ((bf16[4,80,1440]{2,1,0:T(8,128)(2,1)}), bf16[4,80,1440]{2,1,0:T(8,128)(2,1)S(1)}, u32[]{:S(2)}, u32[]{:S(2)}) async-start(bf16[4,80,1440]{2,1,0:T(8,128)(2,1)} %broadcast_in_dim.41), calls=%async_computation.1 | async-start | bytes 1966080 | tf_op jit(solution)/shard_map/all_to_all | solution.py:67
  49.7 3.1 %copy-start.14 = (bf16[1920,640]{1,0:T(8,128)(2,1)S(1)}, bf16[1920,640]{1,0:T(8,128)(2,1)}, u32[]{:S(2)}) copy-start(bf16[1920,640]{1,0:T(8,128)(2,1)} %param.12) | copy-start | bytes 7372804
  64.3 12.1 %copy-start.5 = (bf16[5,32,4,640]{3,1,0,2:T(8,128)(2,1)S(1)}, bf16[5,32,4,640]{3,1,0,2:T(8,128)(2,1)}, u32[]{:S(2)}) copy-start(bf16[5,32,4,640]{3,1,0,2:T(8,128)(2,1)} %copy-done.4) | copy-start | bytes 2457604
  64.3 26.0 %collective-permute-start.4 = (bf16[80,5760]{1,0:T(8,128)(2,1)S(1)}, bf16[80,5760]{1,0:T(8,128)(2,1)}, u32[]{:S(2)}, u32[]{:S(2)}) collective-permute-start(bf16[80,5760]{1,0:T(8,128)(2,1)S(1)} %concatenate.19.w0), channel_id=1, source_target_pairs={{256,0},{288,32},{320,64},{352,96},{384,128},{416,160},{448,192},{... | collective-permute-start | bytes 2764808 | tf_op jit(solution)/shard_map/ppermute | solution.py:71
  68.0 40.2 %collective-permute-start.6 = (bf16[80,5760]{1,0:T(8,128)(2,1)S(1)}, bf16[80,5760]{1,0:T(8,128)(2,1)}, u32[]{:S(2)}, u32[]{:S(2)}) collective-permute-start(bf16[80,5760]{1,0:T(8,128)(2,1)S(1)} %concatenate.19.w0), channel_id=1, source_target_pairs={{128,0},{160,32},{192,64},{224,96},{0,128},{32,160},{64,192},{96,2... | collective-permute-start | bytes 2764808 | tf_op jit(solution)/shard_map/ppermute | solution.py:71
  71.4 41.3 %collective-permute-start.8 = (bf16[80,5760]{1,0:T(8,128)(2,1)S(1)}, bf16[80,5760]{1,0:T(8,128)(2,1)}, u32[]{:S(2)}, u32[]{:S(2)}) collective-permute-start(bf16[80,5760]{1,0:T(8,128)(2,1)S(1)} %concatenate.19.w0), channel_id=1, source_target_pairs={{384,0},{416,32},{448,64},{480,96},{256,128},{288,160},{320,192},{... | collective-permute-start | bytes 2764808 | tf_op jit(solution)/shard_map/ppermute | solution.py:71
  75.3 39.4 %copy-start.8 = (f32[640]{0:T(1024)S(1)}, f32[640]{0:T(1024)}, u32[]{:S(2)}) copy-start(f32[640]{0:T(1024)} %param.11) | copy-start | bytes 7684
  75.3 39.8 %copy-start.9 = (f32[640]{0:T(1024)S(1)}, f32[640]{0:T(1024)}, u32[]{:S(2)}) copy-start(f32[640]{0:T(1024)} %param.13) | copy-start | bytes 7684
  76.4 38.3 %copy-start.6 = (bf16[5,32,640]{2,1,0:T(8,128)(2,1)}, bf16[5,32,640]{2,1,0:T(8,128)(2,1)S(1)}, u32[]{:S(2)}) copy-start(bf16[5,32,640]{2,1,0:T(8,128)(2,1)S(1)} %get-tuple-element.27) | copy-start | bytes 614404
  76.4 38.7 %copy-start.7 = (bf16[5,32,640]{2,1,0:T(8,128)(2,1)}, bf16[5,32,640]{2,1,0:T(8,128)(2,1)S(1)}, u32[]{:S(2)}) copy-start(bf16[5,32,640]{2,1,0:T(8,128)(2,1)S(1)} %get-tuple-element.28) | copy-start | bytes 614404
  76.5 7.3 %collective-permute-start.2 = (bf16[6,1,32,640]{3,2,0,1:T(8,128)(2,1)S(1)}, bf16[6,1,32,640]{3,2,0,1:T(8,128)(2,1)S(1)}, u32[]{:S(2)}, u32[]{:S(2)}) collective-permute-start(bf16[6,1,32,640]{3,2,0,1:T(8,128)(2,1)S(1)} %get-tuple-element.20), channel_id=1, source_target_pairs={{0,1},{1,2},{2,3},{3,4},{4,5},{5,6},{6,7},{7,8},{8,9},{9,10},{10,1... | collective-permute-start | bytes 737288 | tf_op jit(solution)/shard_map/ppermute | solution.py:96
  78.4 11.2 %collective-permute-start.3 = (bf16[6,1,32,640]{3,2,0,1:T(8,128)(2,1)S(1)}, bf16[6,1,32,640]{3,2,0,1:T(8,128)(2,1)S(1)}, u32[]{:S(2)}, u32[]{:S(2)}) collective-permute-start(bf16[6,1,32,640]{3,2,0,1:T(8,128)(2,1)S(1)} %get-tuple-element.19), channel_id=1, source_target_pairs={{1,0},{2,1},{3,2},{4,3},{5,4},{6,5},{7,6},{8,7},{9,8},{10,9},{11,1... | collective-permute-start | bytes 737288 | tf_op jit(solution)/shard_map/ppermute | solution.py:97
  83.9 0.7 copy-start
  84.6 32.3 %collective-permute-start.5 = (bf16[80,5760]{1,0:T(8,128)(2,1)S(1)}, bf16[80,5760]{1,0:T(8,128)(2,1)}, u32[]{:S(2)}, u32[]{:S(2)}) collective-permute-start(bf16[80,5760]{1,0:T(8,128)(2,1)S(1)} %concatenate.19.w0), channel_id=1, source_target_pairs={{0,32},{32,0},{64,96},{96,64},{128,160},{160,128},{192,224},{224,1... | collective-permute-start | bytes 2764808 | tf_op jit(solution)/shard_map/ppermute | solution.py:231
  89.6 0.7 copy-start.2
  90.3 26.5 %collective-permute-start.10 = (bf16[80,5760]{1,0:T(8,128)(2,1)}, bf16[80,5760]{1,0:T(8,128)(2,1)}, u32[]{:S(2)}, u32[]{:S(2)}) collective-permute-start(bf16[80,5760]{1,0:T(8,128)(2,1)} %collective-permute-done.4.w6), channel_id=1, source_target_pairs={{0,32},{32,0},{64,96},{96,64},{128,160},{160,128},{192,224},{224,1... | collective-permute-start | bytes 2764808 | tf_op jit(solution)/shard_map/ppermute | solution.py:238
  108.2 8.6 %collective-permute-start.7 = (bf16[80,5760]{1,0:T(8,128)(2,1)}, bf16[80,5760]{1,0:T(8,128)(2,1)}, u32[]{:S(2)}, u32[]{:S(2)}) collective-permute-start(bf16[80,5760]{1,0:T(8,128)(2,1)} %collective-permute-done.6.w2), channel_id=1, source_target_pairs={{0,32},{32,0},{64,96},{96,64},{128,160},{160,128},{192,224},{224,1... | collective-permute-start | bytes 2764808 | tf_op jit(solution)/shard_map/ppermute | solution.py:238
  112.6 4.7 %collective-permute-start.9 = (bf16[80,5760]{1,0:T(8,128)(2,1)}, bf16[80,5760]{1,0:T(8,128)(2,1)}, u32[]{:S(2)}, u32[]{:S(2)}) collective-permute-start(bf16[80,5760]{1,0:T(8,128)(2,1)} %collective-permute-done.8.w4), channel_id=1, source_target_pairs={{0,32},{32,0},{64,96},{96,64},{128,160},{160,128},{192,224},{224,1... | collective-permute-start | bytes 2764808 | tf_op jit(solution)/shard_map/ppermute | solution.py:238
  115.1 2.2 %copy-start.1 = (bf16[6,1,32,640]{3,2,0,1:T(8,128)(2,1)S(1)}, bf16[6,1,32,640]{3,2,0,1:T(8,128)(2,1)}, u32[]{:S(2)}) copy-start(bf16[6,1,32,640]{3,2,0,1:T(8,128)(2,1)} %copy-done) | copy-start | bytes 737284
  115.1 2.2 %copy-start.3 = (bf16[6,1,32,640]{3,2,0,1:T(8,128)(2,1)S(1)}, bf16[6,1,32,640]{3,2,0,1:T(8,128)(2,1)}, u32[]{:S(2)}) copy-start(bf16[6,1,32,640]{3,2,0,1:T(8,128)(2,1)} %copy-done.2) | copy-start | bytes 737284

commit v9 on v8

--- a/solution.py
+++ b/solution.py
@@ -129,7 +129,7 @@
 
 
 def block_kernel(
-    lat_rows, flags_ref, wide_any, earlier_any, later_any, w0, w1, w2, w3, w4, w5, w6, w7, kernel_any,
+    lat_rows, flags_ref, wide_any, earlier_any, later_any, w0, w1, w2, w3, w4, w5, w6, w7, t0, t1, t2,
     bias_ref, tbias_ref, out_ref, planes_ref, weights_ref, kernel_ref, taps_ref, sems,
 ):
     pieces = (w0, w1, w2, w3, w4, w5, w6, w7)
@@ -149,7 +149,10 @@
         for a in range(3)
         for i, w in enumerate(pieces)
     ]
-    pairs += [(kernel_any, kernel_ref)]
+    channels = planes_ref.shape[2]
+    pairs += [
+        (t, kernel_ref.at[pl.ds(k * channels, channels)]) for k, t in enumerate((t0, t1, t2))
+    ]
     moves = [
         pltpu.make_async_copy(source, target, sems.at[i])
         for i, (source, target) in enumerate(pairs)
@@ -163,13 +166,17 @@
     planes, rows, channels = planes_ref.shape
     columns, inner = planes - 2, rows - 2 * lat_rows
     total = None
-    for a in range(3):
-        for move in moves[3 + a * len(pieces) : 3 + (a + 1) * len(pieces)]:
+    for first, end in ((0, 1), (1, 3)):
+        for move in moves[3 + first * len(pieces) : 3 + end * len(pieces)]:
             move.wait()
-        taps = [taps_ref[a, b : b + columns].reshape(columns * rows, channels) for b in range(3)]
+        taps = [
+            taps_ref[a, b : b + columns].reshape(columns * rows, channels)
+            for a in range(first, end)
+            for b in range(3)
+        ]
         term = lax.dot_general(
             jnp.concatenate(taps, axis=1),
-            weights_ref[:, 3 * a * channels : 3 * (a + 1) * channels],
+            weights_ref[:, 3 * first * channels : 3 * end * channels],
             (((1,), (1,)), ((), ())),
             preferred_element_type=jnp.float32,
         )
@@ -183,7 +190,8 @@
         hidden[:, k * lat_rows : k * lat_rows + inner].reshape(columns * inner, channels)
         for k in range(3)
     ]
-    moves[-1].wait()
+    for move in moves[-3:]:
+        move.wait()
     mixed = jnp.dot(
         jnp.concatenate(stacked, axis=1), kernel_ref[...], preferred_element_type=jnp.float32
     )
@@ -196,9 +204,9 @@
     count, inner, channels = wide.shape
     rows = inner + 2 * lat_rows
     planes = jax.ShapeDtypeStruct((count, rows, channels), wide.dtype)
-    moved = (wide, earlier, later, *weights, kernel)
+    moved = (wide, earlier, later, *weights, *kernel)
     joined = (len(weights) * weights[0].shape[0], weights[0].shape[1])
-    shapes = (planes.shape, joined, kernel.shape, (3, *planes.shape))
+    shapes = (planes.shape, joined, (3 * channels, channels), (3, *planes.shape))
     flops = (count - 2) * 2 * channels * channels * (9 * rows + 3 * inner)
     return pl.pallas_call(
         functools.partial(block_kernel, lat_rows),
@@ -206,7 +214,7 @@
         in_specs=[SMEM] + [ANY] * len(moved) + [VMEM, VMEM],
         out_specs=VMEM,
         scratch_shapes=[pltpu.VMEM(s, jnp.bfloat16) for s in shapes]
-        + [pltpu.SemaphoreType.DMA((3 * len(weights) + 4,))],
+        + [pltpu.SemaphoreType.DMA((3 * len(weights) + 6,))],
         compiler_params=params(34),
         cost_estimate=pl.CostEstimate(flops=flops, bytes_accessed=2**24, transcendentals=0),
     )(flags, *moved, bias, tbias)
@@ -225,11 +233,11 @@
         jnp.dot(order.astype(jnp.bfloat16), temporal_kernel[k * channels : (k + 1) * channels])
         for k in range(3)
     ]
-    ordered = jnp.concatenate(ordered, axis=0)
     mine = joined_x(over_x(along_z))
+    mine, *ordered = lax.optimization_barrier((mine, *ordered))
     pieces = over_y(mine)
     others = [lax.ppermute(mine, "lon", CORES)]
-    far, near, columns, ordered, _ = lax.optimization_barrier((far, near, columns, ordered, mine))
+    far, near, columns, *ordered = lax.optimization_barrier((far, near, columns, *ordered))
     before = jnp.where(core == 1, near, far)
     after = jnp.where(core == 1, far, near)
     wide = jnp.concatenate([before[None], columns, after[None]], axis=0)

time: 135 us -> 138 us (1.022)
  starting transfers between devices: 52.6 us -> 55.3 us
  Pallas kernels: 15.8 us -> 17.9 us
  other arithmetic: 5.78 us -> 4.14 us
  local copies, waits for them, and re-layouts: 8.62 us -> 7.18 us
  waiting for transfers between devices: 44.5 us -> 45.9 us
    ppermute x3, starting transfers between devices: 11 us -> 13.3 us  [body(): others += [lax.ppermute(piece, 'lon', CORES) for piece in pieces[1:]]]
    all_to_all x1, waiting for transfers between devices: 21.5 us -> 23.6 us  [gather_z(): lax.all_to_all(copies(shard, 16), ('lon', 'frame'), 0, 0, axis_index_grou...]
    pallas_call x1, Pallas kernels: 15.8 us -> 17.9 us  [block(): pl.pallas_call(functools.partial(block_kernel, lat_rows), out_shape=jax.S...]
    concatenate x1 -> x0, other arithmetic: 1.85 us -> none  [body(): ordered = jnp.concatenate(ordered, axis=0)]
    unnamed x31 -> x25, local copies, waits for them, and re-layouts: 3.58 us -> 2.17 us
  transfers between devices with their start and end apart: 13 -> 13, of which waited for: 5 -> 5; matrix products, arithmetic and copies ran while one was open for 12% -> 10% of each run, Pallas kernels for 0% -> 0%
where the time goes in v9:
time: 138 us
  starting transfers between devices  55.3 us (40%)
  waiting for transfers between devices  45.9 us (33%)
  Pallas kernels  17.9 us (13%)
  local copies, waits for them, and re-layouts  7.18 us (5%)
  matrix products  6.83 us (5%)
  other arithmetic  4.14 us (3%)
    all_to_all x1, waiting for transfers between devices, gather_z(): lax.all_to_all(copies(shard, 16), ('lon', 'frame'), 0, 0, axis_index_grou...  23.6 us
    pallas_call x1, Pallas kernels, block(): pl.pallas_call(functools.partial(block_kernel, lat_rows), out_shape=jax.S...  17.9 us
    ppermute x3, starting transfers between devices, body(): others += [lax.ppermute(piece, 'lon', CORES) for piece in pieces[1:]]  13.3 us
    ppermute x3, waiting for transfers between devices, over_y(): lax.ppermute(block, 'lon', across_y(k))  13 us
    all_to_all x1, starting transfers between devices, gather_z(): lax.all_to_all(copies(shard, 16), ('lon', 'frame'), 0, 0, axis_index_grou...  11.2 us
    ppermute x3, starting transfers between devices, over_y(): lax.ppermute(block, 'lon', across_y(k))  8.98 us
    dot_general x3, matrix products, body(): jnp.dot(order.astype(jnp.bfloat16), temporal_kernel[k * channels:(k + 1)...  6.83 us
    all_to_all x1, waiting for transfers between devices, over_x(): lax.all_to_all(copies(block, X), 'frame', 0, 0, axis_index_groups=x_group...  6.72 us
  transfers between devices with their start and end apart: 13, of which 5 were waited for; matrix products, arithmetic and copies ran while one was open for 10% of the time, Pallas kernels for 0%

profile of v9, /device:TPU:297, one launch (start us, length us, event | category | flops | bytes accessed | tf_op | source)
XLA Modules:
  0.0 137.6 jit_solution(8572905533356462452)
XLA Ops:
  0.0 1.5 %broadcast_in_dim.39 = bf16[16,40,180]{2,1,0:T(8,128)(2,1)} broadcast(bf16[40,180]{1,0:T(8,128)(2,1)} %bitcast.47), dimensions={1,2} | broadcast | bytes 244800 | tf_op jit(solution)/shard_map/broadcast_in_dim | solution.py:53
  1.5 11.2 %all-to-all-start = ((bf16[16,40,180]{2,1,0:T(8,128)(2,1)}), bf16[16,40,180]{2,1,0:T(8,128)(2,1)S(1)}, u32[]{:S(2)}, u32[]{:S(2)}) async-start(bf16[16,40,180]{2,1,0:T(8,128)(2,1)} %broadcast_in_dim.39), calls=%async_computation | async-start | bytes 655360 | tf_op jit(solution)/shard_map/all_to_all | solution.py:59
  12.7 1.2 copy.33
  13.9 0.0 copy-start.3
  13.9 0.9 copy-done.3
  14.8 5.2 %collective-permute-start = (bf16[5,32,640]{2,1,0:T(8,128)(2,1)S(1)}, bf16[5,32,640]{2,1,0:T(8,128)(2,1)S(1)}, u32[]{:S(2)}, u32[]{:S(2)}) collective-permute-start(bf16[5,32,640]{2,1,0:T(8,128)(2,1)S(1)} %get-tuple-element.38), channel_id=1, source_target_pairs={{0,480},{32,64},{64,32},{96,128},{128,96},{160,192},{192,160},{224... | collective-permute-start | bytes 614408 | tf_op jit(solution)/shard_map/ppermute | solution.py:88
  20.1 1.9 %collective-permute-start.1 = (bf16[5,32,640]{2,1,0:T(8,128)(2,1)S(1)}, bf16[5,32,640]{2,1,0:T(8,128)(2,1)}, u32[]{:S(2)}, u32[]{:S(2)}) collective-permute-start(bf16[5,32,640]{2,1,0:T(8,128)(2,1)S(1)} %get-tuple-element.37), channel_id=1, source_target_pairs={{0,32},{32,0},{64,96},{96,64},{128,160},{160,128},{192,224},{224,1... | collective-permute-start | bytes 614408 | tf_op jit(solution)/shard_map/ppermute | solution.py:89
  22.0 0.0 copy-done.7
  22.1 23.6 %all-to-all-done = bf16[16,40,180]{2,1,0:T(8,128)(2,1)S(1)} async-done(((bf16[16,40,180]{2,1,0:T(8,128)(2,1)}), bf16[16,40,180]{2,1,0:T(8,128)(2,1)S(1)}, u32[]{:S(2)}, u32[]{:S(2)}) %all-to-all-start) | async-done | bytes 230432 | tf_op jit(solution)/shard_map/all_to_all | solution.py:59
  45.7 0.1 copy.24
  45.8 0.3 broadcast_in_dim.40
  46.1 1.0 broadcast_in_dim.41
  47.1 4.0 %all-to-all-start.1 = ((bf16[4,80,1440]{2,1,0:T(8,128)(2,1)}), bf16[4,80,1440]{2,1,0:T(8,128)(2,1)S(1)}, u32[]{:S(2)}, u32[]{:S(2)}) async-start(bf16[4,80,1440]{2,1,0:T(8,128)(2,1)} %broadcast_in_dim.41), calls=%async_computation.1 | async-start | bytes 1966080 | tf_op jit(solution)/shard_map/all_to_all | solution.py:67
  51.2 3.1 %fusion.t2 = bf16[640,640]{1,0:T(8,128)(2,1)} fusion(bf16[1920,640]{1,0:T(8,128)(2,1)} %param.12, s32[640]{0:T(1024)S(1)} %multiply_add_fusion), kind=kOutput, calls=%fused_computation.2 | convolution fusion | flops 524697600 | bytes 1640960 | tf_op jit(solution)/shard_map/dot_general | solution.py:233
  54.3 1.8 %fusion.1.t1 = bf16[640,640]{1,0:T(8,128)(2,1)} fusion(bf16[1920,640]{1,0:T(8,128)(2,1)S(1)} %copy-done.11, s32[640]{0:T(1024)S(1)} %multiply_add_fusion), kind=kOutput, calls=%fused_computation.3 | convolution fusion | flops 524697600 | bytes 1642496 | tf_op jit(solution)/shard_map/dot_general | solution.py:233
  56.1 1.9 %fusion.2.t0 = bf16[640,640]{1,0:T(8,128)(2,1)} fusion(bf16[1920,640]{1,0:T(8,128)(2,1)S(1)} %copy-done.11, s32[640]{0:T(1024)S(1)} %multiply_add_fusion), kind=kOutput, calls=%fused_computation.4 | convolution fusion | flops 524697600 | bytes 1642496 | tf_op jit(solution)/shard_map/dot_general | solution.py:233
  58.0 6.7 %all-to-all-done.1 = bf16[4,80,1440]{2,1,0:T(8,128)(2,1)S(1)} async-done(((bf16[4,80,1440]{2,1,0:T(8,128)(2,1)}), bf16[4,80,1440]{2,1,0:T(8,128)(2,1)S(1)}, u32[]{:S(2)}, u32[]{:S(2)}) %all-to-all-start.1) | async-done | bytes 921632 | tf_op jit(solution)/shard_map/all_to_all | solution.py:67
  64.7 0.1 slice_bitcast_fusion
  64.8 0.7 concatenate.15.w0
  65.5 0.0 copy-start.5
  65.5 0.0 copy-start.6
  65.5 2.9 %collective-permute-start.4 = (bf16[80,5760]{1,0:T(8,128)(2,1)S(1)}, bf16[80,5760]{1,0:T(8,128)(2,1)S(1)}, u32[]{:S(2)}, u32[]{:S(2)}) collective-permute-start(bf16[80,5760]{1,0:T(8,128)(2,1)S(1)} %concatenate.15.w0), channel_id=1, source_target_pairs={{256,0},{288,32},{320,64},{352,96},{384,128},{416,160},{448,192},{... | collective-permute-start | bytes 2764808 | tf_op jit(solution)/shard_map/ppermute | solution.py:71
  68.4 4.0 %collective-permute-start.6 = (bf16[80,5760]{1,0:T(8,128)(2,1)S(1)}, bf16[80,5760]{1,0:T(8,128)(2,1)S(1)}, u32[]{:S(2)}, u32[]{:S(2)}) collective-permute-start(bf16[80,5760]{1,0:T(8,128)(2,1)S(1)} %concatenate.15.w0), channel_id=1, source_target_pairs={{128,0},{160,32},{192,64},{224,96},{0,128},{32,160},{64,192},{96,2... | collective-permute-start | bytes 2764808 | tf_op jit(solution)/shard_map/ppermute | solution.py:71
  72.5 2.1 %collective-permute-start.8 = (bf16[80,5760]{1,0:T(8,128)(2,1)S(1)}, bf16[80,5760]{1,0:T(8,128)(2,1)}, u32[]{:S(2)}, u32[]{:S(2)}) collective-permute-start(bf16[80,5760]{1,0:T(8,128)(2,1)S(1)} %concatenate.15.w0), channel_id=1, source_target_pairs={{384,0},{416,32},{448,64},{480,96},{256,128},{288,160},{320,192},{... | collective-permute-start | bytes 2764808 | tf_op jit(solution)/shard_map/ppermute | solution.py:71
  74.5 0.0 collective-permute-done
  74.6 0.0 collective-permute-done.1
  74.6 1.0 broadcast_select_fusion.1
  75.6 1.1 pad_maximum_fusion.1
  76.7 1.9 %collective-permute-start.2 = (bf16[6,1,32,640]{3,2,0,1:T(8,128)(2,1)S(1)}, bf16[6,1,32,640]{3,2,0,1:T(8,128)(2,1)S(1)}, u32[]{:S(2)}, u32[]{:S(2)}) collective-permute-start(bf16[6,1,32,640]{3,2,0,1:T(8,128)(2,1)S(1)} %get-tuple-element.32), channel_id=1, source_target_pairs={{0,1},{1,2},{2,3},{3,4},{4,5},{5,6},{6,7},{7,8},{8,9},{9,10},{10,1... | collective-permute-start | bytes 737288 | tf_op jit(solution)/shard_map/ppermute | solution.py:96
  78.6 3.4 %collective-permute-start.3 = (bf16[6,1,32,640]{3,2,0,1:T(8,128)(2,1)S(1)}, bf16[6,1,32,640]{3,2,0,1:T(8,128)(2,1)S(1)}, u32[]{:S(2)}, u32[]{:S(2)}) collective-permute-start(bf16[6,1,32,640]{3,2,0,1:T(8,128)(2,1)S(1)} %get-tuple-element.31), channel_id=1, source_target_pairs={{1,0},{2,1},{3,2},{4,3},{5,4},{6,5},{7,6},{8,7},{9,8},{10,9},{11,1... | collective-permute-start | bytes 737288 | tf_op jit(solution)/shard_map/ppermute | solution.py:97
  82.0 1.9 %collective-permute-done.2 = bf16[6,1,32,640]{3,2,0,1:T(8,128)(2,1)S(1)} collective-permute-done((bf16[6,1,32,640]{3,2,0,1:T(8,128)(2,1)S(1)}, bf16[6,1,32,640]{3,2,0,1:T(8,128)(2,1)S(1)}, u32[]{:S(2)}, u32[]{:S(2)}) %collective-permute-start.2) | collective-permute-done | bytes 245792 | tf_op jit(solution)/shard_map/ppermute | solution.py:96
  83.9 5.4 %collective-permute-start.5 = (bf16[80,5760]{1,0:T(8,128)(2,1)S(1)}, bf16[80,5760]{1,0:T(8,128)(2,1)}, u32[]{:S(2)}, u32[]{:S(2)}) collective-permute-start(bf16[80,5760]{1,0:T(8,128)(2,1)S(1)} %concatenate.15.w0), channel_id=1, source_target_pairs={{0,32},{32,0},{64,96},{96,64},{128,160},{160,128},{192,224},{224,1... | collective-permute-start | bytes 2764808 | tf_op jit(solution)/shard_map/ppermute | solution.py:239
  89.3 0.0 collective-permute-done.3
  89.3 0.0 collective-permute-done.4.w6
  89.3 6.7 %collective-permute-start.10 = (bf16[80,5760]{1,0:T(8,128)(2,1)S(1)}, bf16[80,5760]{1,0:T(8,128)(2,1)}, u32[]{:S(2)}, u32[]{:S(2)}) collective-permute-start(bf16[80,5760]{1,0:T(8,128)(2,1)S(1)} %collective-permute-done.4.w6), channel_id=1, source_target_pairs={{0,32},{32,0},{64,96},{96,64},{128,160},{160,128},{192,224},{224,1... | collective-permute-start | bytes 2764808 | tf_op jit(solution)/shard_map/ppermute | solution.py:246
  96.1 13.0 %collective-permute-done.6.w2 = bf16[80,5760]{1,0:T(8,128)(2,1)S(1)} collective-permute-done((bf16[80,5760]{1,0:T(8,128)(2,1)S(1)}, bf16[80,5760]{1,0:T(8,128)(2,1)S(1)}, u32[]{:S(2)}, u32[]{:S(2)}) %collective-permute-start.6) | collective-permute-done | bytes 921632 | tf_op jit(solution)/shard_map/ppermute | solution.py:71
  109.1 4.5 %collective-permute-start.7 = (bf16[80,5760]{1,0:T(8,128)(2,1)S(1)}, bf16[80,5760]{1,0:T(8,128)(2,1)}, u32[]{:S(2)}, u32[]{:S(2)}) collective-permute-start(bf16[80,5760]{1,0:T(8,128)(2,1)S(1)} %collective-permute-done.6.w2), channel_id=1, source_target_pairs={{0,32},{32,0},{64,96},{96,64},{128,160},{160,128},{192,224},{224,1... | collective-permute-start | bytes 2764808 | tf_op jit(solution)/shard_map/ppermute | solution.py:246
  113.6 0.0 collective-permute-done.8.w4
  113.6 2.1 %collective-permute-start.9 = (bf16[80,5760]{1,0:T(8,128)(2,1)}, bf16[80,5760]{1,0:T(8,128)(2,1)}, u32[]{:S(2)}, u32[]{:S(2)}) collective-permute-start(bf16[80,5760]{1,0:T(8,128)(2,1)} %collective-permute-done.8.w4), channel_id=1, source_target_pairs={{0,32},{32,0},{64,96},{96,64},{128,160},{160,128},{192,224},{224,1... | collective-permute-start | bytes 2764808 | tf_op jit(solution)/shard_map/ppermute | solution.py:246
  115.7 0.3 select_reduce_fusion
  116.1 0.1 add_convert_fusion.flags_ref
  116.2 1.6 %pad_maximum_fusion.wide_any = bf16[6,160,640]{2,1,0:T(8,128)(2,1)S(1)} fusion(bf16[1,160,640]{2,1,0:T(8,128)(2,1)} %bitcast.45, bf16[4,160,640]{2,1,0:T(8,128)(2,1)} %bitcast.41, bf16[1,160,640]{2,1,0:T(8,128)(2,1)S(1)} %bitcast.43), kind=kLoop, calls=%fused_computation.5 | loop fusion | flops 1228800 | bytes 2457600 | tf_op jit(solution)/shard_map/concatenate | solution.py:243
  117.8 0.0 collective-permute-done.5.w1
  117.8 0.0 collective-permute-done.10.w7
  117.8 0.0 collective-permute-done.7.w3
  117.8 0.5 collective-permute-done.9.w5
  118.3 17.9 %shard_map.91 = bf16[4,160,640]{2,1,0:T(8,128)(2,1)S(1)} custom-call(s32[2]{0:T(128)S(1)} %add_convert_fusion.flags_ref, bf16[6,160,640]{2,1,0:T(8,128)(2,1)S(1)} %pad_maximum_fusion.wide_any, bf16[6,32,640]{2,1,0:T(8,128)(2,1)S(1)} %bitcast.37, bf16[6,32,640]{2,1,0:T(8,128)(2,1)S(1)} %bitcast.38, bf16[80,5760]{1,0:T(8,128)(2,1)S(1)} %concatenate.15.w0, ...), custom_call_target="tpu_custom_call" | custom-call | flops 8178892800 | bytes 16777216 | tf_op jit(solution)/shard_map/pallas_call | solution.py:211
  136.3 1.3 copy.32
  (23 shorter events, 0.1 us)
Async XLA Ops:
  1.5 20.5 %copy-start.7 = (s32[640]{0:T(1024)S(1)}, s32[640]{0:T(1024)}, u32[]{:S(2)}) copy-start(s32[640]{0:T(1024)} %constant.58.clone) | copy-start | bytes 7684
  1.5 20.5 %copy-start.8 = (s32[640]{0:T(1024)S(1)}, s32[640]{0:T(1024)}, u32[]{:S(2)}) copy-start(s32[640]{0:T(1024)} %constant.59.clone) | copy-start | bytes 7684
  1.5 20.5 %copy-start.9 = (s32[640]{0:T(1024)S(1)}, s32[640]{0:T(1024)}, u32[]{:S(2)}) copy-start(s32[640]{0:T(1024)} %constant.61.clone) | copy-start | bytes 7684
  1.5 20.6 %copy-start.10 = (s32[640]{0:T(1024)S(1)}, s32[640]{0:T(1024)}, u32[]{:S(2)}) copy-start(s32[640]{0:T(1024)} %constant.64) | copy-start | bytes 7684
  1.5 44.2 %all-to-all-start = ((bf16[16,40,180]{2,1,0:T(8,128)(2,1)}), bf16[16,40,180]{2,1,0:T(8,128)(2,1)S(1)}, u32[]{:S(2)}, u32[]{:S(2)}) async-start(bf16[16,40,180]{2,1,0:T(8,128)(2,1)} %broadcast_in_dim.39), calls=%async_computation | async-start | bytes 655360 | tf_op jit(solution)/shard_map/all_to_all | solution.py:59
  13.9 0.9 copy-start.3
  14.8 59.7 %collective-permute-start = (bf16[5,32,640]{2,1,0:T(8,128)(2,1)S(1)}, bf16[5,32,640]{2,1,0:T(8,128)(2,1)S(1)}, u32[]{:S(2)}, u32[]{:S(2)}) collective-permute-start(bf16[5,32,640]{2,1,0:T(8,128)(2,1)S(1)} %get-tuple-element.38), channel_id=1, source_target_pairs={{0,480},{32,64},{64,32},{96,128},{128,96},{160,192},{192,160},{224... | collective-permute-start | bytes 614408 | tf_op jit(solution)/shard_map/ppermute | solution.py:88
  20.1 54.5 %collective-permute-start.1 = (bf16[5,32,640]{2,1,0:T(8,128)(2,1)S(1)}, bf16[5,32,640]{2,1,0:T(8,128)(2,1)}, u32[]{:S(2)}, u32[]{:S(2)}) collective-permute-start(bf16[5,32,640]{2,1,0:T(8,128)(2,1)S(1)} %get-tuple-element.37), channel_id=1, source_target_pairs={{0,32},{32,0},{64,96},{96,64},{128,160},{160,128},{192,224},{224,1... | collective-permute-start | bytes 614408 | tf_op jit(solution)/shard_map/ppermute | solution.py:89
  47.1 17.6 %all-to-all-start.1 = ((bf16[4,80,1440]{2,1,0:T(8,128)(2,1)}), bf16[4,80,1440]{2,1,0:T(8,128)(2,1)S(1)}, u32[]{:S(2)}, u32[]{:S(2)}) async-start(bf16[4,80,1440]{2,1,0:T(8,128)(2,1)} %broadcast_in_dim.41), calls=%async_computation.1 | async-start | bytes 1966080 | tf_op jit(solution)/shard_map/all_to_all | solution.py:67
  51.2 3.1 %copy-start.11 = (bf16[1920,640]{1,0:T(8,128)(2,1)S(1)}, bf16[1920,640]{1,0:T(8,128)(2,1)}, u32[]{:S(2)}) copy-start(bf16[1920,640]{1,0:T(8,128)(2,1)} %param.12) | copy-start | bytes 7372804
  65.5 50.2 %copy-start.5 = (f32[640]{0:T(1024)S(1)}, f32[640]{0:T(1024)}, u32[]{:S(2)}) copy-start(f32[640]{0:T(1024)} %param.11) | copy-start | bytes 7684
  65.5 50.6 %copy-start.6 = (f32[640]{0:T(1024)S(1)}, f32[640]{0:T(1024)}, u32[]{:S(2)}) copy-start(f32[640]{0:T(1024)} %param.13) | copy-start | bytes 7684
  65.5 23.8 %collective-permute-start.4 = (bf16[80,5760]{1,0:T(8,128)(2,1)S(1)}, bf16[80,5760]{1,0:T(8,128)(2,1)S(1)}, u32[]{:S(2)}, u32[]{:S(2)}) collective-permute-start(bf16[80,5760]{1,0:T(8,128)(2,1)S(1)} %concatenate.15.w0), channel_id=1, source_target_pairs={{256,0},{288,32},{320,64},{352,96},{384,128},{416,160},{448,192},{... | collective-permute-start | bytes 2764808 | tf_op jit(solution)/shard_map/ppermute | solution.py:71
  68.4 40.7 %collective-permute-start.6 = (bf16[80,5760]{1,0:T(8,128)(2,1)S(1)}, bf16[80,5760]{1,0:T(8,128)(2,1)S(1)}, u32[]{:S(2)}, u32[]{:S(2)}) collective-permute-start(bf16[80,5760]{1,0:T(8,128)(2,1)S(1)} %concatenate.15.w0), channel_id=1, source_target_pairs={{128,0},{160,32},{192,64},{224,96},{0,128},{32,160},{64,192},{96,2... | collective-permute-start | bytes 2764808 | tf_op jit(solution)/shard_map/ppermute | solution.py:71
  72.5 41.1 %collective-permute-start.8 = (bf16[80,5760]{1,0:T(8,128)(2,1)S(1)}, bf16[80,5760]{1,0:T(8,128)(2,1)}, u32[]{:S(2)}, u32[]{:S(2)}) collective-permute-start(bf16[80,5760]{1,0:T(8,128)(2,1)S(1)} %concatenate.15.w0), channel_id=1, source_target_pairs={{384,0},{416,32},{448,64},{480,96},{256,128},{288,160},{320,192},{... | collective-permute-start | bytes 2764808 | tf_op jit(solution)/shard_map/ppermute | solution.py:71
  75.5 1.1 copy-start.4
  76.7 7.2 %collective-permute-start.2 = (bf16[6,1,32,640]{3,2,0,1:T(8,128)(2,1)S(1)}, bf16[6,1,32,640]{3,2,0,1:T(8,128)(2,1)S(1)}, u32[]{:S(2)}, u32[]{:S(2)}) collective-permute-start(bf16[6,1,32,640]{3,2,0,1:T(8,128)(2,1)S(1)} %get-tuple-element.32), channel_id=1, source_target_pairs={{0,1},{1,2},{2,3},{3,4},{4,5},{5,6},{6,7},{7,8},{8,9},{9,10},{10,1... | collective-permute-start | bytes 737288 | tf_op jit(solution)/shard_map/ppermute | solution.py:96
  78.6 10.7 %collective-permute-start.3 = (bf16[6,1,32,640]{3,2,0,1:T(8,128)(2,1)S(1)}, bf16[6,1,32,640]{3,2,0,1:T(8,128)(2,1)S(1)}, u32[]{:S(2)}, u32[]{:S(2)}) collective-permute-start(bf16[6,1,32,640]{3,2,0,1:T(8,128)(2,1)S(1)} %get-tuple-element.31), channel_id=1, source_target_pairs={{1,0},{2,1},{3,2},{4,3},{5,4},{6,5},{7,6},{8,7},{9,8},{10,9},{11,1... | collective-permute-start | bytes 737288 | tf_op jit(solution)/shard_map/ppermute | solution.py:97
  83.9 33.9 %collective-permute-start.5 = (bf16[80,5760]{1,0:T(8,128)(2,1)S(1)}, bf16[80,5760]{1,0:T(8,128)(2,1)}, u32[]{:S(2)}, u32[]{:S(2)}) collective-permute-start(bf16[80,5760]{1,0:T(8,128)(2,1)S(1)} %concatenate.15.w0), channel_id=1, source_target_pairs={{0,32},{32,0},{64,96},{96,64},{128,160},{160,128},{192,224},{224,1... | collective-permute-start | bytes 2764808 | tf_op jit(solution)/shard_map/ppermute | solution.py:239
  89.3 28.5 %collective-permute-start.10 = (bf16[80,5760]{1,0:T(8,128)(2,1)S(1)}, bf16[80,5760]{1,0:T(8,128)(2,1)}, u32[]{:S(2)}, u32[]{:S(2)}) collective-permute-start(bf16[80,5760]{1,0:T(8,128)(2,1)S(1)} %collective-permute-done.4.w6), channel_id=1, source_target_pairs={{0,32},{32,0},{64,96},{96,64},{128,160},{160,128},{192,224},{224,1... | collective-permute-start | bytes 2764808 | tf_op jit(solution)/shard_map/ppermute | solution.py:246
  109.1 8.7 %collective-permute-start.7 = (bf16[80,5760]{1,0:T(8,128)(2,1)S(1)}, bf16[80,5760]{1,0:T(8,128)(2,1)}, u32[]{:S(2)}, u32[]{:S(2)}) collective-permute-start(bf16[80,5760]{1,0:T(8,128)(2,1)S(1)} %collective-permute-done.6.w2), channel_id=1, source_target_pairs={{0,32},{32,0},{64,96},{96,64},{128,160},{160,128},{192,224},{224,1... | collective-permute-start | bytes 2764808 | tf_op jit(solution)/shard_map/ppermute | solution.py:246
  113.6 4.7 %collective-permute-start.9 = (bf16[80,5760]{1,0:T(8,128)(2,1)}, bf16[80,5760]{1,0:T(8,128)(2,1)}, u32[]{:S(2)}, u32[]{:S(2)}) collective-permute-start(bf16[80,5760]{1,0:T(8,128)(2,1)} %collective-permute-done.8.w4), channel_id=1, source_target_pairs={{0,32},{32,0},{64,96},{96,64},{128,160},{160,128},{192,224},{224,1... | collective-permute-start | bytes 2764808 | tf_op jit(solution)/shard_map/ppermute | solution.py:246
  116.1 2.2 %copy-start = (bf16[640,640]{1,0:T(8,128)(2,1)S(1)}, bf16[640,640]{1,0:T(8,128)(2,1)}, u32[]{:S(2)}) copy-start(bf16[640,640]{1,0:T(8,128)(2,1)} %fusion.t2) | copy-start | bytes 2457604
  116.1 2.2 %copy-start.1 = (bf16[640,640]{1,0:T(8,128)(2,1)S(1)}, bf16[640,640]{1,0:T(8,128)(2,1)}, u32[]{:S(2)}) copy-start(bf16[640,640]{1,0:T(8,128)(2,1)} %fusion.1.t1) | copy-start | bytes 2457604
  116.1 2.2 %copy-start.2 = (bf16[640,640]{1,0:T(8,128)(2,1)S(1)}, bf16[640,640]{1,0:T(8,128)(2,1)}, u32[]{:S(2)}) copy-start(bf16[640,640]{1,0:T(8,128)(2,1)} %fusion.2.t0) | copy-start | bytes 2457604

commit v10 on v9

--- a/solution.py
+++ b/solution.py
@@ -166,7 +166,7 @@
     planes, rows, channels = planes_ref.shape
     columns, inner = planes - 2, rows - 2 * lat_rows
     total = None
-    for first, end in ((0, 1), (1, 3)):
+    for first, end in ((0, 1), (1, 2), (2, 3)):
         for move in moves[3 + first * len(pieces) : 3 + end * len(pieces)]:
             move.wait()
         taps = [

time: 138 us -> 136 us (0.986)
  Pallas kernels: 17.9 us -> 15.6 us
    pallas_call x1, Pallas kernels: 17.9 us -> 15.6 us  [block(): pl.pallas_call(functools.partial(block_kernel, lat_rows), out_shape=jax.S...]
  transfers between devices with their start and end apart: 13 -> 13, of which waited for: 5 -> 5; matrix products, arithmetic and copies ran while one was open for 10% -> 11% of each run, Pallas kernels for 0% -> 0%
where the time goes in v10:
time: 136 us; the launch traced here: 135 us
  starting transfers between devices  55.3 us (41%)
  waiting for transfers between devices  45.9 us (34%)
  Pallas kernels  15.6 us (11%)
  local copies, waits for them, and re-layouts  7.18 us (5%)
  matrix products  6.83 us (5%)
  other arithmetic  4.14 us (3%)
    all_to_all x1, waiting for transfers between devices, gather_z(): lax.all_to_all(copies(shard, 16), ('lon', 'frame'), 0, 0, axis_index_grou...  23.6 us
    pallas_call x1, Pallas kernels, block(): pl.pallas_call(functools.partial(block_kernel, lat_rows), out_shape=jax.S...  15.6 us
    ppermute x3, starting transfers between devices, body(): others += [lax.ppermute(piece, 'lon', CORES) for piece in pieces[1:]]  13.3 us
    ppermute x3, waiting for transfers between devices, over_y(): lax.ppermute(block, 'lon', across_y(k))  13 us
    all_to_all x1, starting transfers between devices, gather_z(): lax.all_to_all(copies(shard, 16), ('lon', 'frame'), 0, 0, axis_index_grou...  11.2 us
    ppermute x3, starting transfers between devices, over_y(): lax.ppermute(block, 'lon', across_y(k))  8.98 us
    dot_general x3, matrix products, body(): jnp.dot(order.astype(jnp.bfloat16), temporal_kernel[k * channels:(k + 1)...  6.83 us
    all_to_all x1, waiting for transfers between devices, over_x(): lax.all_to_all(copies(block, X), 'frame', 0, 0, axis_index_groups=x_group...  6.72 us
  transfers between devices with their start and end apart: 13, of which 5 were waited for; matrix products, arithmetic and copies ran while one was open for 11% of the time, Pallas kernels for 0%

profile of v10, /device:TPU:297, one launch (start us, length us, event | category | flops | bytes accessed | tf_op | source)
XLA Modules:
  0.0 135.3 jit_solution(4845896415088259220)
XLA Ops:
  0.0 1.5 %broadcast_in_dim.39 = bf16[16,40,180]{2,1,0:T(8,128)(2,1)} broadcast(bf16[40,180]{1,0:T(8,128)(2,1)} %bitcast.47), dimensions={1,2} | broadcast | bytes 244800 | tf_op jit(solution)/shard_map/broadcast_in_dim | solution.py:53
  1.5 11.2 %all-to-all-start = ((bf16[16,40,180]{2,1,0:T(8,128)(2,1)}), bf16[16,40,180]{2,1,0:T(8,128)(2,1)S(1)}, u32[]{:S(2)}, u32[]{:S(2)}) async-start(bf16[16,40,180]{2,1,0:T(8,128)(2,1)} %broadcast_in_dim.39), calls=%async_computation | async-start | bytes 655360 | tf_op jit(solution)/shard_map/all_to_all | solution.py:59
  12.7 1.2 copy.33
  13.9 0.0 copy-start.3
  13.9 0.9 copy-done.3
  14.8 5.2 %collective-permute-start = (bf16[5,32,640]{2,1,0:T(8,128)(2,1)S(1)}, bf16[5,32,640]{2,1,0:T(8,128)(2,1)S(1)}, u32[]{:S(2)}, u32[]{:S(2)}) collective-permute-start(bf16[5,32,640]{2,1,0:T(8,128)(2,1)S(1)} %get-tuple-element.38), channel_id=1, source_target_pairs={{0,480},{32,64},{64,32},{96,128},{128,96},{160,192},{192,160},{224... | collective-permute-start | bytes 614408 | tf_op jit(solution)/shard_map/ppermute | solution.py:88
  20.1 1.9 %collective-permute-start.1 = (bf16[5,32,640]{2,1,0:T(8,128)(2,1)S(1)}, bf16[5,32,640]{2,1,0:T(8,128)(2,1)}, u32[]{:S(2)}, u32[]{:S(2)}) collective-permute-start(bf16[5,32,640]{2,1,0:T(8,128)(2,1)S(1)} %get-tuple-element.37), channel_id=1, source_target_pairs={{0,32},{32,0},{64,96},{96,64},{128,160},{160,128},{192,224},{224,1... | collective-permute-start | bytes 614408 | tf_op jit(solution)/shard_map/ppermute | solution.py:89
  22.0 0.0 copy-done.7
  22.1 23.6 %all-to-all-done = bf16[16,40,180]{2,1,0:T(8,128)(2,1)S(1)} async-done(((bf16[16,40,180]{2,1,0:T(8,128)(2,1)}), bf16[16,40,180]{2,1,0:T(8,128)(2,1)S(1)}, u32[]{:S(2)}, u32[]{:S(2)}) %all-to-all-start) | async-done | bytes 230432 | tf_op jit(solution)/shard_map/all_to_all | solution.py:59
  45.7 0.1 copy.24
  45.8 0.3 broadcast_in_dim.40
  46.1 1.0 broadcast_in_dim.41
  47.1 4.0 %all-to-all-start.1 = ((bf16[4,80,1440]{2,1,0:T(8,128)(2,1)}), bf16[4,80,1440]{2,1,0:T(8,128)(2,1)S(1)}, u32[]{:S(2)}, u32[]{:S(2)}) async-start(bf16[4,80,1440]{2,1,0:T(8,128)(2,1)} %broadcast_in_dim.41), calls=%async_computation.1 | async-start | bytes 1966080 | tf_op jit(solution)/shard_map/all_to_all | solution.py:67
  51.2 3.1 %fusion.t2 = bf16[640,640]{1,0:T(8,128)(2,1)} fusion(bf16[1920,640]{1,0:T(8,128)(2,1)} %param.12, s32[640]{0:T(1024)S(1)} %multiply_add_fusion), kind=kOutput, calls=%fused_computation.2 | convolution fusion | flops 524697600 | bytes 1640960 | tf_op jit(solution)/shard_map/dot_general | solution.py:233
  54.3 1.8 %fusion.1.t1 = bf16[640,640]{1,0:T(8,128)(2,1)} fusion(bf16[1920,640]{1,0:T(8,128)(2,1)S(1)} %copy-done.11, s32[640]{0:T(1024)S(1)} %multiply_add_fusion), kind=kOutput, calls=%fused_computation.3 | convolution fusion | flops 524697600 | bytes 1642496 | tf_op jit(solution)/shard_map/dot_general | solution.py:233
  56.1 1.9 %fusion.2.t0 = bf16[640,640]{1,0:T(8,128)(2,1)} fusion(bf16[1920,640]{1,0:T(8,128)(2,1)S(1)} %copy-done.11, s32[640]{0:T(1024)S(1)} %multiply_add_fusion), kind=kOutput, calls=%fused_computation.4 | convolution fusion | flops 524697600 | bytes 1642496 | tf_op jit(solution)/shard_map/dot_general | solution.py:233
  58.0 6.7 %all-to-all-done.1 = bf16[4,80,1440]{2,1,0:T(8,128)(2,1)S(1)} async-done(((bf16[4,80,1440]{2,1,0:T(8,128)(2,1)}), bf16[4,80,1440]{2,1,0:T(8,128)(2,1)S(1)}, u32[]{:S(2)}, u32[]{:S(2)}) %all-to-all-start.1) | async-done | bytes 921632 | tf_op jit(solution)/shard_map/all_to_all | solution.py:67
  64.7 0.1 slice_bitcast_fusion
  64.8 0.7 concatenate.15.w0
  65.5 0.0 copy-start.5
  65.5 0.0 copy-start.6
  65.5 2.9 %collective-permute-start.4 = (bf16[80,5760]{1,0:T(8,128)(2,1)S(1)}, bf16[80,5760]{1,0:T(8,128)(2,1)S(1)}, u32[]{:S(2)}, u32[]{:S(2)}) collective-permute-start(bf16[80,5760]{1,0:T(8,128)(2,1)S(1)} %concatenate.15.w0), channel_id=1, source_target_pairs={{256,0},{288,32},{320,64},{352,96},{384,128},{416,160},{448,192},{... | collective-permute-start | bytes 2764808 | tf_op jit(solution)/shard_map/ppermute | solution.py:71
  68.4 4.0 %collective-permute-start.6 = (bf16[80,5760]{1,0:T(8,128)(2,1)S(1)}, bf16[80,5760]{1,0:T(8,128)(2,1)S(1)}, u32[]{:S(2)}, u32[]{:S(2)}) collective-permute-start(bf16[80,5760]{1,0:T(8,128)(2,1)S(1)} %concatenate.15.w0), channel_id=1, source_target_pairs={{128,0},{160,32},{192,64},{224,96},{0,128},{32,160},{64,192},{96,2... | collective-permute-start | bytes 2764808 | tf_op jit(solution)/shard_map/ppermute | solution.py:71
  72.5 2.1 %collective-permute-start.8 = (bf16[80,5760]{1,0:T(8,128)(2,1)S(1)}, bf16[80,5760]{1,0:T(8,128)(2,1)}, u32[]{:S(2)}, u32[]{:S(2)}) collective-permute-start(bf16[80,5760]{1,0:T(8,128)(2,1)S(1)} %concatenate.15.w0), channel_id=1, source_target_pairs={{384,0},{416,32},{448,64},{480,96},{256,128},{288,160},{320,192},{... | collective-permute-start | bytes 2764808 | tf_op jit(solution)/shard_map/ppermute | solution.py:71
  74.5 0.0 collective-permute-done
  74.6 0.0 collective-permute-done.1
  74.6 1.0 broadcast_select_fusion.1
  75.6 1.1 pad_maximum_fusion.1
  76.7 1.9 %collective-permute-start.2 = (bf16[6,1,32,640]{3,2,0,1:T(8,128)(2,1)S(1)}, bf16[6,1,32,640]{3,2,0,1:T(8,128)(2,1)S(1)}, u32[]{:S(2)}, u32[]{:S(2)}) collective-permute-start(bf16[6,1,32,640]{3,2,0,1:T(8,128)(2,1)S(1)} %get-tuple-element.32), channel_id=1, source_target_pairs={{0,1},{1,2},{2,3},{3,4},{4,5},{5,6},{6,7},{7,8},{8,9},{9,10},{10,1... | collective-permute-start | bytes 737288 | tf_op jit(solution)/shard_map/ppermute | solution.py:96
  78.6 3.4 %collective-permute-start.3 = (bf16[6,1,32,640]{3,2,0,1:T(8,128)(2,1)S(1)}, bf16[6,1,32,640]{3,2,0,1:T(8,128)(2,1)S(1)}, u32[]{:S(2)}, u32[]{:S(2)}) collective-permute-start(bf16[6,1,32,640]{3,2,0,1:T(8,128)(2,1)S(1)} %get-tuple-element.31), channel_id=1, source_target_pairs={{1,0},{2,1},{3,2},{4,3},{5,4},{6,5},{7,6},{8,7},{9,8},{10,9},{11,1... | collective-permute-start | bytes 737288 | tf_op jit(solution)/shard_map/ppermute | solution.py:97
  82.0 1.9 %collective-permute-done.2 = bf16[6,1,32,640]{3,2,0,1:T(8,128)(2,1)S(1)} collective-permute-done((bf16[6,1,32,640]{3,2,0,1:T(8,128)(2,1)S(1)}, bf16[6,1,32,640]{3,2,0,1:T(8,128)(2,1)S(1)}, u32[]{:S(2)}, u32[]{:S(2)}) %collective-permute-start.2) | collective-permute-done | bytes 245792 | tf_op jit(solution)/shard_map/ppermute | solution.py:96
  83.9 5.4 %collective-permute-start.5 = (bf16[80,5760]{1,0:T(8,128)(2,1)S(1)}, bf16[80,5760]{1,0:T(8,128)(2,1)}, u32[]{:S(2)}, u32[]{:S(2)}) collective-permute-start(bf16[80,5760]{1,0:T(8,128)(2,1)S(1)} %concatenate.15.w0), channel_id=1, source_target_pairs={{0,32},{32,0},{64,96},{96,64},{128,160},{160,128},{192,224},{224,1... | collective-permute-start | bytes 2764808 | tf_op jit(solution)/shard_map/ppermute | solution.py:239
  89.3 0.0 collective-permute-done.3
  89.3 0.0 collective-permute-done.4.w6
  89.3 6.7 %collective-permute-start.10 = (bf16[80,5760]{1,0:T(8,128)(2,1)S(1)}, bf16[80,5760]{1,0:T(8,128)(2,1)}, u32[]{:S(2)}, u32[]{:S(2)}) collective-permute-start(bf16[80,5760]{1,0:T(8,128)(2,1)S(1)} %collective-permute-done.4.w6), channel_id=1, source_target_pairs={{0,32},{32,0},{64,96},{96,64},{128,160},{160,128},{192,224},{224,1... | collective-permute-start | bytes 2764808 | tf_op jit(solution)/shard_map/ppermute | solution.py:246
  96.1 13.0 %collective-permute-done.6.w2 = bf16[80,5760]{1,0:T(8,128)(2,1)S(1)} collective-permute-done((bf16[80,5760]{1,0:T(8,128)(2,1)S(1)}, bf16[80,5760]{1,0:T(8,128)(2,1)S(1)}, u32[]{:S(2)}, u32[]{:S(2)}) %collective-permute-start.6) | collective-permute-done | bytes 921632 | tf_op jit(solution)/shard_map/ppermute | solution.py:71
  109.1 4.5 %collective-permute-start.7 = (bf16[80,5760]{1,0:T(8,128)(2,1)S(1)}, bf16[80,5760]{1,0:T(8,128)(2,1)}, u32[]{:S(2)}, u32[]{:S(2)}) collective-permute-start(bf16[80,5760]{1,0:T(8,128)(2,1)S(1)} %collective-permute-done.6.w2), channel_id=1, source_target_pairs={{0,32},{32,0},{64,96},{96,64},{128,160},{160,128},{192,224},{224,1... | collective-permute-start | bytes 2764808 | tf_op jit(solution)/shard_map/ppermute | solution.py:246
  113.6 0.0 collective-permute-done.8.w4
  113.6 2.1 %collective-permute-start.9 = (bf16[80,5760]{1,0:T(8,128)(2,1)}, bf16[80,5760]{1,0:T(8,128)(2,1)}, u32[]{:S(2)}, u32[]{:S(2)}) collective-permute-start(bf16[80,5760]{1,0:T(8,128)(2,1)} %collective-permute-done.8.w4), channel_id=1, source_target_pairs={{0,32},{32,0},{64,96},{96,64},{128,160},{160,128},{192,224},{224,1... | collective-permute-start | bytes 2764808 | tf_op jit(solution)/shard_map/ppermute | solution.py:246
  115.7 0.3 select_reduce_fusion
  116.1 0.1 add_convert_fusion.flags_ref
  116.2 1.6 %pad_maximum_fusion.wide_any = bf16[6,160,640]{2,1,0:T(8,128)(2,1)S(1)} fusion(bf16[1,160,640]{2,1,0:T(8,128)(2,1)} %bitcast.45, bf16[4,160,640]{2,1,0:T(8,128)(2,1)} %bitcast.41, bf16[1,160,640]{2,1,0:T(8,128)(2,1)S(1)} %bitcast.43), kind=kLoop, calls=%fused_computation.5 | loop fusion | flops 1228800 | bytes 2457600 | tf_op jit(solution)/shard_map/concatenate | solution.py:243
  117.8 0.0 collective-permute-done.5.w1
  117.8 0.0 collective-permute-done.10.w7
  117.8 0.0 collective-permute-done.7.w3
  117.8 0.5 collective-permute-done.9.w5
  118.3 15.6 %shard_map.91 = bf16[4,160,640]{2,1,0:T(8,128)(2,1)S(1)} custom-call(s32[2]{0:T(128)S(1)} %add_convert_fusion.flags_ref, bf16[6,160,640]{2,1,0:T(8,128)(2,1)S(1)} %pad_maximum_fusion.wide_any, bf16[6,32,640]{2,1,0:T(8,128)(2,1)S(1)} %bitcast.37, bf16[6,32,640]{2,1,0:T(8,128)(2,1)S(1)} %bitcast.38, bf16[80,5760]{1,0:T(8,128)(2,1)S(1)} %concatenate.15.w0, ...), custom_call_target="tpu_custom_call" | custom-call | flops 8178892800 | bytes 16777216 | tf_op jit(solution)/shard_map/pallas_call | solution.py:211
  133.9 1.3 copy.32
  (23 shorter events, 0.1 us)
Async XLA Ops:
  1.5 20.5 %copy-start.7 = (s32[640]{0:T(1024)S(1)}, s32[640]{0:T(1024)}, u32[]{:S(2)}) copy-start(s32[640]{0:T(1024)} %constant.58.clone) | copy-start | bytes 7684
  1.5 20.5 %copy-start.8 = (s32[640]{0:T(1024)S(1)}, s32[640]{0:T(1024)}, u32[]{:S(2)}) copy-start(s32[640]{0:T(1024)} %constant.59.clone) | copy-start | bytes 7684
  1.5 20.5 %copy-start.9 = (s32[640]{0:T(1024)S(1)}, s32[640]{0:T(1024)}, u32[]{:S(2)}) copy-start(s32[640]{0:T(1024)} %constant.61.clone) | copy-start | bytes 7684
  1.5 20.6 %copy-start.10 = (s32[640]{0:T(1024)S(1)}, s32[640]{0:T(1024)}, u32[]{:S(2)}) copy-start(s32[640]{0:T(1024)} %constant.64) | copy-start | bytes 7684
  1.5 44.2 %all-to-all-start = ((bf16[16,40,180]{2,1,0:T(8,128)(2,1)}), bf16[16,40,180]{2,1,0:T(8,128)(2,1)S(1)}, u32[]{:S(2)}, u32[]{:S(2)}) async-start(bf16[16,40,180]{2,1,0:T(8,128)(2,1)} %broadcast_in_dim.39), calls=%async_computation | async-start | bytes 655360 | tf_op jit(solution)/shard_map/all_to_all | solution.py:59
  13.9 0.9 copy-start.3
  14.8 59.7 %collective-permute-start = (bf16[5,32,640]{2,1,0:T(8,128)(2,1)S(1)}, bf16[5,32,640]{2,1,0:T(8,128)(2,1)S(1)}, u32[]{:S(2)}, u32[]{:S(2)}) collective-permute-start(bf16[5,32,640]{2,1,0:T(8,128)(2,1)S(1)} %get-tuple-element.38), channel_id=1, source_target_pairs={{0,480},{32,64},{64,32},{96,128},{128,96},{160,192},{192,160},{224... | collective-permute-start | bytes 614408 | tf_op jit(solution)/shard_map/ppermute | solution.py:88
  20.1 54.5 %collective-permute-start.1 = (bf16[5,32,640]{2,1,0:T(8,128)(2,1)S(1)}, bf16[5,32,640]{2,1,0:T(8,128)(2,1)}, u32[]{:S(2)}, u32[]{:S(2)}) collective-permute-start(bf16[5,32,640]{2,1,0:T(8,128)(2,1)S(1)} %get-tuple-element.37), channel_id=1, source_target_pairs={{0,32},{32,0},{64,96},{96,64},{128,160},{160,128},{192,224},{224,1... | collective-permute-start | bytes 614408 | tf_op jit(solution)/shard_map/ppermute | solution.py:89
  47.1 17.6 %all-to-all-start.1 = ((bf16[4,80,1440]{2,1,0:T(8,128)(2,1)}), bf16[4,80,1440]{2,1,0:T(8,128)(2,1)S(1)}, u32[]{:S(2)}, u32[]{:S(2)}) async-start(bf16[4,80,1440]{2,1,0:T(8,128)(2,1)} %broadcast_in_dim.41), calls=%async_computation.1 | async-start | bytes 1966080 | tf_op jit(solution)/shard_map/all_to_all | solution.py:67
  51.2 3.1 %copy-start.11 = (bf16[1920,640]{1,0:T(8,128)(2,1)S(1)}, bf16[1920,640]{1,0:T(8,128)(2,1)}, u32[]{:S(2)}) copy-start(bf16[1920,640]{1,0:T(8,128)(2,1)} %param.12) | copy-start | bytes 7372804
  65.5 50.2 %copy-start.5 = (f32[640]{0:T(1024)S(1)}, f32[640]{0:T(1024)}, u32[]{:S(2)}) copy-start(f32[640]{0:T(1024)} %param.11) | copy-start | bytes 7684
  65.5 50.6 %copy-start.6 = (f32[640]{0:T(1024)S(1)}, f32[640]{0:T(1024)}, u32[]{:S(2)}) copy-start(f32[640]{0:T(1024)} %param.13) | copy-start | bytes 7684
  65.5 23.8 %collective-permute-start.4 = (bf16[80,5760]{1,0:T(8,128)(2,1)S(1)}, bf16[80,5760]{1,0:T(8,128)(2,1)S(1)}, u32[]{:S(2)}, u32[]{:S(2)}) collective-permute-start(bf16[80,5760]{1,0:T(8,128)(2,1)S(1)} %concatenate.15.w0), channel_id=1, source_target_pairs={{256,0},{288,32},{320,64},{352,96},{384,128},{416,160},{448,192},{... | collective-permute-start | bytes 2764808 | tf_op jit(solution)/shard_map/ppermute | solution.py:71
  68.4 40.7 %collective-permute-start.6 = (bf16[80,5760]{1,0:T(8,128)(2,1)S(1)}, bf16[80,5760]{1,0:T(8,128)(2,1)S(1)}, u32[]{:S(2)}, u32[]{:S(2)}) collective-permute-start(bf16[80,5760]{1,0:T(8,128)(2,1)S(1)} %concatenate.15.w0), channel_id=1, source_target_pairs={{128,0},{160,32},{192,64},{224,96},{0,128},{32,160},{64,192},{96,2... | collective-permute-start | bytes 2764808 | tf_op jit(solution)/shard_map/ppermute | solution.py:71
  72.5 41.1 %collective-permute-start.8 = (bf16[80,5760]{1,0:T(8,128)(2,1)S(1)}, bf16[80,5760]{1,0:T(8,128)(2,1)}, u32[]{:S(2)}, u32[]{:S(2)}) collective-permute-start(bf16[80,5760]{1,0:T(8,128)(2,1)S(1)} %concatenate.15.w0), channel_id=1, source_target_pairs={{384,0},{416,32},{448,64},{480,96},{256,128},{288,160},{320,192},{... | collective-permute-start | bytes 2764808 | tf_op jit(solution)/shard_map/ppermute | solution.py:71
  75.5 1.1 copy-start.4
  76.7 7.2 %collective-permute-start.2 = (bf16[6,1,32,640]{3,2,0,1:T(8,128)(2,1)S(1)}, bf16[6,1,32,640]{3,2,0,1:T(8,128)(2,1)S(1)}, u32[]{:S(2)}, u32[]{:S(2)}) collective-permute-start(bf16[6,1,32,640]{3,2,0,1:T(8,128)(2,1)S(1)} %get-tuple-element.32), channel_id=1, source_target_pairs={{0,1},{1,2},{2,3},{3,4},{4,5},{5,6},{6,7},{7,8},{8,9},{9,10},{10,1... | collective-permute-start | bytes 737288 | tf_op jit(solution)/shard_map/ppermute | solution.py:96
  78.6 10.7 %collective-permute-start.3 = (bf16[6,1,32,640]{3,2,0,1:T(8,128)(2,1)S(1)}, bf16[6,1,32,640]{3,2,0,1:T(8,128)(2,1)S(1)}, u32[]{:S(2)}, u32[]{:S(2)}) collective-permute-start(bf16[6,1,32,640]{3,2,0,1:T(8,128)(2,1)S(1)} %get-tuple-element.31), channel_id=1, source_target_pairs={{1,0},{2,1},{3,2},{4,3},{5,4},{6,5},{7,6},{8,7},{9,8},{10,9},{11,1... | collective-permute-start | bytes 737288 | tf_op jit(solution)/shard_map/ppermute | solution.py:97
  83.9 33.9 %collective-permute-start.5 = (bf16[80,5760]{1,0:T(8,128)(2,1)S(1)}, bf16[80,5760]{1,0:T(8,128)(2,1)}, u32[]{:S(2)}, u32[]{:S(2)}) collective-permute-start(bf16[80,5760]{1,0:T(8,128)(2,1)S(1)} %concatenate.15.w0), channel_id=1, source_target_pairs={{0,32},{32,0},{64,96},{96,64},{128,160},{160,128},{192,224},{224,1... | collective-permute-start | bytes 2764808 | tf_op jit(solution)/shard_map/ppermute | solution.py:239
  89.3 28.5 %collective-permute-start.10 = (bf16[80,5760]{1,0:T(8,128)(2,1)S(1)}, bf16[80,5760]{1,0:T(8,128)(2,1)}, u32[]{:S(2)}, u32[]{:S(2)}) collective-permute-start(bf16[80,5760]{1,0:T(8,128)(2,1)S(1)} %collective-permute-done.4.w6), channel_id=1, source_target_pairs={{0,32},{32,0},{64,96},{96,64},{128,160},{160,128},{192,224},{224,1... | collective-permute-start | bytes 2764808 | tf_op jit(solution)/shard_map/ppermute | solution.py:246
  109.1 8.7 %collective-permute-start.7 = (bf16[80,5760]{1,0:T(8,128)(2,1)S(1)}, bf16[80,5760]{1,0:T(8,128)(2,1)}, u32[]{:S(2)}, u32[]{:S(2)}) collective-permute-start(bf16[80,5760]{1,0:T(8,128)(2,1)S(1)} %collective-permute-done.6.w2), channel_id=1, source_target_pairs={{0,32},{32,0},{64,96},{96,64},{128,160},{160,128},{192,224},{224,1... | collective-permute-start | bytes 2764808 | tf_op jit(solution)/shard_map/ppermute | solution.py:246
  113.6 4.7 %collective-permute-start.9 = (bf16[80,5760]{1,0:T(8,128)(2,1)}, bf16[80,5760]{1,0:T(8,128)(2,1)}, u32[]{:S(2)}, u32[]{:S(2)}) collective-permute-start(bf16[80,5760]{1,0:T(8,128)(2,1)} %collective-permute-done.8.w4), channel_id=1, source_target_pairs={{0,32},{32,0},{64,96},{96,64},{128,160},{160,128},{192,224},{224,1... | collective-permute-start | bytes 2764808 | tf_op jit(solution)/shard_map/ppermute | solution.py:246
  116.1 2.2 %copy-start = (bf16[640,640]{1,0:T(8,128)(2,1)S(1)}, bf16[640,640]{1,0:T(8,128)(2,1)}, u32[]{:S(2)}) copy-start(bf16[640,640]{1,0:T(8,128)(2,1)} %fusion.t2) | copy-start | bytes 2457604
  116.1 2.2 %copy-start.1 = (bf16[640,640]{1,0:T(8,128)(2,1)S(1)}, bf16[640,640]{1,0:T(8,128)(2,1)}, u32[]{:S(2)}) copy-start(bf16[640,640]{1,0:T(8,128)(2,1)} %fusion.1.t1) | copy-start | bytes 2457604
  116.1 2.2 %copy-start.2 = (bf16[640,640]{1,0:T(8,128)(2,1)S(1)}, bf16[640,640]{1,0:T(8,128)(2,1)}, u32[]{:S(2)}) copy-start(bf16[640,640]{1,0:T(8,128)(2,1)} %fusion.2.t0) | copy-start | bytes 2457604
